TPU v7x, 32 devices: a whole 2x2x4 slice. The times are simulated.
32 devices in a mesh: section: 8 (over z, core), fsdp: 4 (over y, x).
Axes of the slice: x: 2, y: 2, z: 4, core: 2. Of those that a mesh axis runs over, the one named last changes fastest.
Arguments:
- tokens: bfloat16 [8, 512, 5120], P('section', 'fsdp'), may hold values from -60 to 60
- cotangents: bfloat16 [8, 512, 1024], P('section', 'fsdp'), may hold values from -6 to 6
- norm_gain: float32 [8, 5120], P('section'), may hold values from 0.1 to 1.9
- master: float32 [8, 5120, 1024], P('section', 'fsdp'), may hold values from -5 to 5
- moment: float32 [8, 5120, 1024], P('section', 'fsdp'), may hold values from -4 to 4
- second: float32 [8, 5120, 1024], P('section', 'fsdp'), may hold values from 0.05 to 2
- head_owner: int32 [8, 4], P('section'), may hold values from 0 to 3, each once within a row
- plan: int32 [4], replicated, may hold values from 0 to 3, each once
Outputs:
- input_grads: bfloat16 [8, 512, 5120], P('section', 'fsdp')
- moment_new: float32 [8, 5120, 1024], P('section', 'fsdp')
- second_new: float32 [8, 5120, 1024], P('section', 'fsdp')
- rollout: bfloat16 [8, 1024, 5120], P('section', 'fsdp')
Inputs may be any that keep to these rules, and one draw needn't show every extreme that they name: `head_owner`: each row lists every head once. `plan`: every slot is named once.
All inputs are finite; a program needn't handle non-finite values.
Results may differ from a plain program's by a relative error of at most 0.011.
Values may be sent and summed in bfloat16 or wider, within the bound.
No kernel may reach another device: no remote copies, remote signals or barrier semaphores. Data moves between devices by JAX's collectives and lax.ppermute only.
A program may use at most 192 MiB of HBM per device.

v0:
```python
import jax
import jax.numpy as jnp
from jax import lax
from jax.sharding import PartitionSpec as P

beta_one = 0.9
beta_two = 0.95
bias_one = 1.0 - 0.9**10
bias_two = 1.0 - 0.95**10
adam_eps = 1e-08
learn_rate = 0.02
weight_decay = 0.1
norm_eps = 1e-06


def entering(x, axis, join, neutral):
    count = lax.axis_size(axis)
    place = lax.axis_index(axis)
    ahead = count - 1 - place
    gathered = lax.all_gather(x.astype(jnp.bfloat16), axis)
    state = jnp.zeros_like(x) + jnp.asarray(neutral, x.dtype)

    def one(lap, state):
        source = count - 1 - lap
        return join(state, lax.dynamic_index_in_dim(gathered, source, 0, False).astype(x.dtype))

    return lax.fori_loop(0, ahead, one, state)


def plan_rows(cot_rows, plan):
    micro_count = plan.shape[0]
    blocks = cot_rows.reshape(micro_count, -1, cot_rows.shape[-1])
    picker = (plan[:, None] == jnp.arange(micro_count, dtype=jnp.int32)[None, :]).astype(
        jnp.bfloat16
    )
    ordered = jnp.einsum("is,smc->imc", picker, blocks, preferred_element_type=jnp.float32)
    return ordered.astype(jnp.bfloat16).reshape(cot_rows.shape)


def input_term(widened, inverse, gain_row, spread):
    scaled = spread * gain_row
    mean_term = jnp.mean(scaled * widened, axis=-1, keepdims=True)
    return inverse * scaled - widened * inverse * inverse * inverse * mean_term


def adam_step(master, moment, second, gradient):
    moment_new = beta_one * moment + (1.0 - beta_one) * gradient
    second_new = beta_two * second + (1.0 - beta_two) * gradient * gradient
    update = moment_new / bias_one / (jnp.sqrt(second_new / bias_two) + adam_eps)
    weights = master - learn_rate * (update + weight_decay * master)
    return (moment_new, second_new, weights)


def arrange(low_rows, owner_row):
    row_count = low_rows.shape[0]
    head_count = owner_row.shape[0]
    by_head = low_rows.reshape(row_count, 2, head_count, -1)
    picker = (owner_row[:, None] == jnp.arange(head_count, dtype=jnp.int32)[None, :]).astype(
        jnp.bfloat16
    )
    placed = jnp.einsum("jh,rphd->rjpd", picker, by_head, preferred_element_type=jnp.float32)
    return placed.astype(jnp.bfloat16).reshape(row_count, -1)


def add_terms(earlier, later):
    return earlier + later


def shards(tokens, cotangents, norm_gain, master, moment, second, head_owner, plan):
    tok_rows = tokens[0]
    gain_row = norm_gain[0]
    master_rows = master[0]
    owner_row = head_owner[0]
    width = tok_rows.shape[1]
    proj_scale = width ** (-0.5)
    ordered = plan_rows(cotangents[0], plan)
    widened = tok_rows.astype(jnp.float32)
    inverse = lax.rsqrt(jnp.mean(widened * widened, axis=-1, keepdims=True) + norm_eps)
    normed = (widened * inverse * gain_row).astype(jnp.bfloat16)
    low_weights = master_rows.astype(jnp.bfloat16)
    spread = (
        jnp.einsum(
            "tc,rc->tr",
            ordered,
            lax.all_gather(low_weights, "fsdp", axis=0, tiled=True),
            preferred_element_type=jnp.float32,
        )
        * proj_scale
    )
    gradient = lax.psum_scatter(
        (
            jnp.einsum("td,tc->dc", normed, ordered, preferred_element_type=jnp.float32)
            * proj_scale
        ).astype(jnp.bfloat16),
        "fsdp",
        scatter_dimension=0,
        tiled=True,
    ).astype(jnp.float32)
    moment_new, second_new, weights = adam_step(master_rows, moment[0], second[0], gradient)
    arranged = arrange(weights.astype(jnp.bfloat16), owner_row)
    rollout = lax.all_to_all(arranged.T, "fsdp", split_axis=0, concat_axis=1, tiled=True)
    own_term = input_term(widened, inverse, gain_row, spread)
    from_above = entering(own_term, "section", add_terms, jnp.zeros_like(own_term))
    input_grads = (own_term + from_above).astype(jnp.bfloat16)
    return (input_grads[None], moment_new[None], second_new[None], rollout[None])


def solution(mesh):
    in_specs = (
        P("section", "fsdp", None),
        P("section", "fsdp", None),
        P("section", None),
        P("section", "fsdp", None),
        P("section", "fsdp", None),
        P("section", "fsdp", None),
        P("section", None),
        P(),
    )
    out_specs = (
        P("section", "fsdp", None),
        P("section", "fsdp", None),
        P("section", "fsdp", None),
        P("section", "fsdp", None),
    )
    return jax.shard_map(shards, mesh=mesh, in_specs=in_specs, out_specs=out_specs, check_vma=False)
```

profile of v0, /device:TPU:0, one launch (start us, length us, event | category | flops | bytes accessed | tf_op | source)
XLA Modules:
  0.0 368.7 jit_solution(4515537473911127318)
XLA Ops:
  7.2 0.0 copy-start
  7.2 0.0 all-gather.4.cloned.1.call-start
  7.2 4.4 %bitcast_convert_fusion = bf16[1280,1024]{1,0:T(8,128)(2,1)} fusion(f32[1,1280,1024]{2,1,0:T(8,128)} %param.13), kind=kLoop, calls=%fused_computation.9 | loop fusion | flops 1310720 | bytes 7864320 | tf_op jit(solution)/shard_map/convert_element_type | solution.py:80
  11.7 0.0 copy-start.6
  11.7 0.0 copy-start.4
  11.7 0.0 all-gather.4.cloned.1.call-update
  11.7 0.0 reduce-scatter.2.cloned.1.call-start
  11.7 0.0 copy-done
  11.7 0.6 copy-done.6
  12.3 0.3 convolution_convert_fusion
  12.7 0.1 copy.17
  12.8 0.0 copy-done.4
  12.8 106.8 %all-gather.4.cloned.1.call-done = bf16[5120,1024]{1,0:T(8,128)(2,1)} async-done(((bf16[1280,1024]{1,0:T(8,128)(2,1)}), bf16[5120,1024]{1,0:T(8,128)(2,1)}) %all-gather.4.cloned.1.call-update) | async-done | bytes 10485776 | tf_op jit(solution)/shard_map/all_gather | solution.py:85
  119.6 0.0 copy-start.3
  119.6 8.1 %fusion.10 = (f32[128]{0:T(128)S(1)}, f32[128]{0:T(128)S(1)}, f32[128,5120]{1,0:T(8,128)S(1)}) fusion(bf16[1,128,5120]{2,1,0:T(8,128)(2,1)} %param.10, f32[5120]{0:T(1024)S(1)} %broadcast_multiply_fusion, bf16[128,1024]{1,0:T(8,128)(2,1)S(1)} %bitcast.91, bf16[5120,1024]{1,0:T(8,128)(2,1)} %all-gather.4.cloned.1.call-done), kind=kOutput, calls=%fused_computation.20 | convolution fusion | flops 1346109184 | bytes 14701568 | tf_op jit(solution)/shard_map/tc,rc->tr/dot_general | solution.py:82
  127.7 0.0 copy-start.2
  127.7 0.0 copy-done.3
  127.7 5.6 %multiply_convert_fusion = bf16[5120,1024]{1,0:T(8,128)(2,1)} fusion(bf16[128,1024]{1,0:T(8,128)(2,1)S(1)} %bitcast.92, bf16[1,128,5120]{2,1,0:T(8,128)(2,1)S(1)} %copy-done.3, f32[5120]{0:T(1024)S(1)} %bitcast.94, f32[128]{0:T(128)S(1)} %add_rsqrt_fusion), kind=kOutput, calls=%fused_computation.1 | convolution fusion | flops 1355284480 | bytes 12079616 | tf_op jit(solution)/shard_map/td,tc->dc/dot_general | solution.py:92
  133.3 0.0 reduce-scatter.2.cloned.1.call-update
  133.3 0.0 all-gather.6.cloned.1.call-start
  133.4 0.0 copy-done.2
  133.4 3.1 fusion.30
  136.5 0.0 all-gather.6.cloned.1.call-update
  136.5 100.5 %reduce-scatter.2.cloned.1.call-done = bf16[1280,1024]{1,0:T(8,128)(2,1)} async-done(((bf16[5120,1024]{1,0:T(8,128)(2,1)}), bf16[1280,1024]{1,0:T(8,128)(2,1)}) %reduce-scatter.2.cloned.1.call-update) | async-done | bytes 2621456 | tf_op jit(solution)/shard_map/reduce_scatter | solution.py:90
  237.1 11.8 %fusion.4 = (bf16[1280,1024]{1,0:T(8,128)(2,1)}, f32[1,1280,1024]{2,1,0:T(8,128)}, f32[1,1280,1024]{2,1,0:T(8,128)}) fusion(f32[1,1280,1024]{2,1,0:T(8,128)} %param.13, bf16[1280,1024]{1,0:T(8,128)(2,1)} %reduce-scatter.2.cloned.1.call-done, f32[1,1280,1024]{2,1,0:T(8,128)} %param.14, f32[1,1280,1024]{2,1,0:T(8,128)} %param.15), kind=kLoop, calls=%fused_computation.12 | loop fusion | flops 22282240 | bytes 31457280 | tf_op jit(solution)/shard_map/convert_element_type | solution.py:100
  248.9 0.0 copy-start.5
  248.9 4.4 %reshape.58 = bf16[1280,2,4,128]{3,2,1,0:T(4,128)(2,1)S(1)} reshape(bf16[1280,1024]{1,0:T(8,128)(2,1)} %get-tuple-element.75) | data formatting | bytes 5242880 | tf_op jit(solution)/shard_map/reshape | solution.py:57
  253.3 0.0 copy-done.5
  253.3 3.0 convert_bitcast_fusion.1
  256.4 5.3 %copy.18 = bf16[1280,4,2,128]{0,3,2,1:T(8,128)(2,1)} copy(bf16[1280,4,2,128]{3,1,2,0:T(4,128)(2,1)} %convert_bitcast_fusion.1) | data formatting | bytes 5242880 | tf_op jit(solution)/shard_map/convert_element_type | solution.py:62
  261.7 4.6 %all-to-all-start = ((bf16[4,256,1280]{2,1,0:T(8,128)(2,1)}), bf16[4,256,1280]{2,1,0:T(8,128)(2,1)}, u32[]{:S(2)}, u32[]{:S(2)}) async-start(bf16[4,256,1280]{2,1,0:T(8,128)(2,1)} %bitcast.20), calls=%async_computation.1 | async-start | bytes 5242880 | tf_op jit(solution)/shard_map/all_to_all | solution.py:101
  266.3 72.4 %all-gather.6.cloned.1.call-done = bf16[1024,5120]{1,0:T(8,128)(2,1)} async-done(((bf16[128,5120]{1,0:T(8,128)(2,1)}), bf16[1024,5120]{1,0:T(8,128)(2,1)}) %all-gather.6.cloned.1.call-update) | async-done | bytes 10485776 | tf_op jit(solution)/shard_map/all_gather | solution.py:20
  338.7 0.2 broadcast_in_dim.20
  339.0 13.5 %while.12 = (s32[]{:T(128)}, f32[128,5120]{1,0:T(8,128)S(1)}, s32[]{:T(128)}, bf16[8,128,5120]{2,1,0:T(8,128)(2,1)}, s32[]{:T(128)}, /*index=5*/s32[]{:T(128)}, s32[]{:T(128)}, s32[]{:T(128)}) while((s32[]{:T(128)}, f32[128,5120]{1,0:T(8,128)S(1)}, s32[]{:T(128)}, bf16[8,128,5120]{2,1,0:T(8,128)(2,1)}, s32[]{:T(128)}, /*index=5*/s32[]{:T(128)}, ...), condition=%wide.region_3.4_spmd, body=%wide.region_2.0_spmd.sunk | while | flops 1310726 | bytes 6553743 | solution.py:27
  339.0 1.9 convert_add_fusion.2
  340.9 1.9 convert_add_fusion.2
  342.8 1.9 convert_add_fusion.2
  344.8 1.9 convert_add_fusion.2
  346.7 1.9 convert_add_fusion.2
  348.6 1.9 convert_add_fusion.2
  350.5 1.9 convert_add_fusion.2
  352.4 4.0 %fusion.18 = bf16[1,128,5120]{2,1,0:T(8,128)(2,1)} fusion(f32[128,5120]{1,0:T(8,128)S(1)} %get-tuple-element.60, f32[128]{0:T(128)S(1)} %broadcast_multiply_fusion.1, bf16[1,128,5120]{2,1,0:T(8,128)(2,1)} %param.10, f32[128,5120]{1,0:T(8,128)} %copy-done.2, f32[128]{0:T(128)S(1)} %add_rsqrt_fusion), kind=kLoop, calls=%fused_computation.30 | loop fusion | flops 5898240 | bytes 7865344 | tf_op jit(solution)/shard_map/broadcast_in_dim | solution.py:105
  356.4 0.0 all-to-all-done
  356.4 3.0 copy.19
  359.4 0.0 copy-start.1
  359.4 2.8 copy.20
  362.2 0.0 copy-done.1
  (3 shorter events, 0.0 us)
Async XLA Ops:
  7.2 4.6 %copy-start = (bf16[1,128,1024]{2,1,0:T(8,128)(2,1)S(1)}, bf16[1,128,1024]{2,1,0:T(8,128)(2,1)}, u32[]{:S(2)}) copy-start(bf16[1,128,1024]{2,1,0:T(8,128)(2,1)} %param.11) | copy-start | bytes 786436
  7.2 112.4 %all-gather.4.cloned.1.call-start = ((), (), s32[]{:S(2)}) async-start(), calls=%async_computation.2 | async-start | bytes 13107200 | tf_op jit(solution)/shard_map/all_gather | solution.py:85
  11.7 0.7 copy-start.6
  11.7 1.1 copy-start.4
  11.7 225.4 %reduce-scatter.2.cloned.1.call-start = ((), (), s32[]{:S(2)}) async-start(), calls=%async_computation.3 | async-start | bytes 13107200 | tf_op jit(solution)/shard_map/reduce_scatter | solution.py:90
  119.6 8.1 %copy-start.3 = (bf16[1,128,5120]{2,1,0:T(8,128)(2,1)S(1)}, bf16[1,128,5120]{2,1,0:T(8,128)(2,1)}, u32[]{:S(2)}) copy-start(bf16[1,128,5120]{2,1,0:T(8,128)(2,1)} %param.10) | copy-start | bytes 3932164
  127.7 5.7 %copy-start.2 = (f32[128,5120]{1,0:T(8,128)}, f32[128,5120]{1,0:T(8,128)S(1)}, u32[]{:S(2)}) copy-start(f32[128,5120]{1,0:T(8,128)S(1)} %get-tuple-element.78) | copy-start | bytes 7864324
  133.3 205.4 %all-gather.6.cloned.1.call-start = ((), (), s32[]{:S(2)}) async-start(), calls=%async_computation.4 | async-start | bytes 11796480 | tf_op jit(solution)/shard_map/all_gather | solution.py:20
  248.9 4.4 %copy-start.5 = (s32[1,4]{1,0:T(1,128)S(1)}, s32[1,4]{1,0:T(1,128)}, u32[]{:S(2)}) copy-start(s32[1,4]{1,0:T(1,128)} %param.16) | copy-start | bytes 52
  261.7 94.7 %all-to-all-start = ((bf16[4,256,1280]{2,1,0:T(8,128)(2,1)}), bf16[4,256,1280]{2,1,0:T(8,128)(2,1)}, u32[]{:S(2)}, u32[]{:S(2)}) async-start(bf16[4,256,1280]{2,1,0:T(8,128)(2,1)} %bitcast.20), calls=%async_computation.1 | async-start | bytes 5242880 | tf_op jit(solution)/shard_map/all_to_all | solution.py:101
  359.4 2.8 copy-start.1
Sparse Core Ops, SparseCore 0:
  11.8 107.7 all-gather.3
  133.5 103.5 reduce-scatter.1
  239.3 99.3 all-gather.5
where the time goes:
time: 370 us; the launch traced here: 369 us
  waiting for transfers between devices  280 us (76%)
  other arithmetic  36.6 us (10%)
  matrix products  17.1 us (5%)
  local copies, waits for them, and re-layouts  16.4 us (4%)
  between operations  13.9 us (4%)
  starting transfers between devices  4.69 us (1%)
    all_gather x1, waiting for transfers between devices, shards(): lax.all_gather(low_weights, 'fsdp', axis=0, tiled=True)  107 us
    reduce_scatter x1, waiting for transfers between devices, shards(): lax.psum_scatter((jnp.einsum('td,tc->dc', normed, ordered, preferred_elem...  101 us
    all_gather x1, waiting for transfers between devices, entering(): gathered = lax.all_gather(x.astype(jnp.bfloat16), axis)  72.4 us
    add x7, other arithmetic, add_terms(): return earlier + later  13.3 us
    convert_element_type x1, other arithmetic, shards(): arranged = arrange(weights.astype(jnp.bfloat16), owner_row)  11.8 us
    dot_general x1, matrix products, shards(): jnp.einsum('tc,rc->tr', ordered, lax.all_gather(low_weights, 'fsdp', axis...  8.09 us
  transfers between devices with their start and end apart: 4, of which 3 were waited for; matrix products, arithmetic and copies ran while one was open for 12% of the time, Pallas kernels for 0%

commit v1 on v0

v1 whole, which is shorter than its diff:
```python
import functools

import jax
import jax.numpy as jnp
from jax import lax
from jax.experimental import pallas as pl
from jax.experimental.pallas import tpu as pltpu
from jax.sharding import PartitionSpec as P

beta_one = 0.9
beta_two = 0.95
bias_one = 1.0 - 0.9**10
bias_two = 1.0 - 0.95**10
adam_eps = 1e-08
learn_rate = 0.02
weight_decay = 0.1
norm_eps = 1e-06

bf16 = jnp.bfloat16
f32 = jnp.float32


def swap(x, axis, k):
    count = lax.axis_size(axis)
    return lax.ppermute(x, axis, [(i, i ^ k) for i in range(count)])


def adam_step(master, moment, second, gradient):
    moment_new = beta_one * moment + (1.0 - beta_one) * gradient
    second_new = beta_two * second + (1.0 - beta_two) * gradient * gradient
    update = moment_new / bias_one / (jnp.sqrt(second_new / bias_two) + adam_eps)
    weights = master - learn_rate * (update + weight_decay * master)
    return (moment_new, second_new, weights)


def plan_rows(cot_rows, plan):
    micro_count = plan.shape[0]
    blocks = cot_rows.reshape(micro_count, -1, cot_rows.shape[-1])
    return jnp.take(blocks, plan, axis=0).reshape(cot_rows.shape)


def suffix_sum(own_term, axis):
    count = lax.axis_size(axis)
    place = lax.axis_index(axis)
    low = own_term.astype(bf16)
    pair = lax.ppermute(low, axis, [(i + 1, i) for i in range(0, count, 2)])
    total = own_term + pair.astype(f32)
    above = jnp.zeros_like(low)
    for z in range(count // 2 - 1, 0, -1):
        got = lax.ppermute(total.astype(bf16), axis, [(2 * z, 2 * z - 2)])
        total = total + got.astype(f32)
        above = above + got
    from_pair = lax.ppermute(above, axis, [(i, i + 1) for i in range(0, count, 2)])
    return jnp.where(place % 2 == 0, total, own_term + from_pair.astype(f32))


def shards_any(tokens, cotangents, norm_gain, master, moment, second, head_owner, plan):
    tok_rows = tokens[0]
    gain_row = norm_gain[0]
    master_rows = master[0]
    owner_row = head_owner[0]
    width = tok_rows.shape[1]
    tok_count = tok_rows.shape[0]
    proj_scale = width ** (-0.5)
    count = lax.axis_size("fsdp")
    place = lax.axis_index("fsdp")
    cols = width // count

    def block_of(x, k):
        return lax.dynamic_slice_in_dim(x, (place ^ k) * cols, cols, axis=-1)

    ordered = plan_rows(cotangents[0], plan)
    all_ordered = [ordered] + [swap(ordered, "fsdp", k) for k in range(1, count)]
    widened = tok_rows.astype(f32)
    inverse = lax.rsqrt(jnp.mean(widened * widened, axis=-1, keepdims=True) + norm_eps)
    normed = (widened * inverse * gain_row).astype(bf16)
    all_normed = [block_of(normed, 0)] + [
        swap(block_of(normed, k), "fsdp", k) for k in range(1, count)
    ]
    low_weights = master_rows.astype(bf16)
    spread = []
    for k in range(count):
        part = (
            jnp.einsum("tc,rc->tr", all_ordered[k], low_weights, preferred_element_type=f32)
            * proj_scale
        )
        spread.append(part if k == 0 else swap(part.astype(bf16), "fsdp", k).astype(f32))

    gradient = (
        jnp.einsum(
            "td,tc->dc",
            jnp.concatenate(all_normed, axis=0),
            jnp.concatenate(all_ordered, axis=0),
            preferred_element_type=f32,
        )
        * proj_scale
    )
    moment_new, second_new, weights = adam_step(master_rows, moment[0], second[0], gradient)
    heads = owner_row.shape[0]
    low_new = weights.astype(bf16).reshape(cols, 2, heads, -1)
    arranged = jnp.take(low_new, owner_row, axis=2).transpose(2, 1, 3, 0).reshape(count, -1, cols)
    rollout = jnp.zeros((arranged.shape[1], width), bf16)
    for k in range(count):
        part = lax.dynamic_index_in_dim(arranged, place ^ k, 0, False)
        if k:
            part = swap(part, "fsdp", k)
        rollout = lax.dynamic_update_slice_in_dim(rollout, part, (place ^ k) * cols, axis=1)

    tok_k = [block_of(tok_rows, k).astype(f32) for k in range(count)]
    scaled = [spread[k] * block_of(gain_row, k) for k in range(count)]
    mean_term = sum(jnp.sum(scaled[k] * tok_k[k], axis=-1, keepdims=True) for k in range(count)) / width
    factor = inverse * inverse * inverse * mean_term
    own_term = jnp.concatenate(
        [inverse * scaled[k] - tok_k[k] * factor for k in range(count)], axis=0
    )
    summed = suffix_sum(own_term, "section").astype(bf16).reshape(count, tok_count, cols)
    input_grads = jnp.zeros((tok_count, width), bf16)
    for k in range(count):
        input_grads = lax.dynamic_update_slice_in_dim(
            input_grads, summed[k], (place ^ k) * cols, axis=1
        )
    return (input_grads[None], moment_new[None], second_new[None], rollout[None])


def call(name, body, grid, prefetch, in_specs, out_specs, out_shape, scratch=(), aliases=None, vmem=24, work=1):
    return pl.pallas_call(
        body,
        grid_spec=pltpu.PrefetchScalarGridSpec(
            num_scalar_prefetch=prefetch,
            grid=grid,
            in_specs=in_specs,
            out_specs=out_specs,
            scratch_shapes=list(scratch),
        ),
        out_shape=out_shape,
        input_output_aliases=aliases or {},
        name=name,
        compiler_params=pltpu.CompilerParams(
            vmem_limit_bytes=vmem * 1024 * 1024,
            dimension_semantics=("arbitrary",) * len(grid),
        ),
        cost_estimate=pl.CostEstimate(flops=work, bytes_accessed=1, transcendentals=0),
    )


def whole(shape):
    return pl.BlockSpec(shape, lambda *_: (0,) * len(shape))


def part_of(place, k, cols):
    return pl.ds(pl.multiple_of((place ^ k) * cols, 128), cols)


def prep_body(count, place_ref, tok_ref, gain_ref, inv_ref, *out_refs):
    place = place_ref[0]
    width = tok_ref.shape[1]
    cols = width // count
    total = jnp.zeros((tok_ref.shape[0], 1), f32)
    for k in range(count):
        x = tok_ref[:, k * cols : (k + 1) * cols].astype(f32)
        total = total + jnp.sum(x * x, axis=-1, keepdims=True)
    inverse = lax.rsqrt(total / width + norm_eps)
    inv_ref[...] = inverse
    for k in range(count):
        part = part_of(place, k, cols)
        x = tok_ref[:, part].astype(f32)
        out_refs[k][...] = (x * inverse * gain_ref[:, part]).astype(bf16).T


def low_body(master_ref, _, low_ref):
    low_ref[...] = master_ref[...].astype(bf16)


def spread_body(count, micro, scale, plan_ref, *refs):
    cots, (low_ref, ordered_ref), outs = refs[:count], refs[count : count + 2], refs[count + 2 :]
    rows = cots[0].shape[0]
    size = rows // micro
    for k in range(count):
        for i in range(micro):
            at = pl.multiple_of(plan_ref[i] * size, size)
            ordered_ref[k * rows + i * size : k * rows + (i + 1) * size, :] = cots[k][
                pl.ds(at, size), :
            ]
    step = 256
    for at in range(0, low_ref.shape[0], step):
        product = lax.dot_general(
            ordered_ref[...],
            low_ref[at : at + step, :],
            (((1,), (1,)), ((), ())),
            preferred_element_type=f32,
        )
        for k in range(count):
            outs[k][:, at : at + step] = (product[k * rows : (k + 1) * rows, :] * scale).astype(bf16)


def grad_body(count, head, scale, place_ref, owner_ref, *refs):
    normed, refs = refs[:count], refs[count:]
    ordered_ref, master_ref, moment_ref, second_ref, moment_out, second_out = refs[:6]
    outs, mark_ref, joined, fresh = refs[6 : 6 + count], *refs[6 + count :]
    tok_count = normed[0].shape[1]
    kv_cols = master_ref.shape[1]
    mark_ref[...] = jnp.zeros_like(mark_ref)
    for k in range(count):
        joined[:, k * tok_count : (k + 1) * tok_count] = normed[k][...]
    step = 256
    size = joined.shape[0]
    rows = pl.ds(pl.multiple_of(pl.program_id(0) * size, size), size)
    for at in range(0, kv_cols, step):
        here = slice(at, at + step)
        part = jnp.dot(joined[...], ordered_ref[:, here], preferred_element_type=f32)
        moment_new = beta_one * moment_ref[rows, here] + ((1.0 - beta_one) * scale) * part
        second_new = beta_two * second_ref[rows, here] + (
            ((1.0 - beta_two) * scale * scale) * part
        ) * part
        moment_out[:, here] = moment_new
        second_out[:, here] = second_new
        scaled = second_new * (1.0 / bias_two)
        root = scaled * lax.rsqrt(scaled) + adam_eps
        weights = master_ref[rows, here] * (1.0 - learn_rate * weight_decay) - (
            moment_new * (learn_rate / bias_one)
        ) * pl.reciprocal(root, approx=True)
        fresh[:, here] = weights.astype(bf16)
    for k in range(count):
        owner = owner_ref[place_ref[0] ^ k] * head
        for p in range(2):
            lanes = pl.ds(pl.multiple_of(p * (kv_cols // 2) + owner, head), head)
            outs[k][p * head : (p + 1) * head, :] = fresh[:, lanes].T


def own_body(count, place_ref, core_ref, tok_ref, gain_ref, inv_ref, *refs):
    spread, (_, keep_ref, give_ref) = refs[:count], refs[count:]
    place = place_ref[0]
    core = core_ref[0]
    width = tok_ref.shape[1]
    cols = width // count
    half = tok_ref.shape[0] // 2
    for out_ref, pick in ((give_ref, 1 - core), (keep_ref, core)):
        rows = pl.ds(pl.multiple_of(pick * half, half), half)
        inverse = inv_ref[rows, :]
        total = jnp.zeros((half, 1), f32)
        for k in range(count):
            part = part_of(place, k, cols)
            scaled = spread[k][rows, :].astype(f32) * gain_ref[:, part]
            total = total + jnp.sum(
                scaled * tok_ref[rows, part].astype(f32), axis=-1, keepdims=True
            )
        factor = inverse * inverse * inverse * (total / width)
        for k in range(count):
            part = part_of(place, k, cols)
            scaled = spread[k][rows, :].astype(f32) * gain_ref[:, part]
            out_ref[:, part] = (
                inverse * scaled - tok_ref[rows, part].astype(f32) * factor
            ).astype(bf16)


def pair_body(chip_ref, keep_ref, got_ref, one_ref, two_ref):
    z = chip_ref[0]
    half = one_ref.shape[0]
    for out_ref, top in ((one_ref, z == 3), (two_ref, z == 2)):
        rows = pl.ds(pl.multiple_of(jnp.where(top, 0, half), half), half)
        out_ref[...] = (keep_ref[rows, :].astype(f32) + got_ref[rows, :].astype(f32)).astype(bf16)


def middle_body(chip_ref, keep_ref, got_ref, one_ref, two_ref, three_ref, four_ref):
    z = chip_ref[0]
    half = one_ref.shape[0]
    rows = pl.ds(pl.multiple_of(jnp.where(z == 2, half, 0), half), half)
    one = one_ref[...].astype(f32)
    two = two_ref[...].astype(f32)
    mine = keep_ref[rows, :].astype(f32) + got_ref[rows, :].astype(f32) + two
    three_ref[...] = (mine + jnp.where(z == 1, one, 0.0)).astype(bf16)
    four_ref[...] = (mine + one).astype(bf16)


def last_body(chip_ref, core_ref, keep_ref, got_ref, one_ref, two_ref, three_ref, four_ref, _, out_ref, send_ref):
    z = chip_ref[0]
    core = core_ref[0]
    half = one_ref.shape[0]
    for part in range(2):
        rows = slice(part * half, (part + 1) * half)
        one = one_ref[...].astype(f32)
        two = two_ref[...].astype(f32)
        three = three_ref[...].astype(f32)
        if part == 0:
            above = jnp.where(z == 1, one + two, three)
        else:
            four = four_ref[...].astype(f32)
            above = jnp.where(z == 0, four, jnp.where(z == 1, three, two))
        keep = keep_ref[rows, :].astype(f32)
        got = got_ref[rows, :].astype(f32)
        both = keep + got + above
        out_ref[rows, :] = jnp.where(core == 0, both, keep + above).astype(bf16)
        send_ref[rows, :] = jnp.where(core == 0, got + above, both).astype(bf16)


def place_body(place_ref, part_ref, *refs):
    refs[-1][...] = part_ref[...]


def marked_body(place_ref, part_ref, _, out_ref, mark_ref):
    out_ref[...] = part_ref[...]
    mark_ref[...] = jnp.zeros_like(mark_ref)


def shards(tokens, cotangents, norm_gain, master, moment, second, head_owner, plan):
    tok_rows, cot_rows = tokens[0], cotangents[0]
    master_rows, moment_rows, second_rows = master[0], moment[0], second[0]
    tok_count, width = tok_rows.shape
    kv_cols = cot_rows.shape[1]
    heads = head_owner.shape[1]
    head = kv_cols // (2 * heads)
    scale = width ** (-0.5)
    count = lax.axis_size("fsdp")
    place = lax.axis_index("fsdp").astype(jnp.int32)[None]
    section = lax.axis_index("section").astype(jnp.int32)
    core, chip = (section & 1)[None], (section >> 1)[None]
    cols = width // count
    half = tok_count // 2
    sds = jax.ShapeDtypeStruct
    dests = range(1, count)
    anywhere = pl.BlockSpec(memory_space=pl.ANY)
    mark = sds((8, 128), f32)

    cots = [cot_rows] + [swap(cot_rows, "fsdp", k) for k in dests]

    inverse, *normed = call(
        "prep",
        functools.partial(prep_body, count),
        (1,),
        1,
        [whole((tok_count, width)), whole((1, width))],
        [whole((tok_count, 1))] + [whole((cols, tok_count))] * count,
        [sds((tok_count, 1), f32)] + [sds((cols, tok_count), bf16)] * count,
    )(place, tok_rows, norm_gain)
    normed = [normed[0]] + [swap(normed[k], "fsdp", k) for k in dests]

    rows_step = 256
    low = call(
        "low",
        low_body,
        (cols // rows_step,),
        0,
        [pl.BlockSpec((rows_step, kv_cols), lambda i: (i, 0)), anywhere],
        pl.BlockSpec((rows_step, kv_cols), lambda i: (i, 0)),
        sds((cols, kv_cols), bf16),
    )(master_rows, inverse)
    ordered, *spread = call(
        "spread",
        functools.partial(spread_body, count, plan.shape[0], scale),
        (1,),
        1,
        [whole((tok_count, kv_cols))] * count + [whole((cols, kv_cols))],
        [whole((count * tok_count, kv_cols))] + [whole((tok_count, cols))] * count,
        [sds((count * tok_count, kv_cols), bf16)] + [sds((tok_count, cols), bf16)] * count,
        work=10**10,
    )(plan, *cots, low)
    spread = [spread[0]] + [swap(spread[k], "fsdp", k) for k in dests]

    state = pl.BlockSpec((rows_step, kv_cols), lambda i, *_: (i, 0))
    resident = pl.BlockSpec(memory_space=pltpu.VMEM)
    moment_new, second_new, *rollout_parts, grad_mark = call(
        "grad",
        functools.partial(grad_body, count, head, scale),
        (cols // rows_step,),
        2,
        [pl.BlockSpec((rows_step, tok_count), lambda i, *_: (i, 0))] * count
        + [resident, resident, resident, resident],
        [state, state]
        + [pl.BlockSpec((2 * head, rows_step), lambda i, *_: (0, i))] * count
        + [whole((8, 128))],
        [sds((cols, kv_cols), f32)] * 2 + [sds((2 * head, cols), bf16)] * count + [mark],
        scratch=[
            pltpu.VMEM((rows_step, count * tok_count), bf16),
            pltpu.VMEM((rows_step, kv_cols), bf16),
        ],
        vmem=20,
    )(place, head_owner[0], *normed, ordered, master_rows, moment_rows, second_rows)

    rollout = ()
    rollout_mark = ()
    for k in (0, 3, 1, 2):
        part = swap(rollout_parts[k], "fsdp", k) if k else rollout_parts[k]
        final = k == 2
        rollout, *rollout_mark = call(
            "place",
            marked_body if final else place_body,
            (1,),
            1,
            [whole((2 * head, cols))] + ([anywhere] if k else []),
            [pl.BlockSpec((2 * head, cols), lambda i, place_ref, k=k: (0, place_ref[0] ^ k))]
            + ([whole((8, 128))] if final else []),
            [sds((2 * head, width), bf16)] + ([mark] if final else []),
            aliases={2: 0} if k else None,
            work=10**9,
        )(place, part, *([rollout] if k else []))

    keep, give = call(
        "own",
        functools.partial(own_body, count),
        (1,),
        2,
        [whole((tok_count, width)), whole((1, width)), whole((tok_count, 1))]
        + [whole((tok_count, cols))] * count
        + [anywhere],
        [whole((half, width))] * 2,
        [sds((half, width), bf16)] * 2,
    )(place, core, tok_rows, norm_gain, inverse, *spread, grad_mark)
    got = swap(give, "section", 1)

    def chips(pairs):
        return [(2 * a + c, 2 * b + c) for c in range(2) for a, b in pairs]

    quarter = half // 2
    full, part = whole((half, width)), whole((quarter, width))
    piece = sds((quarter, width), bf16)
    one, two = call("pair", pair_body, (1,), 1, [full, full], [part, part], [piece, piece])(
        chip, keep, got
    )
    one = lax.ppermute(one, "section", chips([(3, 1), (1, 2)]))
    two = lax.ppermute(two, "section", chips([(2, 1), (3, 2)]))
    three, four = call(
        "middle", middle_body, (1,), 1, [full, full, part, part], [part, part], [piece, piece]
    )(chip, keep, got, one, two)
    three = lax.ppermute(three, "section", chips([(1, 0), (2, 1), (3, 2)]))
    four = lax.ppermute(four, "section", chips([(2, 0)]))
    grads, send = call(
        "last",
        last_body,
        (1,),
        2,
        [full, full, part, part, part, part, anywhere],
        [pl.BlockSpec((half, width), lambda i, chip_ref, core_ref: (core_ref[0], 0)), full],
        [sds((tok_count, width), bf16), sds((half, width), bf16)],
    )(chip, core, keep, got, one, two, three, four, *rollout_mark)
    other = swap(send, "section", 1)
    grads = call(
        "join",
        place_body,
        (1,),
        1,
        [full, anywhere],
        pl.BlockSpec((half, width), lambda i, core_ref: (1 - core_ref[0], 0)),
        sds((tok_count, width), bf16),
        aliases={2: 0},
    )(core, other, grads)
    return (grads[None], moment_new[None], second_new[None], rollout[None])


def choose(*args):
    tokens, cotangents, norm_gain, master, moment, second, head_owner, plan = args
    count, sections = lax.axis_size("fsdp"), lax.axis_size("section")
    tok_count, width = tokens.shape[1:]
    kv_cols, heads = cotangents.shape[2], head_owner.shape[1]
    fits = (
        count == 4
        and sections == 8
        and heads == count
        and plan.shape[0] == 4
        and kv_cols == 2 * heads * 128
        and (width // count) % 256 == 0
        and tok_count % 128 == 0
        and tok_count % (16 * plan.shape[0]) == 0
    )
    return (shards if fits else shards_any)(*args)


def solution(mesh):
    in_specs = (
        P("section", "fsdp", None),
        P("section", "fsdp", None),
        P("section", None),
        P("section", "fsdp", None),
        P("section", "fsdp", None),
        P("section", "fsdp", None),
        P("section", None),
        P(),
    )
    out_specs = (
        P("section", "fsdp", None),
        P("section", "fsdp", None),
        P("section", "fsdp", None),
        P("section", "fsdp", None),
    )
    return jax.shard_map(choose, mesh=mesh, in_specs=in_specs, out_specs=out_specs, check_vma=False)
```

time: 370 us -> 97.8 us (0.26)
  waiting for transfers between devices: 280 us -> 39.4 us
  other arithmetic: 36.6 us -> 0 us
  Pallas kernels: 0 us -> 22.5 us
  matrix products: 17.1 us -> 0 us
  starting transfers between devices: 4.69 us -> 19.4 us
  between operations: 13.9 us -> 0.79 us
    all_gather x2 -> x0, waiting for transfers between devices: 179 us -> none  [the longest x1 107 us: shards(): lax.all_gather(low_weights, 'fsdp', axis=0, tiled=True)]
    reduce_scatter x1 -> x0, waiting for transfers between devices: 101 us -> none  [shards(): lax.psum_scatter((jnp.einsum('td,tc->dc', normed, ordered, preferred_elem...]
    ppermute x0 -> x18, waiting for transfers between devices: none -> 39.4 us  [the longest x14 32.2 us: swap(): return lax.ppermute(x, axis, [(i, i ^ k) for i in range(count)])]
    pallas_call x0 -> x13, Pallas kernels: none -> 22.5 us  [the longest x1 8.75 us: shards(): call('grad', functools.partial(grad_body, count, head, scale), (cols // r...]
    ppermute x0 -> x18, starting transfers between devices: none -> 19.4 us  [the longest x14 15.4 us: swap(): return lax.ppermute(x, axis, [(i, i ^ k) for i in range(count)])]
    convert_element_type x3 -> x0, other arithmetic: 19.3 us -> none  [the longest x1 11.8 us: shards(): arranged = arrange(weights.astype(jnp.bfloat16), owner_row)]
    dot_general x4 -> x0, matrix products: 17.1 us -> none  [the longest x1 8.09 us: shards(): jnp.einsum('tc,rc->tr', ordered, lax.all_gather(low_weights, 'fsdp', axis...]
    add x7 -> x0, other arithmetic: 13.3 us -> none  [add_terms(): return earlier + later]
  transfers between devices with their start and end apart: 4 -> 18, of which waited for: 3 -> 7; matrix products, arithmetic and copies ran while one was open for 12% -> 0% of each run, Pallas kernels for 0% -> 19%
where the time goes in v1:
time: 97.8 us; the launch traced here: 97.3 us
  waiting for transfers between devices  39.4 us (40%)
  Pallas kernels  22.5 us (23%)
  starting transfers between devices  19.4 us (20%)
  local copies, waits for them, and re-layouts  15.3 us (16%)
    ppermute x14, waiting for transfers between devices, swap(): return lax.ppermute(x, axis, [(i, i ^ k) for i in range(count)])  32.2 us
    ppermute x14, starting transfers between devices, swap(): return lax.ppermute(x, axis, [(i, i ^ k) for i in range(count)])  15.4 us
    unnamed x34, local copies, waits for them, and re-layouts  15.3 us
    pallas_call x1, Pallas kernels, shards(): call('grad', functools.partial(grad_body, count, head, scale), (cols // r...  8.75 us
    ppermute x1, waiting for transfers between devices, shards(): four = lax.ppermute(four, 'section', chips([(2, 0)]))  7.14 us
    pallas_call x4, Pallas kernels, shards(): call('place', marked_body if final else place_body, (1,), 1, [whole((2 *...  4.61 us
    pallas_call x1, Pallas kernels, shards(): call('spread', functools.partial(spread_body, count, plan.shape[0], scale...  2.97 us
  transfers between devices with their start and end apart: 18, of which 7 were waited for; matrix products, arithmetic and copies ran while one was open for 0% of the time, Pallas kernels for 19%

profile of v1, /device:TPU:0, one launch (start us, length us, event | category | flops | bytes accessed | tf_op | source)
XLA Modules:
  0.0 97.3 jit_solution(3826465439218194326)
XLA Ops:
  0.6 3.0 %collective-permute-start = (bf16[128,1024]{1,0:T(8,128)(2,1)}, bf16[128,1024]{1,0:T(8,128)(2,1)S(1)}, u32[]{:S(2)}, u32[]{:S(2)}) collective-permute-start(bf16[128,1024]{1,0:T(8,128)(2,1)} %bitcast.20), channel_id=1, source_target_pairs={{0,1},{1,0},{2,3},{3,2},{4,5},{5,4},{6,7},{7,6},{8,9},{9,8},{10,11... | collective-permute-start | bytes 786440 | tf_op jit(solution)/shard_map/ppermute | solution.py:25
  3.6 1.5 %collective-permute-start.1 = (bf16[128,1024]{1,0:T(8,128)(2,1)}, bf16[128,1024]{1,0:T(8,128)(2,1)S(1)}, u32[]{:S(2)}, u32[]{:S(2)}) collective-permute-start(bf16[128,1024]{1,0:T(8,128)(2,1)} %bitcast.21), channel_id=1, source_target_pairs={{0,2},{1,3},{2,0},{3,1},{4,6},{5,7},{6,4},{7,5},{8,10},{9,11},{10,... | collective-permute-start | bytes 786440 | tf_op jit(solution)/shard_map/ppermute | solution.py:25
  5.2 0.0 collective-permute-start.2
  5.2 1.3 %copy-done.2 = bf16[1,128,5120]{2,1,0:T(8,128)(2,1)S(1)} copy-done((bf16[1,128,5120]{2,1,0:T(8,128)(2,1)S(1)}, bf16[1,128,5120]{2,1,0:T(8,128)(2,1)}, u32[]{:S(2)}) %copy-start.2) | copy-done | bytes 1310744
  6.5 0.7 copy-done.6
  7.2 1.5 %prep.1 = (f32[128,1]{1,0:T(8,128)S(1)}, bf16[1280,128]{1,0:T(8,128)(2,1)S(1)}, bf16[1280,128]{1,0:T(8,128)(2,1)S(1)}, bf16[1280,128]{1,0:T(8,128)(2,1)}, bf16[1280,128]{1,0:T(8,128)(2,1)}) custom-call(s32[1]{0:T(128)} %bitcast.2.place_ref, bf16[128,5120]{1,0:T(8,128)(2,1)S(1)} %bitcast.15, f32[1,5120]{1,0:T(1,128)S(1)} %copy-done.6), custom_call_target="tpu_custom_call" | custom-call | flops 1 | bytes 1 | tf_op jit(solution)/shard_map/prep/pallas_call | solution.py:326
  8.7 1.9 %collective-permute-start.6 = (bf16[1280,128]{1,0:T(8,128)(2,1)S(1)}, bf16[1280,128]{1,0:T(8,128)(2,1)S(1)}, u32[]{:S(2)}, u32[]{:S(2)}) collective-permute-start(bf16[1280,128]{1,0:T(8,128)(2,1)S(1)} %get-tuple-element.37), channel_id=1, source_target_pairs={{0,1},{1,0},{2,3},{3,2},{4,5},{5,4},{6,7},{7,6},{8,9},{9,8},{10,11... | collective-permute-start | bytes 983048 | tf_op jit(solution)/shard_map/ppermute | solution.py:25
  10.7 1.5 %collective-permute-start.7 = (bf16[1280,128]{1,0:T(8,128)(2,1)}, bf16[1280,128]{1,0:T(8,128)(2,1)S(1)}, u32[]{:S(2)}, u32[]{:S(2)}) collective-permute-start(bf16[1280,128]{1,0:T(8,128)(2,1)} %get-tuple-element.38), channel_id=1, source_target_pairs={{0,2},{1,3},{2,0},{3,1},{4,6},{5,7},{6,4},{7,5},{8,10},{9,11},{10,... | collective-permute-start | bytes 983048 | tf_op jit(solution)/shard_map/ppermute | solution.py:25
  12.2 2.5 %copy-done = f32[1,1280,1024]{2,1,0:T(8,128)S(1)} copy-done((f32[1,1280,1024]{2,1,0:T(8,128)S(1)}, f32[1,1280,1024]{2,1,0:T(8,128)}, u32[]{:S(2)}) %copy-start) | copy-done | bytes 5242904
  14.7 0.3 low.1.refs_4_
  15.0 0.0 collective-permute-done.refs_1_
  15.0 0.0 copy-start.8
  15.0 0.1 collective-permute-start.8
  15.1 2.6 %collective-permute-done.1.refs_2_ = bf16[128,1024]{1,0:T(8,128)(2,1)S(1)} collective-permute-done((bf16[128,1024]{1,0:T(8,128)(2,1)}, bf16[128,1024]{1,0:T(8,128)(2,1)S(1)}, u32[]{:S(2)}, u32[]{:S(2)}) %collective-permute-start.1) | collective-permute-done | bytes 262176 | tf_op jit(solution)/shard_map/ppermute | solution.py:25
  17.7 0.7 copy-done.12
  18.4 0.0 collective-permute-done.2.refs_3_
  18.4 0.7 copy-done.14
  19.1 0.0 copy-done.11
  19.1 0.0 copy-done.16
  19.1 0.9 copy-done.13
  20.1 0.9 copy-done.15
  21.0 3.0 %spread.1 = (bf16[512,1024]{1,0:T(8,128)(2,1)S(1)}, bf16[128,1280]{1,0:T(8,128)(2,1)S(1)}, bf16[128,1280]{1,0:T(8,128)(2,1)}, bf16[128,1280]{1,0:T(8,128)(2,1)}, bf16[128,1280]{1,0:T(8,128)(2,1)}) custom-call(s32[4]{0:T(128)S(1)} %copy-done.16, bf16[128,1024]{1,0:T(8,128)(2,1)S(1)} %bitcast.23, bf16[128,1024]{1,0:T(8,128)(2,1)S(1)} %collective-permute-done.refs_1_, ...), custom_call_target="tpu_custom_call" | custom-call | flops 10000000000 | bytes 1 | tf_op jit(solution)/shard_map/spread/pallas_call | solution.py:347
  24.0 1.2 %collective-permute-start.3 = (bf16[128,1280]{1,0:T(8,128)(2,1)}, bf16[128,1280]{1,0:T(8,128)(2,1)S(1)}, u32[]{:S(2)}, u32[]{:S(2)}) collective-permute-start(bf16[128,1280]{1,0:T(8,128)(2,1)} %get-tuple-element.33), channel_id=1, source_target_pairs={{0,1},{1,0},{2,3},{3,2},{4,5},{5,4},{6,7},{7,6},{8,9},{9,8},{10,11... | collective-permute-start | bytes 983048 | tf_op jit(solution)/shard_map/ppermute | solution.py:25
  25.2 1.2 %collective-permute-start.4 = (bf16[128,1280]{1,0:T(8,128)(2,1)}, bf16[128,1280]{1,0:T(8,128)(2,1)S(1)}, u32[]{:S(2)}, u32[]{:S(2)}) collective-permute-start(bf16[128,1280]{1,0:T(8,128)(2,1)} %get-tuple-element.34), channel_id=1, source_target_pairs={{0,2},{1,3},{2,0},{3,1},{4,6},{5,7},{6,4},{7,5},{8,10},{9,11},{10,... | collective-permute-start | bytes 983048 | tf_op jit(solution)/shard_map/ppermute | solution.py:25
  26.4 0.0 collective-permute-done.6.refs_1_
  26.4 1.5 %collective-permute-start.5 = (bf16[128,1280]{1,0:T(8,128)(2,1)}, bf16[128,1280]{1,0:T(8,128)(2,1)S(1)}, u32[]{:S(2)}, u32[]{:S(2)}) collective-permute-start(bf16[128,1280]{1,0:T(8,128)(2,1)} %get-tuple-element.35), channel_id=1, source_target_pairs={{0,3},{1,2},{2,1},{3,0},{4,7},{5,6},{6,5},{7,4},{8,11},{9,10},{10,... | collective-permute-start | bytes 983048 | tf_op jit(solution)/shard_map/ppermute | solution.py:25
  27.9 3.9 %collective-permute-done.7.refs_2_ = bf16[1280,128]{1,0:T(8,128)(2,1)S(1)} collective-permute-done((bf16[1280,128]{1,0:T(8,128)(2,1)}, bf16[1280,128]{1,0:T(8,128)(2,1)S(1)}, u32[]{:S(2)}, u32[]{:S(2)}) %collective-permute-start.7) | collective-permute-done | bytes 327712 | tf_op jit(solution)/shard_map/ppermute | solution.py:25
  31.8 0.6 collective-permute-done.8.refs_3_
  32.4 0.0 copy-done.8
  32.4 2.5 %copy-done.1 = f32[1,1280,1024]{2,1,0:T(8,128)S(1)} copy-done((f32[1,1280,1024]{2,1,0:T(8,128)S(1)}, f32[1,1280,1024]{2,1,0:T(8,128)}, u32[]{:S(2)}) %copy-start.1) | copy-done | bytes 5242904
  34.9 2.5 %copy-done.4 = f32[1,1280,1024]{2,1,0:T(8,128)S(1)} copy-done((f32[1,1280,1024]{2,1,0:T(8,128)S(1)}, f32[1,1280,1024]{2,1,0:T(8,128)}, u32[]{:S(2)}) %copy-start.4) | copy-done | bytes 5242904
  37.3 2.5 %copy-done.5 = f32[1,1280,1024]{2,1,0:T(8,128)S(1)} copy-done((f32[1,1280,1024]{2,1,0:T(8,128)S(1)}, f32[1,1280,1024]{2,1,0:T(8,128)}, u32[]{:S(2)}) %copy-start.5) | copy-done | bytes 5242904
  39.8 8.8 %grad.1 = (f32[1280,1024]{1,0:T(8,128)}, f32[1280,1024]{1,0:T(8,128)}, bf16[256,1280]{1,0:T(8,128)(2,1)S(1)}, bf16[256,1280]{1,0:T(8,128)(2,1)}, bf16[256,1280]{...) custom-call(s32[1]{0:T(128)} %bitcast.2.place_ref, s32[4]{0:T(128)S(1)} %bitcast.19, ...), custom_call_target="tpu_custom_call" | custom-call | flops 1 | bytes 1 | tf_op jit(solution)/shard_map/grad/pallas_call | solution.py:361
  48.6 0.0 collective-permute-done.3.refs_1_
  48.6 0.0 collective-permute-done.4.refs_2_
  48.6 0.0 collective-permute-done.5.refs_3_
  48.6 0.0 copy-done.3
  48.6 1.7 %own.1 = (bf16[64,5120]{1,0:T(8,128)(2,1)S(1)}, bf16[64,5120]{1,0:T(8,128)(2,1)}) custom-call(s32[1]{0:T(128)} %bitcast.2.place_ref, s32[1]{0:T(128)} %bitcast.core_ref.place_ref, bf16[128,5120]{1,0:T(8,128)(2,1)S(1)} %bitcast.16, f32[1,5120]{1,0:T(1,128)S(1)} %copy-done.7, f32[128,1]{1,0:T(8,128)S(1)} %get-tuple-element.31._.inv_ref, ...), custom_call_target="tpu_custom_call" | custom-call | flops 1 | bytes 1 | tf_op jit(solution)/shard_map/own/pallas_call | solution.py:397
  50.3 0.0 collective-permute-start.9
  50.4 1.4 %collective-permute-start.16 = (bf16[256,1280]{1,0:T(8,128)(2,1)}, bf16[256,1280]{1,0:T(8,128)(2,1)S(1)}, u32[]{:S(2)}, u32[]{:S(2)}) collective-permute-start(bf16[256,1280]{1,0:T(8,128)(2,1)} %get-tuple-element.50), channel_id=1, source_target_pairs={{0,3},{1,2},{2,1},{3,0},{4,7},{5,6},{6,5},{7,4},{8,11},{9,10},{10,... | collective-permute-start | bytes 1966088 | tf_op jit(solution)/shard_map/ppermute | solution.py:25
  51.8 1.8 %collective-permute-start.15 = (bf16[256,1280]{1,0:T(8,128)(2,1)}, bf16[256,1280]{1,0:T(8,128)(2,1)S(1)}, u32[]{:S(2)}, u32[]{:S(2)}) collective-permute-start(bf16[256,1280]{1,0:T(8,128)(2,1)} %get-tuple-element.49), channel_id=1, source_target_pairs={{0,1},{1,0},{2,3},{3,2},{4,5},{5,4},{6,7},{7,6},{8,9},{9,8},{10,11... | collective-permute-start | bytes 1966088 | tf_op jit(solution)/shard_map/ppermute | solution.py:25
  53.6 0.2 collective-permute-start.14
  53.8 0.0 collective-permute-done.9.got_ref
  53.8 0.2 pair.1
  54.0 0.7 collective-permute-start.10
  54.7 0.7 collective-permute-start.11
  55.4 0.0 collective-permute-done.10.one_ref
  55.4 0.0 collective-permute-done.11.two_ref
  55.4 0.2 middle.1
  55.7 1.3 %collective-permute-start.12 = (bf16[32,5120]{1,0:T(8,128)(2,1)S(1)}, bf16[32,5120]{1,0:T(8,128)(2,1)S(1)}, u32[]{:S(2)}, u32[]{:S(2)}) collective-permute-start(bf16[32,5120]{1,0:T(8,128)(2,1)S(1)} %get-tuple-element.46), channel_id=1, source_target_pairs={{8,0},{16,8},{24,16},{12,4},{20,12},{28,20},{9,1},{17,9},{25,17},{... | collective-permute-start | bytes 983048 | tf_op jit(solution)/shard_map/ppermute | solution.py:424
  57.0 1.3 %collective-permute-start.13 = (bf16[32,5120]{1,0:T(8,128)(2,1)S(1)}, bf16[32,5120]{1,0:T(8,128)(2,1)S(1)}, u32[]{:S(2)}, u32[]{:S(2)}) collective-permute-start(bf16[32,5120]{1,0:T(8,128)(2,1)S(1)} %get-tuple-element.47), channel_id=1, source_target_pairs={{16,0},{20,4},{17,1},{21,5},{18,2},{22,6},{19,3},{23,7}} | collective-permute-start | bytes 983048 | tf_op jit(solution)/shard_map/ppermute | solution.py:425
  58.3 0.9 place.4.refs_0_
  59.1 9.9 %collective-permute-done.16.part_ref = bf16[256,1280]{1,0:T(8,128)(2,1)S(1)} collective-permute-done((bf16[256,1280]{1,0:T(8,128)(2,1)}, bf16[256,1280]{1,0:T(8,128)(2,1)S(1)}, u32[]{:S(2)}, u32[]{:S(2)}) %collective-permute-start.16) | collective-permute-done | bytes 655392 | tf_op jit(solution)/shard_map/ppermute | solution.py:25
  69.0 0.9 place.5.refs_0_
  69.9 13.1 %collective-permute-done.15.part_ref = bf16[256,1280]{1,0:T(8,128)(2,1)S(1)} collective-permute-done((bf16[256,1280]{1,0:T(8,128)(2,1)}, bf16[256,1280]{1,0:T(8,128)(2,1)S(1)}, u32[]{:S(2)}, u32[]{:S(2)}) %collective-permute-start.15) | collective-permute-done | bytes 655392 | tf_op jit(solution)/shard_map/ppermute | solution.py:25
  83.0 0.9 place.6._
  83.9 0.0 collective-permute-done.14.part_ref
  83.9 2.0 %place.7 = (bf16[256,5120]{1,0:T(8,128)(2,1)}, f32[8,128]{1,0:T(8,128)S(1)}) custom-call(s32[1]{0:T(128)} %bitcast.2.place_ref, bf16[256,1280]{1,0:T(8,128)(2,1)} %collective-permute-done.14.part_ref, bf16[256,5120]{1,0:T(8,128)(2,1)} %place.6._), custom_call_target="tpu_custom_call", output_to_operand_aliasing={{0}: (2, {})} | custom-call | flops 1000000000 | bytes 1 | tf_op jit(solution)/shard_map/place/pallas_call | solution.py:384
  85.9 0.0 collective-permute-done.12.three_ref
  85.9 7.1 %collective-permute-done.13.four_ref = bf16[32,5120]{1,0:T(8,128)(2,1)S(1)} collective-permute-done((bf16[32,5120]{1,0:T(8,128)(2,1)S(1)}, bf16[32,5120]{1,0:T(8,128)(2,1)S(1)}, u32[]{:S(2)}, u32[]{:S(2)}) %collective-permute-start.13) | collective-permute-done | bytes 327712 | tf_op jit(solution)/shard_map/ppermute | solution.py:425
  93.0 1.3 %last.1 = (bf16[128,5120]{1,0:T(8,128)(2,1)}, bf16[64,5120]{1,0:T(8,128)(2,1)S(1)}) custom-call(s32[1]{0:T(128)} %bitcast.1.chip_ref, s32[1]{0:T(128)} %bitcast.core_ref.place_ref, bf16[64,5120]{1,0:T(8,128)(2,1)S(1)} %get-tuple-element.42.keep_ref, bf16[64,5120]{1,0:T(8,128)(2,1)S(1)} %collective-permute-done.9.got_ref, ...), custom_call_target="tpu_custom_call" | custom-call | flops 1 | bytes 1 | tf_op jit(solution)/shard_map/last/pallas_call | solution.py:426
  94.3 0.0 collective-permute-start.17
  94.3 2.1 %collective-permute-done.17.part_ref = bf16[64,5120]{1,0:T(8,128)(2,1)S(1)} collective-permute-done((bf16[64,5120]{1,0:T(8,128)(2,1)S(1)}, bf16[64,5120]{1,0:T(8,128)(2,1)S(1)}, u32[]{:S(2)}, u32[]{:S(2)}) %collective-permute-start.17) | collective-permute-done | bytes 655392 | tf_op jit(solution)/shard_map/ppermute | solution.py:25
  96.4 0.9 join.1
  (19 shorter events, 0.0 us)
Async XLA Ops:
  0.6 14.4 %collective-permute-start = (bf16[128,1024]{1,0:T(8,128)(2,1)}, bf16[128,1024]{1,0:T(8,128)(2,1)S(1)}, u32[]{:S(2)}, u32[]{:S(2)}) collective-permute-start(bf16[128,1024]{1,0:T(8,128)(2,1)} %bitcast.20), channel_id=1, source_target_pairs={{0,1},{1,0},{2,3},{3,2},{4,5},{5,4},{6,7},{7,6},{8,9},{9,8},{10,11... | collective-permute-start | bytes 786440 | tf_op jit(solution)/shard_map/ppermute | solution.py:25
  3.6 14.1 %collective-permute-start.1 = (bf16[128,1024]{1,0:T(8,128)(2,1)}, bf16[128,1024]{1,0:T(8,128)(2,1)S(1)}, u32[]{:S(2)}, u32[]{:S(2)}) collective-permute-start(bf16[128,1024]{1,0:T(8,128)(2,1)} %bitcast.21), channel_id=1, source_target_pairs={{0,2},{1,3},{2,0},{3,1},{4,6},{5,7},{6,4},{7,5},{8,10},{9,11},{10,... | collective-permute-start | bytes 786440 | tf_op jit(solution)/shard_map/ppermute | solution.py:25
  5.2 13.3 %collective-permute-start.2 = (bf16[128,1024]{1,0:T(8,128)(2,1)}, bf16[128,1024]{1,0:T(8,128)(2,1)S(1)}, u32[]{:S(2)}, u32[]{:S(2)}) collective-permute-start(bf16[128,1024]{1,0:T(8,128)(2,1)} %bitcast.22), channel_id=1, source_target_pairs={{0,3},{1,2},{2,1},{3,0},{4,7},{5,6},{6,5},{7,4},{8,11},{9,10},{10,... | collective-permute-start | bytes 786440 | tf_op jit(solution)/shard_map/ppermute | solution.py:25
  5.2 1.3 %copy-start.2 = (bf16[1,128,5120]{2,1,0:T(8,128)(2,1)S(1)}, bf16[1,128,5120]{2,1,0:T(8,128)(2,1)}, u32[]{:S(2)}) copy-start(bf16[1,128,5120]{2,1,0:T(8,128)(2,1)} %param.8) | copy-start | bytes 3932164
  6.5 0.7 copy-start.6
  8.7 17.7 %collective-permute-start.6 = (bf16[1280,128]{1,0:T(8,128)(2,1)S(1)}, bf16[1280,128]{1,0:T(8,128)(2,1)S(1)}, u32[]{:S(2)}, u32[]{:S(2)}) collective-permute-start(bf16[1280,128]{1,0:T(8,128)(2,1)S(1)} %get-tuple-element.37), channel_id=1, source_target_pairs={{0,1},{1,0},{2,3},{3,2},{4,5},{5,4},{6,7},{7,6},{8,9},{9,8},{10,11... | collective-permute-start | bytes 983048 | tf_op jit(solution)/shard_map/ppermute | solution.py:25
  10.7 21.1 %collective-permute-start.7 = (bf16[1280,128]{1,0:T(8,128)(2,1)}, bf16[1280,128]{1,0:T(8,128)(2,1)S(1)}, u32[]{:S(2)}, u32[]{:S(2)}) collective-permute-start(bf16[1280,128]{1,0:T(8,128)(2,1)} %get-tuple-element.38), channel_id=1, source_target_pairs={{0,2},{1,3},{2,0},{3,1},{4,6},{5,7},{6,4},{7,5},{8,10},{9,11},{10,... | collective-permute-start | bytes 983048 | tf_op jit(solution)/shard_map/ppermute | solution.py:25
  12.2 2.5 %copy-start = (f32[1,1280,1024]{2,1,0:T(8,128)S(1)}, f32[1,1280,1024]{2,1,0:T(8,128)}, u32[]{:S(2)}) copy-start(f32[1,1280,1024]{2,1,0:T(8,128)} %param.11) | copy-start | bytes 15728644
  14.7 4.4 %copy-start.11 = (bf16[1,128,1024]{2,1,0:T(8,128)(2,1)S(1)}, bf16[1,128,1024]{2,1,0:T(8,128)(2,1)}, u32[]{:S(2)}) copy-start(bf16[1,128,1024]{2,1,0:T(8,128)(2,1)} %param.9) | copy-start | bytes 786436
  14.7 4.4 %copy-start.16 = (s32[4]{0:T(128)S(1)}, s32[4]{0:T(128)}, u32[]{:S(2)}) copy-start(s32[4]{0:T(128)} %plan_ref.1) | copy-start | bytes 52
  15.0 17.3 %copy-start.8 = (s32[1,4]{1,0:T(1,128)S(1)}, s32[1,4]{1,0:T(1,128)}, u32[]{:S(2)}) copy-start(s32[1,4]{1,0:T(1,128)} %param.14) | copy-start | bytes 52
  15.0 17.3 %collective-permute-start.8 = (bf16[1280,128]{1,0:T(8,128)(2,1)}, bf16[1280,128]{1,0:T(8,128)(2,1)}, u32[]{:S(2)}, u32[]{:S(2)}) collective-permute-start(bf16[1280,128]{1,0:T(8,128)(2,1)} %get-tuple-element.39), channel_id=1, source_target_pairs={{0,3},{1,2},{2,1},{3,0},{4,7},{5,6},{6,5},{7,4},{8,11},{9,10},{10,... | collective-permute-start | bytes 983048 | tf_op jit(solution)/shard_map/ppermute | solution.py:25
  17.7 0.7 copy-start.12
  18.4 0.7 copy-start.14
  19.1 1.0 copy-start.13
  20.1 0.9 copy-start.15
  24.0 24.6 %collective-permute-start.3 = (bf16[128,1280]{1,0:T(8,128)(2,1)}, bf16[128,1280]{1,0:T(8,128)(2,1)S(1)}, u32[]{:S(2)}, u32[]{:S(2)}) collective-permute-start(bf16[128,1280]{1,0:T(8,128)(2,1)} %get-tuple-element.33), channel_id=1, source_target_pairs={{0,1},{1,0},{2,3},{3,2},{4,5},{5,4},{6,7},{7,6},{8,9},{9,8},{10,11... | collective-permute-start | bytes 983048 | tf_op jit(solution)/shard_map/ppermute | solution.py:25
  25.2 23.4 %collective-permute-start.4 = (bf16[128,1280]{1,0:T(8,128)(2,1)}, bf16[128,1280]{1,0:T(8,128)(2,1)S(1)}, u32[]{:S(2)}, u32[]{:S(2)}) collective-permute-start(bf16[128,1280]{1,0:T(8,128)(2,1)} %get-tuple-element.34), channel_id=1, source_target_pairs={{0,2},{1,3},{2,0},{3,1},{4,6},{5,7},{6,4},{7,5},{8,10},{9,11},{10,... | collective-permute-start | bytes 983048 | tf_op jit(solution)/shard_map/ppermute | solution.py:25
  26.4 22.2 %collective-permute-start.5 = (bf16[128,1280]{1,0:T(8,128)(2,1)}, bf16[128,1280]{1,0:T(8,128)(2,1)S(1)}, u32[]{:S(2)}, u32[]{:S(2)}) collective-permute-start(bf16[128,1280]{1,0:T(8,128)(2,1)} %get-tuple-element.35), channel_id=1, source_target_pairs={{0,3},{1,2},{2,1},{3,0},{4,7},{5,6},{6,5},{7,4},{8,11},{9,10},{10,... | collective-permute-start | bytes 983048 | tf_op jit(solution)/shard_map/ppermute | solution.py:25
  32.4 2.5 %copy-start.1 = (f32[1,1280,1024]{2,1,0:T(8,128)S(1)}, f32[1,1280,1024]{2,1,0:T(8,128)}, u32[]{:S(2)}) copy-start(f32[1,1280,1024]{2,1,0:T(8,128)} %param.11) | copy-start | bytes 15728644
  34.9 2.5 %copy-start.4 = (f32[1,1280,1024]{2,1,0:T(8,128)S(1)}, f32[1,1280,1024]{2,1,0:T(8,128)}, u32[]{:S(2)}) copy-start(f32[1,1280,1024]{2,1,0:T(8,128)} %param.12) | copy-start | bytes 15728644
  37.3 2.5 %copy-start.5 = (f32[1,1280,1024]{2,1,0:T(8,128)S(1)}, f32[1,1280,1024]{2,1,0:T(8,128)}, u32[]{:S(2)}) copy-start(f32[1,1280,1024]{2,1,0:T(8,128)} %param.13) | copy-start | bytes 15728644
  39.8 8.8 %copy-start.3 = (bf16[1,128,5120]{2,1,0:T(8,128)(2,1)S(1)}, bf16[1,128,5120]{2,1,0:T(8,128)(2,1)}, u32[]{:S(2)}) copy-start(bf16[1,128,5120]{2,1,0:T(8,128)(2,1)} %param.8) | copy-start | bytes 3932164
  39.8 8.8 %copy-start.7 = (f32[1,5120]{1,0:T(1,128)S(1)}, f32[1,5120]{1,0:T(1,128)}, u32[]{:S(2)}) copy-start(f32[1,5120]{1,0:T(1,128)} %gain_ref.3) | copy-start | bytes 61444
  48.6 3.2 %copy-start.9 = (bf16[256,1280]{1,0:T(8,128)(2,1)}, bf16[256,1280]{1,0:T(8,128)(2,1)S(1)}, u32[]{:S(2)}) copy-start(bf16[256,1280]{1,0:T(8,128)(2,1)S(1)} %get-tuple-element.51.part_ref) | copy-start | bytes 1966084
  50.3 3.5 %collective-permute-start.9 = (bf16[64,5120]{1,0:T(8,128)(2,1)}, bf16[64,5120]{1,0:T(8,128)(2,1)S(1)}, u32[]{:S(2)}, u32[]{:S(2)}) collective-permute-start(bf16[64,5120]{1,0:T(8,128)(2,1)} %get-tuple-element.43), channel_id=1, source_target_pairs={{0,4},{4,0},{8,12},{12,8},{16,20},{20,16},{24,28},{28,24},{1,5},{5... | collective-permute-start | bytes 1966088 | tf_op jit(solution)/shard_map/ppermute | solution.py:25
  50.4 18.7 %collective-permute-start.16 = (bf16[256,1280]{1,0:T(8,128)(2,1)}, bf16[256,1280]{1,0:T(8,128)(2,1)S(1)}, u32[]{:S(2)}, u32[]{:S(2)}) collective-permute-start(bf16[256,1280]{1,0:T(8,128)(2,1)} %get-tuple-element.50), channel_id=1, source_target_pairs={{0,3},{1,2},{2,1},{3,0},{4,7},{5,6},{6,5},{7,4},{8,11},{9,10},{10,... | collective-permute-start | bytes 1966088 | tf_op jit(solution)/shard_map/ppermute | solution.py:25
  51.8 6.5 %copy-start.10 = (bf16[256,1280]{1,0:T(8,128)(2,1)S(1)}, bf16[256,1280]{1,0:T(8,128)(2,1)}, u32[]{:S(2)}) copy-start(bf16[256,1280]{1,0:T(8,128)(2,1)} %copy-done.9) | copy-start | bytes 1966084
  51.8 31.2 %collective-permute-start.15 = (bf16[256,1280]{1,0:T(8,128)(2,1)}, bf16[256,1280]{1,0:T(8,128)(2,1)S(1)}, u32[]{:S(2)}, u32[]{:S(2)}) collective-permute-start(bf16[256,1280]{1,0:T(8,128)(2,1)} %get-tuple-element.49), channel_id=1, source_target_pairs={{0,1},{1,0},{2,3},{3,2},{4,5},{5,4},{6,7},{7,6},{8,9},{9,8},{10,11... | collective-permute-start | bytes 1966088 | tf_op jit(solution)/shard_map/ppermute | solution.py:25
  53.6 30.3 %collective-permute-start.14 = (bf16[256,1280]{1,0:T(8,128)(2,1)}, bf16[256,1280]{1,0:T(8,128)(2,1)}, u32[]{:S(2)}, u32[]{:S(2)}) collective-permute-start(bf16[256,1280]{1,0:T(8,128)(2,1)} %get-tuple-element.48), channel_id=1, source_target_pairs={{0,2},{1,3},{2,0},{3,1},{4,6},{5,7},{6,4},{7,5},{8,10},{9,11},{10,... | collective-permute-start | bytes 1966088 | tf_op jit(solution)/shard_map/ppermute | solution.py:25
  54.0 1.4 %collective-permute-start.10 = (bf16[32,5120]{1,0:T(8,128)(2,1)S(1)}, bf16[32,5120]{1,0:T(8,128)(2,1)S(1)}, u32[]{:S(2)}, u32[]{:S(2)}) collective-permute-start(bf16[32,5120]{1,0:T(8,128)(2,1)S(1)} %get-tuple-element.44), channel_id=1, source_target_pairs={{24,8},{8,16},{28,12},{12,20},{25,9},{9,17},{29,13},{13,21},{26,10... | collective-permute-start | bytes 983048 | tf_op jit(solution)/shard_map/ppermute | solution.py:419
  54.7 0.7 collective-permute-start.11
  55.7 30.2 %collective-permute-start.12 = (bf16[32,5120]{1,0:T(8,128)(2,1)S(1)}, bf16[32,5120]{1,0:T(8,128)(2,1)S(1)}, u32[]{:S(2)}, u32[]{:S(2)}) collective-permute-start(bf16[32,5120]{1,0:T(8,128)(2,1)S(1)} %get-tuple-element.46), channel_id=1, source_target_pairs={{8,0},{16,8},{24,16},{12,4},{20,12},{28,20},{9,1},{17,9},{25,17},{... | collective-permute-start | bytes 983048 | tf_op jit(solution)/shard_map/ppermute | solution.py:424
  57.0 36.1 %collective-permute-start.13 = (bf16[32,5120]{1,0:T(8,128)(2,1)S(1)}, bf16[32,5120]{1,0:T(8,128)(2,1)S(1)}, u32[]{:S(2)}, u32[]{:S(2)}) collective-permute-start(bf16[32,5120]{1,0:T(8,128)(2,1)S(1)} %get-tuple-element.47), channel_id=1, source_target_pairs={{16,0},{20,4},{17,1},{21,5},{18,2},{22,6},{19,3},{23,7}} | collective-permute-start | bytes 983048 | tf_op jit(solution)/shard_map/ppermute | solution.py:425
  94.3 2.1 %collective-permute-start.17 = (bf16[64,5120]{1,0:T(8,128)(2,1)S(1)}, bf16[64,5120]{1,0:T(8,128)(2,1)S(1)}, u32[]{:S(2)}, u32[]{:S(2)}) collective-permute-start(bf16[64,5120]{1,0:T(8,128)(2,1)S(1)} %get-tuple-element.53), channel_id=1, source_target_pairs={{0,4},{4,0},{8,12},{12,8},{16,20},{20,16},{24,28},{28,24},{1,5},{5... | collective-permute-start | bytes 1966088 | tf_op jit(solution)/shard_map/ppermute | solution.py:25

commit v2 on v1

--- a/solution.py
+++ b/solution.py
@@ -122,7 +122,7 @@
     return (input_grads[None], moment_new[None], second_new[None], rollout[None])
 
 
-def call(name, body, grid, prefetch, in_specs, out_specs, out_shape, scratch=(), aliases=None, vmem=24, work=1):
+def call(name, body, grid, prefetch, in_specs, out_specs, out_shape, scratch=(), aliases=None, vmem=16, work=1):
     return pl.pallas_call(
         body,
         grid_spec=pltpu.PrefetchScalarGridSpec(
@@ -167,8 +167,22 @@
         out_refs[k][...] = (x * inverse * gain_ref[:, part]).astype(bf16).T
 
 
-def low_body(master_ref, _, low_ref):
-    low_ref[...] = master_ref[...].astype(bf16)
+def low_body(master_ref, moment_ref, _, master_out, moment_out, low_ref, sems):
+    copies = [
+        pltpu.make_async_copy(master_ref, master_out, sems.at[0]),
+        pltpu.make_async_copy(moment_ref, moment_out, sems.at[1]),
+    ]
+    for copy in copies:
+        copy.start()
+    copies[0].wait()
+    low_ref[...] = master_out[...].astype(bf16)
+    copies[1].wait()
+
+
+def load_body(second_ref, _, second_out, sems):
+    copy = pltpu.make_async_copy(second_ref, second_out, sems.at[0])
+    copy.start()
+    copy.wait()
 
 
 def spread_body(count, micro, scale, plan_ref, *refs):
@@ -335,29 +349,42 @@
     normed = [normed[0]] + [swap(normed[k], "fsdp", k) for k in dests]
 
     rows_step = 256
-    low = call(
+    resident = pl.BlockSpec(memory_space=pltpu.VMEM)
+    distant = pl.BlockSpec(memory_space=pltpu.HBM)
+    wide = sds((cols, kv_cols), f32)
+    master_near, moment_near, low = call(
         "low",
         low_body,
-        (cols // rows_step,),
+        (),
         0,
-        [pl.BlockSpec((rows_step, kv_cols), lambda i: (i, 0)), anywhere],
-        pl.BlockSpec((rows_step, kv_cols), lambda i: (i, 0)),
-        sds((cols, kv_cols), bf16),
-    )(master_rows, inverse)
+        [distant, distant, anywhere],
+        [resident] * 3,
+        [wide, wide, sds((cols, kv_cols), bf16)],
+        scratch=[pltpu.SemaphoreType.DMA((2,))],
+    )(master_rows, moment_rows, inverse)
     ordered, *spread = call(
         "spread",
         functools.partial(spread_body, count, plan.shape[0], scale),
-        (1,),
+        (),
         1,
-        [whole((tok_count, kv_cols))] * count + [whole((cols, kv_cols))],
-        [whole((count * tok_count, kv_cols))] + [whole((tok_count, cols))] * count,
+        [resident] * (count + 1),
+        [resident] * (count + 1),
         [sds((count * tok_count, kv_cols), bf16)] + [sds((tok_count, cols), bf16)] * count,
         work=10**10,
     )(plan, *cots, low)
+    (second_near,) = call(
+        "load",
+        load_body,
+        (),
+        0,
+        [distant, anywhere],
+        [resident],
+        [wide],
+        scratch=[pltpu.SemaphoreType.DMA((1,))],
+    )(second_rows, spread[0])
     spread = [spread[0]] + [swap(spread[k], "fsdp", k) for k in dests]
 
     state = pl.BlockSpec((rows_step, kv_cols), lambda i, *_: (i, 0))
-    resident = pl.BlockSpec(memory_space=pltpu.VMEM)
     moment_new, second_new, *rollout_parts, grad_mark = call(
         "grad",
         functools.partial(grad_body, count, head, scale),
@@ -374,7 +401,7 @@
             pltpu.VMEM((rows_step, kv_cols), bf16),
         ],
         vmem=20,
-    )(place, head_owner[0], *normed, ordered, master_rows, moment_rows, second_rows)
+    )(place, head_owner[0], *normed, ordered, master_near, moment_near, second_near)
 
     rollout = ()
     rollout_mark = ()

time: 97.8 us -> 94.4 us (0.965)
  waiting for transfers between devices: 39.4 us -> 33.2 us
  local copies, waits for them, and re-layouts: 15.3 us -> 18.4 us
    ppermute x14, waiting for transfers between devices: 32.2 us -> 24.9 us  [swap(): return lax.ppermute(x, axis, [(i, i ^ k) for i in range(count)])]
    unnamed x34 -> x40, local copies, waits for them, and re-layouts: 15.3 us -> 18.4 us
    pallas_call x4, Pallas kernels: 4.61 us -> 3.52 us  [shards(): call('place', marked_body if final else place_body, (1,), 1, [whole((2 *...]
    ppermute x1, waiting for transfers between devices: 7.14 us -> 8.19 us  [shards(): four = lax.ppermute(four, 'section', chips([(2, 0)]))]
    pallas_call x1 -> x2, Pallas kernels: 0.32 us -> 1.33 us  [the longest x1 0.97 us: shards(): call('low', low_body, (), 0, [distant, distant, anywhere], [resident] * 3...]
  transfers between devices with their start and end apart: 18 -> 18, of which waited for: 7 -> 7; matrix products, arithmetic and copies ran while one was open for 0% -> 0% of each run, Pallas kernels for 19% -> 20%
where the time goes in v2:
time: 94.4 us; the launch traced here: 93.9 us
  waiting for transfers between devices  33.2 us (35%)
  Pallas kernels  22.3 us (24%)
  starting transfers between devices  19.1 us (20%)
  local copies, waits for them, and re-layouts  18.4 us (19%)
    ppermute x14, waiting for transfers between devices, swap(): return lax.ppermute(x, axis, [(i, i ^ k) for i in range(count)])  24.9 us
    unnamed x40, local copies, waits for them, and re-layouts  18.4 us
    ppermute x14, starting transfers between devices, swap(): return lax.ppermute(x, axis, [(i, i ^ k) for i in range(count)])  15.1 us
    pallas_call x1, Pallas kernels, shards(): call('grad', functools.partial(grad_body, count, head, scale), (cols // r...  8.67 us
    ppermute x1, waiting for transfers between devices, shards(): four = lax.ppermute(four, 'section', chips([(2, 0)]))  8.19 us
    pallas_call x4, Pallas kernels, shards(): call('place', marked_body if final else place_body, (1,), 1, [whole((2 *...  3.52 us
    pallas_call x1, Pallas kernels, shards(): call('spread', functools.partial(spread_body, count, plan.shape[0], scale...  3.01 us
  transfers between devices with their start and end apart: 18, of which 7 were waited for; matrix products, arithmetic and copies ran while one was open for 0% of the time, Pallas kernels for 20%

profile of v2, /device:TPU:0, one launch (start us, length us, event | category | flops | bytes accessed | tf_op | source)
XLA Modules:
  0.0 93.9 jit_solution(9459649087368268530)
XLA Ops:
  0.6 3.0 %collective-permute-start = (bf16[128,1024]{1,0:T(8,128)(2,1)}, bf16[128,1024]{1,0:T(8,128)(2,1)S(1)}, u32[]{:S(2)}, u32[]{:S(2)}) collective-permute-start(bf16[128,1024]{1,0:T(8,128)(2,1)} %bitcast.19), channel_id=1, source_target_pairs={{0,1},{1,0},{2,3},{3,2},{4,5},{5,4},{6,7},{7,6},{8,9},{9,8},{10,11... | collective-permute-start | bytes 786440 | tf_op jit(solution)/shard_map/ppermute | solution.py:25
  3.6 1.5 %collective-permute-start.1 = (bf16[128,1024]{1,0:T(8,128)(2,1)}, bf16[128,1024]{1,0:T(8,128)(2,1)S(1)}, u32[]{:S(2)}, u32[]{:S(2)}) collective-permute-start(bf16[128,1024]{1,0:T(8,128)(2,1)} %bitcast.20), channel_id=1, source_target_pairs={{0,2},{1,3},{2,0},{3,1},{4,6},{5,7},{6,4},{7,5},{8,10},{9,11},{10,... | collective-permute-start | bytes 786440 | tf_op jit(solution)/shard_map/ppermute | solution.py:25
  5.2 0.0 collective-permute-start.2
  5.2 1.3 %copy-done.3 = bf16[1,128,5120]{2,1,0:T(8,128)(2,1)S(1)} copy-done((bf16[1,128,5120]{2,1,0:T(8,128)(2,1)S(1)}, bf16[1,128,5120]{2,1,0:T(8,128)(2,1)}, u32[]{:S(2)}) %copy-start.3) | copy-done | bytes 1310744
  6.5 0.7 copy-done.9
  7.2 1.5 %prep.1 = (f32[128,1]{1,0:T(8,128)S(1)}, bf16[1280,128]{1,0:T(8,128)(2,1)S(1)}, bf16[1280,128]{1,0:T(8,128)(2,1)S(1)}, bf16[1280,128]{1,0:T(8,128)(2,1)}, bf16[1280,128]{1,0:T(8,128)(2,1)}) custom-call(s32[1]{0:T(128)} %bitcast.2.place_ref, bf16[128,5120]{1,0:T(8,128)(2,1)S(1)} %bitcast.16, f32[1,5120]{1,0:T(1,128)S(1)} %copy-done.9), custom_call_target="tpu_custom_call" | custom-call | flops 1 | bytes 1 | tf_op jit(solution)/shard_map/prep/pallas_call | solution.py:340
  8.7 1.9 %collective-permute-start.6 = (bf16[1280,128]{1,0:T(8,128)(2,1)S(1)}, bf16[1280,128]{1,0:T(8,128)(2,1)S(1)}, u32[]{:S(2)}, u32[]{:S(2)}) collective-permute-start(bf16[1280,128]{1,0:T(8,128)(2,1)S(1)} %get-tuple-element.41), channel_id=1, source_target_pairs={{0,1},{1,0},{2,3},{3,2},{4,5},{5,4},{6,7},{7,6},{8,9},{9,8},{10,11... | collective-permute-start | bytes 983048 | tf_op jit(solution)/shard_map/ppermute | solution.py:25
  10.7 1.5 %collective-permute-start.7 = (bf16[1280,128]{1,0:T(8,128)(2,1)}, bf16[1280,128]{1,0:T(8,128)(2,1)S(1)}, u32[]{:S(2)}, u32[]{:S(2)}) collective-permute-start(bf16[1280,128]{1,0:T(8,128)(2,1)} %get-tuple-element.42), channel_id=1, source_target_pairs={{0,2},{1,3},{2,0},{3,1},{4,6},{5,7},{6,4},{7,5},{8,10},{9,11},{10,... | collective-permute-start | bytes 983048 | tf_op jit(solution)/shard_map/ppermute | solution.py:25
  12.2 2.5 %copy-done = f32[1,1280,1024]{2,1,0:T(8,128)S(1)} copy-done((f32[1,1280,1024]{2,1,0:T(8,128)S(1)}, f32[1,1280,1024]{2,1,0:T(8,128)}, u32[]{:S(2)}) %copy-start) | copy-done | bytes 5242904
  14.7 2.5 %copy-done.1 = f32[1,1280,1024]{2,1,0:T(8,128)S(1)} copy-done((f32[1,1280,1024]{2,1,0:T(8,128)S(1)}, f32[1,1280,1024]{2,1,0:T(8,128)}, u32[]{:S(2)}) %copy-start.1) | copy-done | bytes 5242904
  17.2 1.0 %low.1 = (f32[1280,1024]{1,0:T(8,128)S(1)}, f32[1280,1024]{1,0:T(8,128)S(1)}, bf16[1280,1024]{1,0:T(8,128)(2,1)S(1)}) custom-call(f32[1280,1024]{1,0:T(8,128)S(1)} %bitcast.13, f32[1280,1024]{1,0:T(8,128)S(1)} %bitcast.14, f32[128,1]{1,0:T(8,128)S(1)} %get-tuple-element.34._.inv_ref), custom_call_target="tpu_custom_call" | custom-call | flops 1 | bytes 1 | tf_op jit(solution)/shard_map/low/pallas_call | solution.py:355
  18.2 0.0 copy-start.5
  18.2 0.0 copy-start.7
  18.2 0.0 collective-permute-done.refs_1_
  18.2 0.1 collective-permute-start.8
  18.3 0.0 collective-permute-done.1.refs_2_
  18.3 0.9 copy-done.15
  19.2 0.0 collective-permute-done.2.refs_3_
  19.2 1.2 %copy-done.17 = bf16[128,1024]{1,0:T(8,128)(2,1)} copy-done((bf16[128,1024]{1,0:T(8,128)(2,1)}, bf16[128,1024]{1,0:T(8,128)(2,1)S(1)}, u32[]{:S(2)}) %copy-start.17) | copy-done | bytes 262168
  20.4 1.1 %copy-done.16 = bf16[128,1024]{1,0:T(8,128)(2,1)S(1)} copy-done((bf16[128,1024]{1,0:T(8,128)(2,1)S(1)}, bf16[128,1024]{1,0:T(8,128)(2,1)}, u32[]{:S(2)}) %copy-start.16) | copy-done | bytes 262168
  21.5 1.1 %copy-done.18 = bf16[128,1024]{1,0:T(8,128)(2,1)S(1)} copy-done((bf16[128,1024]{1,0:T(8,128)(2,1)S(1)}, bf16[128,1024]{1,0:T(8,128)(2,1)}, u32[]{:S(2)}) %copy-start.18) | copy-done | bytes 262168
  22.7 3.0 %spread.1 = (bf16[512,1024]{1,0:T(8,128)(2,1)S(1)}, bf16[128,1280]{1,0:T(8,128)(2,1)S(1)}, bf16[128,1280]{1,0:T(8,128)(2,1)}, bf16[128,1280]{1,0:T(8,128)(2,1)}, bf16[128,1280]{1,0:T(8,128)(2,1)}) custom-call(s32[4]{0:T(128)S(1)} %copy-done.19, bf16[128,1024]{1,0:T(8,128)(2,1)S(1)} %bitcast.22, bf16[128,1024]{1,0:T(8,128)(2,1)S(1)} %collective-permute-done.refs_1_, ...), custom_call_target="tpu_custom_call" | custom-call | flops 10000000000 | bytes 1 | tf_op jit(solution)/shard_map/spread/pallas_call | solution.py:365
  25.7 2.0 %collective-permute-start.3 = (bf16[128,1280]{1,0:T(8,128)(2,1)}, bf16[128,1280]{1,0:T(8,128)(2,1)S(1)}, u32[]{:S(2)}, u32[]{:S(2)}) collective-permute-start(bf16[128,1280]{1,0:T(8,128)(2,1)} %get-tuple-element.37), channel_id=1, source_target_pairs={{0,1},{1,0},{2,3},{3,2},{4,5},{5,4},{6,7},{7,6},{8,9},{9,8},{10,11... | collective-permute-start | bytes 983048 | tf_op jit(solution)/shard_map/ppermute | solution.py:25
  27.7 0.7 collective-permute-start.4
  28.4 0.0 collective-permute-done.6.refs_1_
  28.4 0.8 collective-permute-start.5
  29.2 2.5 %copy-done.2 = f32[1,1280,1024]{2,1,0:T(8,128)S(1)} copy-done((f32[1,1280,1024]{2,1,0:T(8,128)S(1)}, f32[1,1280,1024]{2,1,0:T(8,128)}, u32[]{:S(2)}) %copy-start.2) | copy-done | bytes 5242904
  31.7 0.4 load.1.refs_7_
  32.1 0.0 collective-permute-done.7.refs_2_
  32.1 0.2 collective-permute-done.8.refs_3_
  32.4 1.9 %copy-done.6 = f32[1280,1024]{1,0:T(8,128)S(1)} copy-done((f32[1280,1024]{1,0:T(8,128)S(1)}, f32[1280,1024]{1,0:T(8,128)}, u32[]{:S(2)}) %copy-start.6) | copy-done | bytes 5242904
  34.2 1.6 %copy-done.8 = f32[1280,1024]{1,0:T(8,128)S(1)} copy-done((f32[1280,1024]{1,0:T(8,128)S(1)}, f32[1280,1024]{1,0:T(8,128)}, u32[]{:S(2)}) %copy-start.8) | copy-done | bytes 5242904
  35.8 8.7 %grad.1 = (f32[1280,1024]{1,0:T(8,128)}, f32[1280,1024]{1,0:T(8,128)}, bf16[256,1280]{1,0:T(8,128)(2,1)S(1)}, bf16[256,1280]{1,0:T(8,128)(2,1)}, bf16[256,1280]{...) custom-call(s32[1]{0:T(128)} %bitcast.2.place_ref, s32[4]{0:T(128)S(1)} %bitcast.18, ...), custom_call_target="tpu_custom_call" | custom-call | flops 1 | bytes 1 | tf_op jit(solution)/shard_map/grad/pallas_call | solution.py:388
  44.5 0.0 collective-permute-done.3.refs_1_
  44.5 0.8 collective-permute-done.4.refs_2_
  45.3 0.0 collective-permute-done.5.refs_3_
  45.3 1.7 %own.1 = (bf16[64,5120]{1,0:T(8,128)(2,1)S(1)}, bf16[64,5120]{1,0:T(8,128)(2,1)}) custom-call(s32[1]{0:T(128)} %bitcast.2.place_ref, s32[1]{0:T(128)} %bitcast.core_ref.place_ref, bf16[128,5120]{1,0:T(8,128)(2,1)S(1)} %bitcast.17, f32[1,5120]{1,0:T(1,128)S(1)} %copy-done.10, f32[128,1]{1,0:T(8,128)S(1)} %get-tuple-element.34._.inv_ref, ...), custom_call_target="tpu_custom_call" | custom-call | flops 1 | bytes 1 | tf_op jit(solution)/shard_map/own/pallas_call | solution.py:424
  47.0 0.0 collective-permute-start.9
  47.0 1.5 %collective-permute-start.16 = (bf16[256,1280]{1,0:T(8,128)(2,1)}, bf16[256,1280]{1,0:T(8,128)(2,1)S(1)}, u32[]{:S(2)}, u32[]{:S(2)}) collective-permute-start(bf16[256,1280]{1,0:T(8,128)(2,1)} %get-tuple-element.56), channel_id=1, source_target_pairs={{0,3},{1,2},{2,1},{3,0},{4,7},{5,6},{6,5},{7,4},{8,11},{9,10},{10,... | collective-permute-start | bytes 1966088 | tf_op jit(solution)/shard_map/ppermute | solution.py:25
  48.5 1.5 %collective-permute-start.15 = (bf16[256,1280]{1,0:T(8,128)(2,1)}, bf16[256,1280]{1,0:T(8,128)(2,1)S(1)}, u32[]{:S(2)}, u32[]{:S(2)}) collective-permute-start(bf16[256,1280]{1,0:T(8,128)(2,1)} %get-tuple-element.55), channel_id=1, source_target_pairs={{0,1},{1,0},{2,3},{3,2},{4,5},{5,4},{6,7},{7,6},{8,9},{9,8},{10,11... | collective-permute-start | bytes 1966088 | tf_op jit(solution)/shard_map/ppermute | solution.py:25
  50.0 0.5 collective-permute-start.14
  50.5 0.0 collective-permute-done.9.got_ref
  50.5 0.2 pair.1
  50.7 0.7 collective-permute-start.10
  51.4 0.7 collective-permute-start.11
  52.1 0.0 collective-permute-done.10.one_ref
  52.1 0.0 collective-permute-done.11.two_ref
  52.1 0.2 middle.1
  52.3 1.3 %collective-permute-start.12 = (bf16[32,5120]{1,0:T(8,128)(2,1)S(1)}, bf16[32,5120]{1,0:T(8,128)(2,1)S(1)}, u32[]{:S(2)}, u32[]{:S(2)}) collective-permute-start(bf16[32,5120]{1,0:T(8,128)(2,1)S(1)} %get-tuple-element.52), channel_id=1, source_target_pairs={{8,0},{16,8},{24,16},{12,4},{20,12},{28,20},{9,1},{17,9},{25,17},{... | collective-permute-start | bytes 983048 | tf_op jit(solution)/shard_map/ppermute | solution.py:451
  53.6 1.3 %collective-permute-start.13 = (bf16[32,5120]{1,0:T(8,128)(2,1)S(1)}, bf16[32,5120]{1,0:T(8,128)(2,1)S(1)}, u32[]{:S(2)}, u32[]{:S(2)}) collective-permute-start(bf16[32,5120]{1,0:T(8,128)(2,1)S(1)} %get-tuple-element.53), channel_id=1, source_target_pairs={{16,0},{20,4},{17,1},{21,5},{18,2},{22,6},{19,3},{23,7}} | collective-permute-start | bytes 983048 | tf_op jit(solution)/shard_map/ppermute | solution.py:452
  55.0 1.1 %copy-done.13 = bf16[256,1280]{1,0:T(8,128)(2,1)S(1)} copy-done((bf16[256,1280]{1,0:T(8,128)(2,1)S(1)}, bf16[256,1280]{1,0:T(8,128)(2,1)}, u32[]{:S(2)}) %copy-start.13) | copy-done | bytes 655384
  56.0 0.9 place.4.refs_0_
  56.9 8.8 %collective-permute-done.16.part_ref = bf16[256,1280]{1,0:T(8,128)(2,1)S(1)} collective-permute-done((bf16[256,1280]{1,0:T(8,128)(2,1)}, bf16[256,1280]{1,0:T(8,128)(2,1)S(1)}, u32[]{:S(2)}, u32[]{:S(2)}) %collective-permute-start.16) | collective-permute-done | bytes 655392 | tf_op jit(solution)/shard_map/ppermute | solution.py:25
  65.7 0.9 place.5.refs_0_
  66.6 12.8 %collective-permute-done.15.part_ref = bf16[256,1280]{1,0:T(8,128)(2,1)S(1)} collective-permute-done((bf16[256,1280]{1,0:T(8,128)(2,1)}, bf16[256,1280]{1,0:T(8,128)(2,1)S(1)}, u32[]{:S(2)}, u32[]{:S(2)}) %collective-permute-start.15) | collective-permute-done | bytes 655392 | tf_op jit(solution)/shard_map/ppermute | solution.py:25
  79.4 0.9 place.6._
  80.3 0.0 collective-permute-done.14.part_ref
  80.3 0.9 place.7
  81.2 0.2 collective-permute-done.12.three_ref
  81.4 8.2 %collective-permute-done.13.four_ref = bf16[32,5120]{1,0:T(8,128)(2,1)S(1)} collective-permute-done((bf16[32,5120]{1,0:T(8,128)(2,1)S(1)}, bf16[32,5120]{1,0:T(8,128)(2,1)S(1)}, u32[]{:S(2)}, u32[]{:S(2)}) %collective-permute-start.13) | collective-permute-done | bytes 327712 | tf_op jit(solution)/shard_map/ppermute | solution.py:452
  89.6 1.3 %last.1 = (bf16[128,5120]{1,0:T(8,128)(2,1)}, bf16[64,5120]{1,0:T(8,128)(2,1)S(1)}) custom-call(s32[1]{0:T(128)} %bitcast.1.chip_ref, s32[1]{0:T(128)} %bitcast.core_ref.place_ref, bf16[64,5120]{1,0:T(8,128)(2,1)S(1)} %get-tuple-element.48.keep_ref, bf16[64,5120]{1,0:T(8,128)(2,1)S(1)} %collective-permute-done.9.got_ref, ...), custom_call_target="tpu_custom_call" | custom-call | flops 1 | bytes 1 | tf_op jit(solution)/shard_map/last/pallas_call | solution.py:453
  90.9 0.0 collective-permute-start.17
  90.9 2.1 %collective-permute-done.17.part_ref = bf16[64,5120]{1,0:T(8,128)(2,1)S(1)} collective-permute-done((bf16[64,5120]{1,0:T(8,128)(2,1)S(1)}, bf16[64,5120]{1,0:T(8,128)(2,1)S(1)}, u32[]{:S(2)}, u32[]{:S(2)}) %collective-permute-start.17) | collective-permute-done | bytes 655392 | tf_op jit(solution)/shard_map/ppermute | solution.py:25
  93.0 0.9 join.1
  (26 shorter events, 0.0 us)
Async XLA Ops:
  0.6 17.6 %collective-permute-start = (bf16[128,1024]{1,0:T(8,128)(2,1)}, bf16[128,1024]{1,0:T(8,128)(2,1)S(1)}, u32[]{:S(2)}, u32[]{:S(2)}) collective-permute-start(bf16[128,1024]{1,0:T(8,128)(2,1)} %bitcast.19), channel_id=1, source_target_pairs={{0,1},{1,0},{2,3},{3,2},{4,5},{5,4},{6,7},{7,6},{8,9},{9,8},{10,11... | collective-permute-start | bytes 786440 | tf_op jit(solution)/shard_map/ppermute | solution.py:25
  3.6 14.6 %collective-permute-start.1 = (bf16[128,1024]{1,0:T(8,128)(2,1)}, bf16[128,1024]{1,0:T(8,128)(2,1)S(1)}, u32[]{:S(2)}, u32[]{:S(2)}) collective-permute-start(bf16[128,1024]{1,0:T(8,128)(2,1)} %bitcast.20), channel_id=1, source_target_pairs={{0,2},{1,3},{2,0},{3,1},{4,6},{5,7},{6,4},{7,5},{8,10},{9,11},{10,... | collective-permute-start | bytes 786440 | tf_op jit(solution)/shard_map/ppermute | solution.py:25
  5.2 14.0 %collective-permute-start.2 = (bf16[128,1024]{1,0:T(8,128)(2,1)}, bf16[128,1024]{1,0:T(8,128)(2,1)S(1)}, u32[]{:S(2)}, u32[]{:S(2)}) collective-permute-start(bf16[128,1024]{1,0:T(8,128)(2,1)} %bitcast.21), channel_id=1, source_target_pairs={{0,3},{1,2},{2,1},{3,0},{4,7},{5,6},{6,5},{7,4},{8,11},{9,10},{10,... | collective-permute-start | bytes 786440 | tf_op jit(solution)/shard_map/ppermute | solution.py:25
  5.2 1.3 %copy-start.3 = (bf16[1,128,5120]{2,1,0:T(8,128)(2,1)S(1)}, bf16[1,128,5120]{2,1,0:T(8,128)(2,1)}, u32[]{:S(2)}) copy-start(bf16[1,128,5120]{2,1,0:T(8,128)(2,1)} %param.8) | copy-start | bytes 3932164
  6.5 0.7 copy-start.9
  8.7 19.7 %collective-permute-start.6 = (bf16[1280,128]{1,0:T(8,128)(2,1)S(1)}, bf16[1280,128]{1,0:T(8,128)(2,1)S(1)}, u32[]{:S(2)}, u32[]{:S(2)}) collective-permute-start(bf16[1280,128]{1,0:T(8,128)(2,1)S(1)} %get-tuple-element.41), channel_id=1, source_target_pairs={{0,1},{1,0},{2,3},{3,2},{4,5},{5,4},{6,7},{7,6},{8,9},{9,8},{10,11... | collective-permute-start | bytes 983048 | tf_op jit(solution)/shard_map/ppermute | solution.py:25
  10.7 21.4 %collective-permute-start.7 = (bf16[1280,128]{1,0:T(8,128)(2,1)}, bf16[1280,128]{1,0:T(8,128)(2,1)S(1)}, u32[]{:S(2)}, u32[]{:S(2)}) collective-permute-start(bf16[1280,128]{1,0:T(8,128)(2,1)} %get-tuple-element.42), channel_id=1, source_target_pairs={{0,2},{1,3},{2,0},{3,1},{4,6},{5,7},{6,4},{7,5},{8,10},{9,11},{10,... | collective-permute-start | bytes 983048 | tf_op jit(solution)/shard_map/ppermute | solution.py:25
  12.2 2.5 %copy-start = (f32[1,1280,1024]{2,1,0:T(8,128)S(1)}, f32[1,1280,1024]{2,1,0:T(8,128)}, u32[]{:S(2)}) copy-start(f32[1,1280,1024]{2,1,0:T(8,128)} %param.11) | copy-start | bytes 15728644
  14.7 2.5 %copy-start.1 = (f32[1,1280,1024]{2,1,0:T(8,128)S(1)}, f32[1,1280,1024]{2,1,0:T(8,128)}, u32[]{:S(2)}) copy-start(f32[1,1280,1024]{2,1,0:T(8,128)} %param.12) | copy-start | bytes 15728644
  17.2 3.2 %copy-start.14 = (bf16[1,128,1024]{2,1,0:T(8,128)(2,1)S(1)}, bf16[1,128,1024]{2,1,0:T(8,128)(2,1)}, u32[]{:S(2)}) copy-start(bf16[1,128,1024]{2,1,0:T(8,128)(2,1)} %param.9) | copy-start | bytes 786436
  17.2 3.2 %copy-start.19 = (s32[4]{0:T(128)S(1)}, s32[4]{0:T(128)}, u32[]{:S(2)}) copy-start(s32[4]{0:T(128)} %plan_ref.1) | copy-start | bytes 52
  18.2 7.5 %copy-start.5 = (f32[1280,1024]{1,0:T(8,128)}, f32[1280,1024]{1,0:T(8,128)S(1)}, u32[]{:S(2)}) copy-start(f32[1280,1024]{1,0:T(8,128)S(1)} %get-tuple-element.45.refs_5_) | copy-start | bytes 15728644
  18.2 7.5 %copy-start.7 = (f32[1280,1024]{1,0:T(8,128)}, f32[1280,1024]{1,0:T(8,128)S(1)}, u32[]{:S(2)}) copy-start(f32[1280,1024]{1,0:T(8,128)S(1)} %get-tuple-element.46.refs_6_) | copy-start | bytes 15728644
  18.2 14.2 %collective-permute-start.8 = (bf16[1280,128]{1,0:T(8,128)(2,1)}, bf16[1280,128]{1,0:T(8,128)(2,1)}, u32[]{:S(2)}, u32[]{:S(2)}) collective-permute-start(bf16[1280,128]{1,0:T(8,128)(2,1)} %get-tuple-element.43), channel_id=1, source_target_pairs={{0,3},{1,2},{2,1},{3,0},{4,7},{5,6},{6,5},{7,4},{8,11},{9,10},{10,... | collective-permute-start | bytes 983048 | tf_op jit(solution)/shard_map/ppermute | solution.py:25
  18.3 0.9 copy-start.15
  19.2 1.2 %copy-start.17 = (bf16[128,1024]{1,0:T(8,128)(2,1)}, bf16[128,1024]{1,0:T(8,128)(2,1)S(1)}, u32[]{:S(2)}) copy-start(bf16[128,1024]{1,0:T(8,128)(2,1)S(1)} %collective-permute-done.2.refs_3_) | copy-start | bytes 786436
  20.4 1.1 %copy-start.16 = (bf16[128,1024]{1,0:T(8,128)(2,1)S(1)}, bf16[128,1024]{1,0:T(8,128)(2,1)}, u32[]{:S(2)}) copy-start(bf16[128,1024]{1,0:T(8,128)(2,1)} %copy-done.15) | copy-start | bytes 786436
  21.5 1.1 %copy-start.18 = (bf16[128,1024]{1,0:T(8,128)(2,1)S(1)}, bf16[128,1024]{1,0:T(8,128)(2,1)}, u32[]{:S(2)}) copy-start(bf16[128,1024]{1,0:T(8,128)(2,1)} %copy-done.17) | copy-start | bytes 786436
  25.7 18.8 %collective-permute-start.3 = (bf16[128,1280]{1,0:T(8,128)(2,1)}, bf16[128,1280]{1,0:T(8,128)(2,1)S(1)}, u32[]{:S(2)}, u32[]{:S(2)}) collective-permute-start(bf16[128,1280]{1,0:T(8,128)(2,1)} %get-tuple-element.37), channel_id=1, source_target_pairs={{0,1},{1,0},{2,3},{3,2},{4,5},{5,4},{6,7},{7,6},{8,9},{9,8},{10,11... | collective-permute-start | bytes 983048 | tf_op jit(solution)/shard_map/ppermute | solution.py:25
  27.7 17.6 %collective-permute-start.4 = (bf16[128,1280]{1,0:T(8,128)(2,1)}, bf16[128,1280]{1,0:T(8,128)(2,1)S(1)}, u32[]{:S(2)}, u32[]{:S(2)}) collective-permute-start(bf16[128,1280]{1,0:T(8,128)(2,1)} %get-tuple-element.38), channel_id=1, source_target_pairs={{0,2},{1,3},{2,0},{3,1},{4,6},{5,7},{6,4},{7,5},{8,10},{9,11},{10,... | collective-permute-start | bytes 983048 | tf_op jit(solution)/shard_map/ppermute | solution.py:25
  28.4 16.9 %collective-permute-start.5 = (bf16[128,1280]{1,0:T(8,128)(2,1)}, bf16[128,1280]{1,0:T(8,128)(2,1)S(1)}, u32[]{:S(2)}, u32[]{:S(2)}) collective-permute-start(bf16[128,1280]{1,0:T(8,128)(2,1)} %get-tuple-element.39), channel_id=1, source_target_pairs={{0,3},{1,2},{2,1},{3,0},{4,7},{5,6},{6,5},{7,4},{8,11},{9,10},{10,... | collective-permute-start | bytes 983048 | tf_op jit(solution)/shard_map/ppermute | solution.py:25
  29.2 2.5 %copy-start.2 = (f32[1,1280,1024]{2,1,0:T(8,128)S(1)}, f32[1,1280,1024]{2,1,0:T(8,128)}, u32[]{:S(2)}) copy-start(f32[1,1280,1024]{2,1,0:T(8,128)} %param.13) | copy-start | bytes 15728644
  31.7 2.5 %copy-start.6 = (f32[1280,1024]{1,0:T(8,128)S(1)}, f32[1280,1024]{1,0:T(8,128)}, u32[]{:S(2)}) copy-start(f32[1280,1024]{1,0:T(8,128)} %copy-done.5) | copy-start | bytes 15728644
  31.7 4.1 %copy-start.8 = (f32[1280,1024]{1,0:T(8,128)S(1)}, f32[1280,1024]{1,0:T(8,128)}, u32[]{:S(2)}) copy-start(f32[1280,1024]{1,0:T(8,128)} %copy-done.7) | copy-start | bytes 15728644
  31.7 4.1 %copy-start.11 = (s32[1,4]{1,0:T(1,128)S(1)}, s32[1,4]{1,0:T(1,128)}, u32[]{:S(2)}) copy-start(s32[1,4]{1,0:T(1,128)} %param.14) | copy-start | bytes 52
  35.8 9.5 %copy-start.4 = (bf16[1,128,5120]{2,1,0:T(8,128)(2,1)S(1)}, bf16[1,128,5120]{2,1,0:T(8,128)(2,1)}, u32[]{:S(2)}) copy-start(bf16[1,128,5120]{2,1,0:T(8,128)(2,1)} %param.8) | copy-start | bytes 3932164
  35.8 9.5 %copy-start.10 = (f32[1,5120]{1,0:T(1,128)S(1)}, f32[1,5120]{1,0:T(1,128)}, u32[]{:S(2)}) copy-start(f32[1,5120]{1,0:T(1,128)} %gain_ref.3) | copy-start | bytes 61444
  44.5 4.1 %copy-start.12 = (bf16[256,1280]{1,0:T(8,128)(2,1)}, bf16[256,1280]{1,0:T(8,128)(2,1)S(1)}, u32[]{:S(2)}) copy-start(bf16[256,1280]{1,0:T(8,128)(2,1)S(1)} %get-tuple-element.57.part_ref) | copy-start | bytes 1966084
  47.0 3.5 %collective-permute-start.9 = (bf16[64,5120]{1,0:T(8,128)(2,1)}, bf16[64,5120]{1,0:T(8,128)(2,1)S(1)}, u32[]{:S(2)}, u32[]{:S(2)}) collective-permute-start(bf16[64,5120]{1,0:T(8,128)(2,1)} %get-tuple-element.49), channel_id=1, source_target_pairs={{0,4},{4,0},{8,12},{12,8},{16,20},{20,16},{24,28},{28,24},{1,5},{5... | collective-permute-start | bytes 1966088 | tf_op jit(solution)/shard_map/ppermute | solution.py:25
  47.0 18.7 %collective-permute-start.16 = (bf16[256,1280]{1,0:T(8,128)(2,1)}, bf16[256,1280]{1,0:T(8,128)(2,1)S(1)}, u32[]{:S(2)}, u32[]{:S(2)}) collective-permute-start(bf16[256,1280]{1,0:T(8,128)(2,1)} %get-tuple-element.56), channel_id=1, source_target_pairs={{0,3},{1,2},{2,1},{3,0},{4,7},{5,6},{6,5},{7,4},{8,11},{9,10},{10,... | collective-permute-start | bytes 1966088 | tf_op jit(solution)/shard_map/ppermute | solution.py:25
  48.5 30.9 %collective-permute-start.15 = (bf16[256,1280]{1,0:T(8,128)(2,1)}, bf16[256,1280]{1,0:T(8,128)(2,1)S(1)}, u32[]{:S(2)}, u32[]{:S(2)}) collective-permute-start(bf16[256,1280]{1,0:T(8,128)(2,1)} %get-tuple-element.55), channel_id=1, source_target_pairs={{0,1},{1,0},{2,3},{3,2},{4,5},{5,4},{6,7},{7,6},{8,9},{9,8},{10,11... | collective-permute-start | bytes 1966088 | tf_op jit(solution)/shard_map/ppermute | solution.py:25
  50.0 30.3 %collective-permute-start.14 = (bf16[256,1280]{1,0:T(8,128)(2,1)}, bf16[256,1280]{1,0:T(8,128)(2,1)S(1)}, u32[]{:S(2)}, u32[]{:S(2)}) collective-permute-start(bf16[256,1280]{1,0:T(8,128)(2,1)} %get-tuple-element.54), channel_id=1, source_target_pairs={{0,2},{1,3},{2,0},{3,1},{4,6},{5,7},{6,4},{7,5},{8,10},{9,11},{10,... | collective-permute-start | bytes 1966088 | tf_op jit(solution)/shard_map/ppermute | solution.py:25
  50.7 1.4 %collective-permute-start.10 = (bf16[32,5120]{1,0:T(8,128)(2,1)S(1)}, bf16[32,5120]{1,0:T(8,128)(2,1)S(1)}, u32[]{:S(2)}, u32[]{:S(2)}) collective-permute-start(bf16[32,5120]{1,0:T(8,128)(2,1)S(1)} %get-tuple-element.50), channel_id=1, source_target_pairs={{24,8},{8,16},{28,12},{12,20},{25,9},{9,17},{29,13},{13,21},{26,10... | collective-permute-start | bytes 983048 | tf_op jit(solution)/shard_map/ppermute | solution.py:446
  51.4 0.7 collective-permute-start.11
  52.3 29.1 %collective-permute-start.12 = (bf16[32,5120]{1,0:T(8,128)(2,1)S(1)}, bf16[32,5120]{1,0:T(8,128)(2,1)S(1)}, u32[]{:S(2)}, u32[]{:S(2)}) collective-permute-start(bf16[32,5120]{1,0:T(8,128)(2,1)S(1)} %get-tuple-element.52), channel_id=1, source_target_pairs={{8,0},{16,8},{24,16},{12,4},{20,12},{28,20},{9,1},{17,9},{25,17},{... | collective-permute-start | bytes 983048 | tf_op jit(solution)/shard_map/ppermute | solution.py:451
  53.6 36.0 %collective-permute-start.13 = (bf16[32,5120]{1,0:T(8,128)(2,1)S(1)}, bf16[32,5120]{1,0:T(8,128)(2,1)S(1)}, u32[]{:S(2)}, u32[]{:S(2)}) collective-permute-start(bf16[32,5120]{1,0:T(8,128)(2,1)S(1)} %get-tuple-element.53), channel_id=1, source_target_pairs={{16,0},{20,4},{17,1},{21,5},{18,2},{22,6},{19,3},{23,7}} | collective-permute-start | bytes 983048 | tf_op jit(solution)/shard_map/ppermute | solution.py:452
  54.9 1.1 %copy-start.13 = (bf16[256,1280]{1,0:T(8,128)(2,1)S(1)}, bf16[256,1280]{1,0:T(8,128)(2,1)}, u32[]{:S(2)}) copy-start(bf16[256,1280]{1,0:T(8,128)(2,1)} %copy-done.12) | copy-start | bytes 1966084
  90.9 2.1 %collective-permute-start.17 = (bf16[64,5120]{1,0:T(8,128)(2,1)S(1)}, bf16[64,5120]{1,0:T(8,128)(2,1)S(1)}, u32[]{:S(2)}, u32[]{:S(2)}) collective-permute-start(bf16[64,5120]{1,0:T(8,128)(2,1)S(1)} %get-tuple-element.59), channel_id=1, source_target_pairs={{0,4},{4,0},{8,12},{12,8},{16,20},{20,16},{24,28},{28,24},{1,5},{5... | collective-permute-start | bytes 1966088 | tf_op jit(solution)/shard_map/ppermute | solution.py:25

commit v3 on v1

--- a/solution.py
+++ b/solution.py
@@ -122,7 +122,7 @@
     return (input_grads[None], moment_new[None], second_new[None], rollout[None])
 
 
-def call(name, body, grid, prefetch, in_specs, out_specs, out_shape, scratch=(), aliases=None, vmem=24, work=1):
+def call(name, body, grid, prefetch, in_specs, out_specs, out_shape, scratch=(), aliases=None, vmem=16, work=1):
     return pl.pallas_call(
         body,
         grid_spec=pltpu.PrefetchScalarGridSpec(
@@ -151,7 +151,7 @@
     return pl.ds(pl.multiple_of((place ^ k) * cols, 128), cols)
 
 
-def prep_body(count, place_ref, tok_ref, gain_ref, inv_ref, *out_refs):
+def prep_body(count, place_ref, core_ref, chip_ref, tok_ref, gain_ref, inv_ref, *out_refs):
     place = place_ref[0]
     width = tok_ref.shape[1]
     cols = width // count
@@ -319,6 +319,7 @@
     sds = jax.ShapeDtypeStruct
     dests = range(1, count)
     anywhere = pl.BlockSpec(memory_space=pl.ANY)
+    resident = pl.BlockSpec(memory_space=pltpu.VMEM)
     mark = sds((8, 128), f32)
 
     cots = [cot_rows] + [swap(cot_rows, "fsdp", k) for k in dests]
@@ -327,11 +328,11 @@
         "prep",
         functools.partial(prep_body, count),
         (1,),
-        1,
+        3,
         [whole((tok_count, width)), whole((1, width))],
         [whole((tok_count, 1))] + [whole((cols, tok_count))] * count,
         [sds((tok_count, 1), f32)] + [sds((cols, tok_count), bf16)] * count,
-    )(place, tok_rows, norm_gain)
+    )(place, core, chip, tok_rows, norm_gain)
     normed = [normed[0]] + [swap(normed[k], "fsdp", k) for k in dests]
 
     rows_step = 256
@@ -347,17 +348,16 @@
     ordered, *spread = call(
         "spread",
         functools.partial(spread_body, count, plan.shape[0], scale),
-        (1,),
+        (),
         1,
-        [whole((tok_count, kv_cols))] * count + [whole((cols, kv_cols))],
-        [whole((count * tok_count, kv_cols))] + [whole((tok_count, cols))] * count,
+        [resident] * (count + 1),
+        [resident] * (count + 1),
         [sds((count * tok_count, kv_cols), bf16)] + [sds((tok_count, cols), bf16)] * count,
         work=10**10,
     )(plan, *cots, low)
     spread = [spread[0]] + [swap(spread[k], "fsdp", k) for k in dests]
 
     state = pl.BlockSpec((rows_step, kv_cols), lambda i, *_: (i, 0))
-    resident = pl.BlockSpec(memory_space=pltpu.VMEM)
     moment_new, second_new, *rollout_parts, grad_mark = call(
         "grad",
         functools.partial(grad_body, count, head, scale),

time: 97.8 us -> 93.8 us (0.959)
  local copies, waits for them, and re-layouts: 15.3 us -> 4.59 us
  waiting for transfers between devices: 39.4 us -> 49.1 us
  Pallas kernels: 22.5 us -> 18.1 us
  starting transfers between devices: 19.4 us -> 20.8 us
    unnamed x34 -> x28, local copies, waits for them, and re-layouts: 15.3 us -> 4.59 us
    ppermute x14, waiting for transfers between devices: 32.2 us -> 40.4 us  [swap(): return lax.ppermute(x, axis, [(i, i ^ k) for i in range(count)])]
    ppermute x14, starting transfers between devices: 15.4 us -> 16.9 us  [swap(): return lax.ppermute(x, axis, [(i, i ^ k) for i in range(count)])]
    pallas_call x1, Pallas kernels: 8.75 us -> 7.6 us  [shards(): call('grad', functools.partial(grad_body, count, head, scale), (cols // r...]
    pallas_call x4, Pallas kernels: 4.61 us -> 3.52 us  [shards(): call('place', marked_body if final else place_body, (1,), 1, [whole((2 *...]
    ppermute x1, waiting for transfers between devices: 7.14 us -> 8.19 us  [shards(): four = lax.ppermute(four, 'section', chips([(2, 0)]))]
  transfers between devices with their start and end apart: 18 -> 18, of which waited for: 7 -> 11; matrix products, arithmetic and copies ran while one was open for 0% -> 0% of each run, Pallas kernels for 19% -> 16%
where the time goes in v3:
time: 93.8 us; the launch traced here: 93.5 us
  waiting for transfers between devices  49.1 us (52%)
  starting transfers between devices  20.8 us (22%)
  Pallas kernels  18.1 us (19%)
  local copies, waits for them, and re-layouts  4.59 us (5%)
    ppermute x14, waiting for transfers between devices, swap(): return lax.ppermute(x, axis, [(i, i ^ k) for i in range(count)])  40.4 us
    ppermute x14, starting transfers between devices, swap(): return lax.ppermute(x, axis, [(i, i ^ k) for i in range(count)])  16.9 us
    ppermute x1, waiting for transfers between devices, shards(): four = lax.ppermute(four, 'section', chips([(2, 0)]))  8.19 us
    pallas_call x1, Pallas kernels, shards(): call('grad', functools.partial(grad_body, count, head, scale), (cols // r...  7.6 us
    unnamed x28, local copies, waits for them, and re-layouts  4.59 us
    pallas_call x4, Pallas kernels, shards(): call('place', marked_body if final else place_body, (1,), 1, [whole((2 *...  3.52 us
    pallas_call x1, Pallas kernels, shards(): call('spread', functools.partial(spread_body, count, plan.shape[0], scale...  2.1 us
  transfers between devices with their start and end apart: 18, of which 11 were waited for; matrix products, arithmetic and copies ran while one was open for 0% of the time, Pallas kernels for 16%

profile of v3, /device:TPU:0, one launch (start us, length us, event | category | flops | bytes accessed | tf_op | source)
XLA Modules:
  0.0 93.5 jit_solution(13619228825625655331)
XLA Ops:
  0.6 3.0 %collective-permute-start = (bf16[128,1024]{1,0:T(8,128)(2,1)}, bf16[128,1024]{1,0:T(8,128)(2,1)S(1)}, u32[]{:S(2)}, u32[]{:S(2)}) collective-permute-start(bf16[128,1024]{1,0:T(8,128)(2,1)} %bitcast.26), channel_id=1, source_target_pairs={{0,1},{1,0},{2,3},{3,2},{4,5},{5,4},{6,7},{7,6},{8,9},{9,8},{10,11... | collective-permute-start | bytes 786440 | tf_op jit(solution)/shard_map/ppermute | solution.py:25
  3.6 1.5 %collective-permute-start.1 = (bf16[128,1024]{1,0:T(8,128)(2,1)}, bf16[128,1024]{1,0:T(8,128)(2,1)S(1)}, u32[]{:S(2)}, u32[]{:S(2)}) collective-permute-start(bf16[128,1024]{1,0:T(8,128)(2,1)} %bitcast.27), channel_id=1, source_target_pairs={{0,2},{1,3},{2,0},{3,1},{4,6},{5,7},{6,4},{7,5},{8,10},{9,11},{10,... | collective-permute-start | bytes 786440 | tf_op jit(solution)/shard_map/ppermute | solution.py:25
  5.2 0.0 collective-permute-start.2
  5.2 1.3 %copy-done.1 = bf16[1,128,5120]{2,1,0:T(8,128)(2,1)S(1)} copy-done((bf16[1,128,5120]{2,1,0:T(8,128)(2,1)S(1)}, bf16[1,128,5120]{2,1,0:T(8,128)(2,1)}, u32[]{:S(2)}) %copy-start.1) | copy-done | bytes 1310744
  6.5 0.7 copy-done.3
  7.2 0.7 prep.1
  8.0 2.0 %collective-permute-start.6 = (bf16[1280,128]{1,0:T(8,128)(2,1)S(1)}, bf16[1280,128]{1,0:T(8,128)(2,1)S(1)}, u32[]{:S(2)}, u32[]{:S(2)}) collective-permute-start(bf16[1280,128]{1,0:T(8,128)(2,1)S(1)} %get-tuple-element.37), channel_id=1, source_target_pairs={{0,1},{1,0},{2,3},{3,2},{4,5},{5,4},{6,7},{7,6},{8,9},{9,8},{10,11... | collective-permute-start | bytes 983048 | tf_op jit(solution)/shard_map/ppermute | solution.py:25
  10.0 1.5 %collective-permute-start.7 = (bf16[1280,128]{1,0:T(8,128)(2,1)S(1)}, bf16[1280,128]{1,0:T(8,128)(2,1)S(1)}, u32[]{:S(2)}, u32[]{:S(2)}) collective-permute-start(bf16[1280,128]{1,0:T(8,128)(2,1)S(1)} %get-tuple-element.38), channel_id=1, source_target_pairs={{0,2},{1,3},{2,0},{3,1},{4,6},{5,7},{6,4},{7,5},{8,10},{9,11},{10,... | collective-permute-start | bytes 983048 | tf_op jit(solution)/shard_map/ppermute | solution.py:25
  11.5 2.5 %copy-done = f32[1,1280,1024]{2,1,0:T(8,128)S(1)} copy-done((f32[1,1280,1024]{2,1,0:T(8,128)S(1)}, f32[1,1280,1024]{2,1,0:T(8,128)}, u32[]{:S(2)}) %copy-start) | copy-done | bytes 5242904
  14.0 0.3 low.1.refs_4_
  14.3 0.0 collective-permute-done.refs_1_
  14.3 0.0 slice-start
  14.3 0.0 slice-start.2
  14.4 0.0 slice-start.4
  14.4 0.0 slice-start.1
  14.4 0.0 slice-start.3
  14.4 0.0 slice-start.5
  14.4 0.0 copy-start.5
  14.4 0.1 collective-permute-start.8
  14.5 3.3 %collective-permute-done.1.refs_2_ = bf16[128,1024]{1,0:T(8,128)(2,1)S(1)} collective-permute-done((bf16[128,1024]{1,0:T(8,128)(2,1)}, bf16[128,1024]{1,0:T(8,128)(2,1)S(1)}, u32[]{:S(2)}, u32[]{:S(2)}) %collective-permute-start.1) | collective-permute-done | bytes 262176 | tf_op jit(solution)/shard_map/ppermute | solution.py:25
  17.9 0.3 collective-permute-done.2.refs_3_
  18.2 2.1 %spread.1 = (bf16[512,1024]{1,0:T(8,128)(2,1)S(1)}, bf16[128,1280]{1,0:T(8,128)(2,1)S(1)}, bf16[128,1280]{1,0:T(8,128)(2,1)S(1)}, bf16[128,1280]{1,0:T(8,128)(2,1)S(1)}, bf16[128,1280]{1,0:T(8,128)(2,1)S(1)}) custom-call(s32[4]{0:T(128)S(1)} %copy-done.7, bf16[128,1024]{1,0:T(8,128)(2,1)S(1)} %bitcast.29, ...), custom_call_target="tpu_custom_call" | custom-call | flops 10000000000 | bytes 1 | tf_op jit(solution)/shard_map/spread/pallas_call | solution.py:348
  20.3 1.6 %collective-permute-start.3 = (bf16[128,1280]{1,0:T(8,128)(2,1)S(1)}, bf16[128,1280]{1,0:T(8,128)(2,1)S(1)}, u32[]{:S(2)}, u32[]{:S(2)}) collective-permute-start(bf16[128,1280]{1,0:T(8,128)(2,1)S(1)} %get-tuple-element.33), channel_id=1, source_target_pairs={{0,1},{1,0},{2,3},{3,2},{4,5},{5,4},{6,7},{7,6},{8,9},{9,8},{10,11... | collective-permute-start | bytes 983048 | tf_op jit(solution)/shard_map/ppermute | solution.py:25
  21.8 0.5 collective-permute-start.4
  22.4 1.3 %collective-permute-done.6.refs_1_ = bf16[1280,128]{1,0:T(8,128)(2,1)S(1)} collective-permute-done((bf16[1280,128]{1,0:T(8,128)(2,1)S(1)}, bf16[1280,128]{1,0:T(8,128)(2,1)S(1)}, u32[]{:S(2)}, u32[]{:S(2)}) %collective-permute-start.6) | collective-permute-done | bytes 327712 | tf_op jit(solution)/shard_map/ppermute | solution.py:25
  23.7 3.0 %collective-permute-start.5 = (bf16[128,1280]{1,0:T(8,128)(2,1)S(1)}, bf16[128,1280]{1,0:T(8,128)(2,1)S(1)}, u32[]{:S(2)}, u32[]{:S(2)}) collective-permute-start(bf16[128,1280]{1,0:T(8,128)(2,1)S(1)} %get-tuple-element.35), channel_id=1, source_target_pairs={{0,3},{1,2},{2,1},{3,0},{4,7},{5,6},{6,5},{7,4},{8,11},{9,10},{10,... | collective-permute-start | bytes 983048 | tf_op jit(solution)/shard_map/ppermute | solution.py:25
  26.7 5.2 %collective-permute-done.7.refs_2_ = bf16[1280,128]{1,0:T(8,128)(2,1)S(1)} collective-permute-done((bf16[1280,128]{1,0:T(8,128)(2,1)S(1)}, bf16[1280,128]{1,0:T(8,128)(2,1)S(1)}, u32[]{:S(2)}, u32[]{:S(2)}) %collective-permute-start.7) | collective-permute-done | bytes 327712 | tf_op jit(solution)/shard_map/ppermute | solution.py:25
  31.9 0.4 collective-permute-done.8.refs_3_
  32.3 0.0 slice-done.1
  32.3 0.0 slice-done.3
  32.3 0.0 slice-done.5
  32.3 0.0 copy-start.2
  32.3 0.0 copy-start.4
  32.4 7.6 %grad.1 = (f32[1280,1024]{1,0:T(8,128)}, f32[1280,1024]{1,0:T(8,128)}, bf16[256,1280]{1,0:T(8,128)(2,1)S(1)}, bf16[256,1280]{1,0:T(8,128)(2,1)S(1)}, bf16[256,12...) custom-call(s32[1]{0:T(128)} %bitcast.2.place_ref, s32[4]{0:T(128)S(1)} %bitcast.25, ...), custom_call_target="tpu_custom_call" | custom-call | flops 1 | bytes 1 | tf_op jit(solution)/shard_map/grad/pallas_call | solution.py:361
  40.0 0.0 collective-permute-done.3.refs_1_
  40.0 5.4 %collective-permute-done.4.refs_2_ = bf16[128,1280]{1,0:T(8,128)(2,1)S(1)} collective-permute-done((bf16[128,1280]{1,0:T(8,128)(2,1)S(1)}, bf16[128,1280]{1,0:T(8,128)(2,1)S(1)}, u32[]{:S(2)}, u32[]{:S(2)}) %collective-permute-start.4) | collective-permute-done | bytes 327712 | tf_op jit(solution)/shard_map/ppermute | solution.py:25
  45.3 0.0 collective-permute-done.5.refs_3_
  45.3 1.2 %own.1 = (bf16[64,5120]{1,0:T(8,128)(2,1)S(1)}, bf16[64,5120]{1,0:T(8,128)(2,1)S(1)}) custom-call(s32[1]{0:T(128)} %bitcast.2.place_ref, s32[1]{0:T(128)} %bitcast.core_ref.place_ref, bf16[128,5120]{1,0:T(8,128)(2,1)S(1)} %bitcast.18, f32[1,5120]{1,0:T(1,128)S(1)} %copy-done.4, f32[128,1]{1,0:T(8,128)S(1)} %get-tuple-element.31._.inv_ref, ...), custom_call_target="tpu_custom_call" | custom-call | flops 1 | bytes 1 | tf_op jit(solution)/shard_map/own/pallas_call | solution.py:397
  46.5 0.1 collective-permute-start.9
  46.6 1.5 %collective-permute-start.16 = (bf16[256,1280]{1,0:T(8,128)(2,1)S(1)}, bf16[256,1280]{1,0:T(8,128)(2,1)S(1)}, u32[]{:S(2)}, u32[]{:S(2)}) collective-permute-start(bf16[256,1280]{1,0:T(8,128)(2,1)S(1)} %get-tuple-element.50), channel_id=1, source_target_pairs={{0,3},{1,2},{2,1},{3,0},{4,7},{5,6},{6,5},{7,4},{8,11},{9,10},{10,... | collective-permute-start | bytes 1966088 | tf_op jit(solution)/shard_map/ppermute | solution.py:25
  48.1 1.5 %collective-permute-start.15 = (bf16[256,1280]{1,0:T(8,128)(2,1)S(1)}, bf16[256,1280]{1,0:T(8,128)(2,1)S(1)}, u32[]{:S(2)}, u32[]{:S(2)}) collective-permute-start(bf16[256,1280]{1,0:T(8,128)(2,1)S(1)} %get-tuple-element.49), channel_id=1, source_target_pairs={{0,1},{1,0},{2,3},{3,2},{4,5},{5,4},{6,7},{7,6},{8,9},{9,8},{10,11... | collective-permute-start | bytes 1966088 | tf_op jit(solution)/shard_map/ppermute | solution.py:25
  49.6 0.5 collective-permute-start.14
  50.1 0.0 collective-permute-done.9.got_ref
  50.2 0.2 pair.1
  50.3 0.7 collective-permute-start.10
  51.0 0.7 collective-permute-start.11
  51.7 0.0 collective-permute-done.10.one_ref
  51.7 0.0 collective-permute-done.11.two_ref
  51.7 0.3 middle.1
  52.0 1.3 %collective-permute-start.12 = (bf16[32,5120]{1,0:T(8,128)(2,1)S(1)}, bf16[32,5120]{1,0:T(8,128)(2,1)S(1)}, u32[]{:S(2)}, u32[]{:S(2)}) collective-permute-start(bf16[32,5120]{1,0:T(8,128)(2,1)S(1)} %get-tuple-element.46), channel_id=1, source_target_pairs={{8,0},{16,8},{24,16},{12,4},{20,12},{28,20},{9,1},{17,9},{25,17},{... | collective-permute-start | bytes 983048 | tf_op jit(solution)/shard_map/ppermute | solution.py:424
  53.3 1.3 %collective-permute-start.13 = (bf16[32,5120]{1,0:T(8,128)(2,1)S(1)}, bf16[32,5120]{1,0:T(8,128)(2,1)S(1)}, u32[]{:S(2)}, u32[]{:S(2)}) collective-permute-start(bf16[32,5120]{1,0:T(8,128)(2,1)S(1)} %get-tuple-element.47), channel_id=1, source_target_pairs={{16,0},{20,4},{17,1},{21,5},{18,2},{22,6},{19,3},{23,7}} | collective-permute-start | bytes 983048 | tf_op jit(solution)/shard_map/ppermute | solution.py:425
  54.6 0.9 place.4.refs_0_
  55.5 9.7 %collective-permute-done.16.part_ref = bf16[256,1280]{1,0:T(8,128)(2,1)S(1)} collective-permute-done((bf16[256,1280]{1,0:T(8,128)(2,1)S(1)}, bf16[256,1280]{1,0:T(8,128)(2,1)S(1)}, u32[]{:S(2)}, u32[]{:S(2)}) %collective-permute-start.16) | collective-permute-done | bytes 655392 | tf_op jit(solution)/shard_map/ppermute | solution.py:25
  65.1 0.9 place.5.refs_0_
  66.0 12.8 %collective-permute-done.15.part_ref = bf16[256,1280]{1,0:T(8,128)(2,1)S(1)} collective-permute-done((bf16[256,1280]{1,0:T(8,128)(2,1)S(1)}, bf16[256,1280]{1,0:T(8,128)(2,1)S(1)}, u32[]{:S(2)}, u32[]{:S(2)}) %collective-permute-start.15) | collective-permute-done | bytes 655392 | tf_op jit(solution)/shard_map/ppermute | solution.py:25
  78.8 0.9 place.6._
  79.7 0.0 collective-permute-done.14.part_ref
  79.7 0.9 place.7
  80.5 0.4 collective-permute-done.12.three_ref
  81.0 8.2 %collective-permute-done.13.four_ref = bf16[32,5120]{1,0:T(8,128)(2,1)S(1)} collective-permute-done((bf16[32,5120]{1,0:T(8,128)(2,1)S(1)}, bf16[32,5120]{1,0:T(8,128)(2,1)S(1)}, u32[]{:S(2)}, u32[]{:S(2)}) %collective-permute-start.13) | collective-permute-done | bytes 327712 | tf_op jit(solution)/shard_map/ppermute | solution.py:425
  89.2 1.3 %last.1 = (bf16[128,5120]{1,0:T(8,128)(2,1)}, bf16[64,5120]{1,0:T(8,128)(2,1)S(1)}) custom-call(s32[1]{0:T(128)} %bitcast.1.chip_ref, s32[1]{0:T(128)} %bitcast.core_ref.place_ref, bf16[64,5120]{1,0:T(8,128)(2,1)S(1)} %get-tuple-element.42.keep_ref, bf16[64,5120]{1,0:T(8,128)(2,1)S(1)} %collective-permute-done.9.got_ref, ...), custom_call_target="tpu_custom_call" | custom-call | flops 1 | bytes 1 | tf_op jit(solution)/shard_map/last/pallas_call | solution.py:426
  90.5 0.0 collective-permute-start.17
  90.5 2.1 %collective-permute-done.17.part_ref = bf16[64,5120]{1,0:T(8,128)(2,1)S(1)} collective-permute-done((bf16[64,5120]{1,0:T(8,128)(2,1)S(1)}, bf16[64,5120]{1,0:T(8,128)(2,1)S(1)}, u32[]{:S(2)}, u32[]{:S(2)}) %collective-permute-start.17) | collective-permute-done | bytes 655392 | tf_op jit(solution)/shard_map/ppermute | solution.py:25
  92.6 0.9 join.1
  (16 shorter events, 0.0 us)
Async XLA Ops:
  0.6 13.7 %collective-permute-start = (bf16[128,1024]{1,0:T(8,128)(2,1)}, bf16[128,1024]{1,0:T(8,128)(2,1)S(1)}, u32[]{:S(2)}, u32[]{:S(2)}) collective-permute-start(bf16[128,1024]{1,0:T(8,128)(2,1)} %bitcast.26), channel_id=1, source_target_pairs={{0,1},{1,0},{2,3},{3,2},{4,5},{5,4},{6,7},{7,6},{8,9},{9,8},{10,11... | collective-permute-start | bytes 786440 | tf_op jit(solution)/shard_map/ppermute | solution.py:25
  3.6 14.2 %collective-permute-start.1 = (bf16[128,1024]{1,0:T(8,128)(2,1)}, bf16[128,1024]{1,0:T(8,128)(2,1)S(1)}, u32[]{:S(2)}, u32[]{:S(2)}) collective-permute-start(bf16[128,1024]{1,0:T(8,128)(2,1)} %bitcast.27), channel_id=1, source_target_pairs={{0,2},{1,3},{2,0},{3,1},{4,6},{5,7},{6,4},{7,5},{8,10},{9,11},{10,... | collective-permute-start | bytes 786440 | tf_op jit(solution)/shard_map/ppermute | solution.py:25
  5.2 13.0 %collective-permute-start.2 = (bf16[128,1024]{1,0:T(8,128)(2,1)}, bf16[128,1024]{1,0:T(8,128)(2,1)S(1)}, u32[]{:S(2)}, u32[]{:S(2)}) collective-permute-start(bf16[128,1024]{1,0:T(8,128)(2,1)} %bitcast.28), channel_id=1, source_target_pairs={{0,3},{1,2},{2,1},{3,0},{4,7},{5,6},{6,5},{7,4},{8,11},{9,10},{10,... | collective-permute-start | bytes 786440 | tf_op jit(solution)/shard_map/ppermute | solution.py:25
  5.2 1.3 %copy-start.1 = (bf16[1,128,5120]{2,1,0:T(8,128)(2,1)S(1)}, bf16[1,128,5120]{2,1,0:T(8,128)(2,1)}, u32[]{:S(2)}) copy-start(bf16[1,128,5120]{2,1,0:T(8,128)(2,1)} %param.8) | copy-start | bytes 3932164
  6.5 0.7 copy-start.3
  8.0 15.7 %collective-permute-start.6 = (bf16[1280,128]{1,0:T(8,128)(2,1)S(1)}, bf16[1280,128]{1,0:T(8,128)(2,1)S(1)}, u32[]{:S(2)}, u32[]{:S(2)}) collective-permute-start(bf16[1280,128]{1,0:T(8,128)(2,1)S(1)} %get-tuple-element.37), channel_id=1, source_target_pairs={{0,1},{1,0},{2,3},{3,2},{4,5},{5,4},{6,7},{7,6},{8,9},{9,8},{10,11... | collective-permute-start | bytes 983048 | tf_op jit(solution)/shard_map/ppermute | solution.py:25
  10.0 21.9 %collective-permute-start.7 = (bf16[1280,128]{1,0:T(8,128)(2,1)S(1)}, bf16[1280,128]{1,0:T(8,128)(2,1)S(1)}, u32[]{:S(2)}, u32[]{:S(2)}) collective-permute-start(bf16[1280,128]{1,0:T(8,128)(2,1)S(1)} %get-tuple-element.38), channel_id=1, source_target_pairs={{0,2},{1,3},{2,0},{3,1},{4,6},{5,7},{6,4},{7,5},{8,10},{9,11},{10,... | collective-permute-start | bytes 983048 | tf_op jit(solution)/shard_map/ppermute | solution.py:25
  11.5 2.5 %copy-start = (f32[1,1280,1024]{2,1,0:T(8,128)S(1)}, f32[1,1280,1024]{2,1,0:T(8,128)}, u32[]{:S(2)}) copy-start(f32[1,1280,1024]{2,1,0:T(8,128)} %param.11) | copy-start | bytes 15728644
  14.0 4.2 %copy-start.6 = (bf16[1,128,1024]{2,1,0:T(8,128)(2,1)S(1)}, bf16[1,128,1024]{2,1,0:T(8,128)(2,1)}, u32[]{:S(2)}) copy-start(bf16[1,128,1024]{2,1,0:T(8,128)(2,1)} %param.9) | copy-start | bytes 786436
  14.0 4.2 %copy-start.7 = (s32[4]{0:T(128)S(1)}, s32[4]{0:T(128)}, u32[]{:S(2)}) copy-start(s32[4]{0:T(128)} %plan_ref.1) | copy-start | bytes 52
  14.3 17.9 %slice-start = ((s8[5242880]{0:T(1024)(128)(4,1)}), s8[4194304]{0:T(1024)(128)(4,1)S(1)}, s32[]{:S(2)}) async-start(s8[5242880]{0:T(1024)(128)(4,1)} %bitcast.14), calls=%async_computation | async-start | bytes 8388608
  14.3 17.9 %slice-start.2 = ((s8[5242880]{0:T(1024)(128)(4,1)}), s8[4194304]{0:T(1024)(128)(4,1)S(1)}, s32[]{:S(2)}) async-start(s8[5242880]{0:T(1024)(128)(4,1)} %bitcast.19), calls=%async_computation.2 | async-start | bytes 8388608
  14.4 17.9 %slice-start.4 = ((s8[5242880]{0:T(1024)(128)(4,1)}), s8[4194304]{0:T(1024)(128)(4,1)S(1)}, s32[]{:S(2)}) async-start(s8[5242880]{0:T(1024)(128)(4,1)} %bitcast.22), calls=%async_computation.4 | async-start | bytes 8388608
  14.4 17.9 %slice-start.1 = ((s8[5242880]{0:T(1024)(128)(4,1)}), s8[1048576]{0:T(1024)(128)(4,1)S(1)}, s32[]{:S(2)}) async-start(s8[5242880]{0:T(1024)(128)(4,1)} %bitcast.14), calls=%async_computation.1 | async-start | bytes 2097152
  14.4 17.9 %slice-start.3 = ((s8[5242880]{0:T(1024)(128)(4,1)}), s8[1048576]{0:T(1024)(128)(4,1)S(1)}, s32[]{:S(2)}) async-start(s8[5242880]{0:T(1024)(128)(4,1)} %bitcast.19), calls=%async_computation.3 | async-start | bytes 2097152
  14.4 17.9 %slice-start.5 = ((s8[5242880]{0:T(1024)(128)(4,1)}), s8[1048576]{0:T(1024)(128)(4,1)S(1)}, s32[]{:S(2)}) async-start(s8[5242880]{0:T(1024)(128)(4,1)} %bitcast.22), calls=%async_computation.5 | async-start | bytes 2097152
  14.4 17.9 %copy-start.5 = (s32[1,4]{1,0:T(1,128)S(1)}, s32[1,4]{1,0:T(1,128)}, u32[]{:S(2)}) copy-start(s32[1,4]{1,0:T(1,128)} %param.14) | copy-start | bytes 52
  14.4 17.8 %collective-permute-start.8 = (bf16[1280,128]{1,0:T(8,128)(2,1)S(1)}, bf16[1280,128]{1,0:T(8,128)(2,1)S(1)}, u32[]{:S(2)}, u32[]{:S(2)}) collective-permute-start(bf16[1280,128]{1,0:T(8,128)(2,1)S(1)} %get-tuple-element.39), channel_id=1, source_target_pairs={{0,3},{1,2},{2,1},{3,0},{4,7},{5,6},{6,5},{7,4},{8,11},{9,10},{10,... | collective-permute-start | bytes 983048 | tf_op jit(solution)/shard_map/ppermute | solution.py:25
  20.3 19.7 %collective-permute-start.3 = (bf16[128,1280]{1,0:T(8,128)(2,1)S(1)}, bf16[128,1280]{1,0:T(8,128)(2,1)S(1)}, u32[]{:S(2)}, u32[]{:S(2)}) collective-permute-start(bf16[128,1280]{1,0:T(8,128)(2,1)S(1)} %get-tuple-element.33), channel_id=1, source_target_pairs={{0,1},{1,0},{2,3},{3,2},{4,5},{5,4},{6,7},{7,6},{8,9},{9,8},{10,11... | collective-permute-start | bytes 983048 | tf_op jit(solution)/shard_map/ppermute | solution.py:25
  21.8 23.5 %collective-permute-start.4 = (bf16[128,1280]{1,0:T(8,128)(2,1)S(1)}, bf16[128,1280]{1,0:T(8,128)(2,1)S(1)}, u32[]{:S(2)}, u32[]{:S(2)}) collective-permute-start(bf16[128,1280]{1,0:T(8,128)(2,1)S(1)} %get-tuple-element.34), channel_id=1, source_target_pairs={{0,2},{1,3},{2,0},{3,1},{4,6},{5,7},{6,4},{7,5},{8,10},{9,11},{10,... | collective-permute-start | bytes 983048 | tf_op jit(solution)/shard_map/ppermute | solution.py:25
  23.7 21.7 %collective-permute-start.5 = (bf16[128,1280]{1,0:T(8,128)(2,1)S(1)}, bf16[128,1280]{1,0:T(8,128)(2,1)S(1)}, u32[]{:S(2)}, u32[]{:S(2)}) collective-permute-start(bf16[128,1280]{1,0:T(8,128)(2,1)S(1)} %get-tuple-element.35), channel_id=1, source_target_pairs={{0,3},{1,2},{2,1},{3,0},{4,7},{5,6},{6,5},{7,4},{8,11},{9,10},{10,... | collective-permute-start | bytes 983048 | tf_op jit(solution)/shard_map/ppermute | solution.py:25
  32.3 13.0 %copy-start.2 = (bf16[1,128,5120]{2,1,0:T(8,128)(2,1)S(1)}, bf16[1,128,5120]{2,1,0:T(8,128)(2,1)}, u32[]{:S(2)}) copy-start(bf16[1,128,5120]{2,1,0:T(8,128)(2,1)} %param.8) | copy-start | bytes 3932164
  32.3 13.0 %copy-start.4 = (f32[1,5120]{1,0:T(1,128)S(1)}, f32[1,5120]{1,0:T(1,128)}, u32[]{:S(2)}) copy-start(f32[1,5120]{1,0:T(1,128)} %gain_ref.3) | copy-start | bytes 61444
  46.5 3.6 %collective-permute-start.9 = (bf16[64,5120]{1,0:T(8,128)(2,1)S(1)}, bf16[64,5120]{1,0:T(8,128)(2,1)S(1)}, u32[]{:S(2)}, u32[]{:S(2)}) collective-permute-start(bf16[64,5120]{1,0:T(8,128)(2,1)S(1)} %get-tuple-element.43), channel_id=1, source_target_pairs={{0,4},{4,0},{8,12},{12,8},{16,20},{20,16},{24,28},{28,24},{1,5},{5... | collective-permute-start | bytes 1966088 | tf_op jit(solution)/shard_map/ppermute | solution.py:25
  46.6 18.5 %collective-permute-start.16 = (bf16[256,1280]{1,0:T(8,128)(2,1)S(1)}, bf16[256,1280]{1,0:T(8,128)(2,1)S(1)}, u32[]{:S(2)}, u32[]{:S(2)}) collective-permute-start(bf16[256,1280]{1,0:T(8,128)(2,1)S(1)} %get-tuple-element.50), channel_id=1, source_target_pairs={{0,3},{1,2},{2,1},{3,0},{4,7},{5,6},{6,5},{7,4},{8,11},{9,10},{10,... | collective-permute-start | bytes 1966088 | tf_op jit(solution)/shard_map/ppermute | solution.py:25
  48.1 30.6 %collective-permute-start.15 = (bf16[256,1280]{1,0:T(8,128)(2,1)S(1)}, bf16[256,1280]{1,0:T(8,128)(2,1)S(1)}, u32[]{:S(2)}, u32[]{:S(2)}) collective-permute-start(bf16[256,1280]{1,0:T(8,128)(2,1)S(1)} %get-tuple-element.49), channel_id=1, source_target_pairs={{0,1},{1,0},{2,3},{3,2},{4,5},{5,4},{6,7},{7,6},{8,9},{9,8},{10,11... | collective-permute-start | bytes 1966088 | tf_op jit(solution)/shard_map/ppermute | solution.py:25
  49.6 30.0 %collective-permute-start.14 = (bf16[256,1280]{1,0:T(8,128)(2,1)S(1)}, bf16[256,1280]{1,0:T(8,128)(2,1)S(1)}, u32[]{:S(2)}, u32[]{:S(2)}) collective-permute-start(bf16[256,1280]{1,0:T(8,128)(2,1)S(1)} %get-tuple-element.48), channel_id=1, source_target_pairs={{0,2},{1,3},{2,0},{3,1},{4,6},{5,7},{6,4},{7,5},{8,10},{9,11},{10,... | collective-permute-start | bytes 1966088 | tf_op jit(solution)/shard_map/ppermute | solution.py:25
  50.3 1.4 %collective-permute-start.10 = (bf16[32,5120]{1,0:T(8,128)(2,1)S(1)}, bf16[32,5120]{1,0:T(8,128)(2,1)S(1)}, u32[]{:S(2)}, u32[]{:S(2)}) collective-permute-start(bf16[32,5120]{1,0:T(8,128)(2,1)S(1)} %get-tuple-element.44), channel_id=1, source_target_pairs={{24,8},{8,16},{28,12},{12,20},{25,9},{9,17},{29,13},{13,21},{26,10... | collective-permute-start | bytes 983048 | tf_op jit(solution)/shard_map/ppermute | solution.py:419
  51.0 0.7 collective-permute-start.11
  52.0 29.0 %collective-permute-start.12 = (bf16[32,5120]{1,0:T(8,128)(2,1)S(1)}, bf16[32,5120]{1,0:T(8,128)(2,1)S(1)}, u32[]{:S(2)}, u32[]{:S(2)}) collective-permute-start(bf16[32,5120]{1,0:T(8,128)(2,1)S(1)} %get-tuple-element.46), channel_id=1, source_target_pairs={{8,0},{16,8},{24,16},{12,4},{20,12},{28,20},{9,1},{17,9},{25,17},{... | collective-permute-start | bytes 983048 | tf_op jit(solution)/shard_map/ppermute | solution.py:424
  53.3 35.9 %collective-permute-start.13 = (bf16[32,5120]{1,0:T(8,128)(2,1)S(1)}, bf16[32,5120]{1,0:T(8,128)(2,1)S(1)}, u32[]{:S(2)}, u32[]{:S(2)}) collective-permute-start(bf16[32,5120]{1,0:T(8,128)(2,1)S(1)} %get-tuple-element.47), channel_id=1, source_target_pairs={{16,0},{20,4},{17,1},{21,5},{18,2},{22,6},{19,3},{23,7}} | collective-permute-start | bytes 983048 | tf_op jit(solution)/shard_map/ppermute | solution.py:425
  90.5 2.1 %collective-permute-start.17 = (bf16[64,5120]{1,0:T(8,128)(2,1)S(1)}, bf16[64,5120]{1,0:T(8,128)(2,1)S(1)}, u32[]{:S(2)}, u32[]{:S(2)}) collective-permute-start(bf16[64,5120]{1,0:T(8,128)(2,1)S(1)} %get-tuple-element.53), channel_id=1, source_target_pairs={{0,4},{4,0},{8,12},{12,8},{16,20},{20,16},{24,28},{28,24},{1,5},{5... | collective-permute-start | bytes 1966088 | tf_op jit(solution)/shard_map/ppermute | solution.py:25

commit v4 on v3

--- a/solution.py
+++ b/solution.py
@@ -151,8 +151,7 @@
     return pl.ds(pl.multiple_of((place ^ k) * cols, 128), cols)
 
 
-def prep_body(count, place_ref, core_ref, chip_ref, tok_ref, gain_ref, inv_ref, *out_refs):
-    place = place_ref[0]
+def prep_body(count, place_ref, core_ref, chip_ref, tok_ref, gain_ref, inv_ref, out_ref):
     width = tok_ref.shape[1]
     cols = width // count
     total = jnp.zeros((tok_ref.shape[0], 1), f32)
@@ -162,25 +161,24 @@
     inverse = lax.rsqrt(total / width + norm_eps)
     inv_ref[...] = inverse
     for k in range(count):
-        part = part_of(place, k, cols)
+        part = slice(k * cols, (k + 1) * cols)
         x = tok_ref[:, part].astype(f32)
-        out_refs[k][...] = (x * inverse * gain_ref[:, part]).astype(bf16).T
+        out_ref[k] = (x * inverse * gain_ref[:, part]).astype(bf16).T
 
 
 def low_body(master_ref, _, low_ref):
     low_ref[...] = master_ref[...].astype(bf16)
 
 
-def spread_body(count, micro, scale, plan_ref, *refs):
+def spread_body(count, micro, scale, place_ref, plan_ref, *refs):
     cots, (low_ref, ordered_ref), outs = refs[:count], refs[count : count + 2], refs[count + 2 :]
     rows = cots[0].shape[0]
     size = rows // micro
     for k in range(count):
         for i in range(micro):
             at = pl.multiple_of(plan_ref[i] * size, size)
-            ordered_ref[k * rows + i * size : k * rows + (i + 1) * size, :] = cots[k][
-                pl.ds(at, size), :
-            ]
+            to = pl.multiple_of((place_ref[0] ^ k) * rows + i * size, size)
+            ordered_ref[pl.ds(to, size), :] = cots[k][pl.ds(at, size), :]
     step = 256
     for at in range(0, low_ref.shape[0], step):
         product = lax.dot_general(
@@ -190,18 +188,17 @@
             preferred_element_type=f32,
         )
         for k in range(count):
-            outs[k][:, at : at + step] = (product[k * rows : (k + 1) * rows, :] * scale).astype(bf16)
-
-
-def grad_body(count, head, scale, place_ref, owner_ref, *refs):
-    normed, refs = refs[:count], refs[count:]
+            outs[0][k, :, at : at + step] = (product[k * rows : (k + 1) * rows, :] * scale).astype(bf16)
+
+
+def grad_body(count, head, scale, owner_ref, normed_ref, *refs):
     ordered_ref, master_ref, moment_ref, second_ref, moment_out, second_out = refs[:6]
-    outs, mark_ref, joined, fresh = refs[6 : 6 + count], *refs[6 + count :]
-    tok_count = normed[0].shape[1]
+    out_ref, mark_ref, joined, fresh = refs[6:]
+    tok_count = normed_ref.shape[2]
     kv_cols = master_ref.shape[1]
     mark_ref[...] = jnp.zeros_like(mark_ref)
     for k in range(count):
-        joined[:, k * tok_count : (k + 1) * tok_count] = normed[k][...]
+        joined[:, k * tok_count : (k + 1) * tok_count] = normed_ref[k]
     step = 256
     size = joined.shape[0]
     rows = pl.ds(pl.multiple_of(pl.program_id(0) * size, size), size)
@@ -221,33 +218,30 @@
         ) * pl.reciprocal(root, approx=True)
         fresh[:, here] = weights.astype(bf16)
     for k in range(count):
-        owner = owner_ref[place_ref[0] ^ k] * head
+        owner = owner_ref[k] * head
         for p in range(2):
             lanes = pl.ds(pl.multiple_of(p * (kv_cols // 2) + owner, head), head)
-            outs[k][p * head : (p + 1) * head, :] = fresh[:, lanes].T
-
-
-def own_body(count, place_ref, core_ref, tok_ref, gain_ref, inv_ref, *refs):
-    spread, (_, keep_ref, give_ref) = refs[:count], refs[count:]
-    place = place_ref[0]
+            out_ref[k, p * head : (p + 1) * head, :] = fresh[:, lanes].T
+
+
+def own_body(core_ref, tok_ref, gain_ref, inv_ref, spread_ref, _, keep_ref, give_ref):
     core = core_ref[0]
-    width = tok_ref.shape[1]
-    cols = width // count
+    count, _, cols = spread_ref.shape
     half = tok_ref.shape[0] // 2
     for out_ref, pick in ((give_ref, 1 - core), (keep_ref, core)):
         rows = pl.ds(pl.multiple_of(pick * half, half), half)
         inverse = inv_ref[rows, :]
         total = jnp.zeros((half, 1), f32)
         for k in range(count):
-            part = part_of(place, k, cols)
-            scaled = spread[k][rows, :].astype(f32) * gain_ref[:, part]
+            part = slice(k * cols, (k + 1) * cols)
+            scaled = spread_ref[k, rows, :].astype(f32) * gain_ref[:, part]
             total = total + jnp.sum(
                 scaled * tok_ref[rows, part].astype(f32), axis=-1, keepdims=True
             )
-        factor = inverse * inverse * inverse * (total / width)
+        factor = inverse * inverse * inverse * (total / (count * cols))
         for k in range(count):
-            part = part_of(place, k, cols)
-            scaled = spread[k][rows, :].astype(f32) * gain_ref[:, part]
+            part = slice(k * cols, (k + 1) * cols)
+            scaled = spread_ref[k, rows, :].astype(f32) * gain_ref[:, part]
             out_ref[:, part] = (
                 inverse * scaled - tok_ref[rows, part].astype(f32) * factor
             ).astype(bf16)
@@ -293,12 +287,12 @@
         send_ref[rows, :] = jnp.where(core == 0, got + above, both).astype(bf16)
 
 
-def place_body(place_ref, part_ref, *refs):
+def place_body(core_ref, part_ref, *refs):
     refs[-1][...] = part_ref[...]
 
 
-def marked_body(place_ref, part_ref, _, out_ref, mark_ref):
-    out_ref[...] = part_ref[...]
+def rollout_body(parts_ref, out_ref, mark_ref):
+    out_ref[...] = parts_ref[0]
     mark_ref[...] = jnp.zeros_like(mark_ref)
 
 
@@ -324,16 +318,16 @@
 
     cots = [cot_rows] + [swap(cot_rows, "fsdp", k) for k in dests]
 
-    inverse, *normed = call(
+    inverse, normed = call(
         "prep",
         functools.partial(prep_body, count),
         (1,),
         3,
         [whole((tok_count, width)), whole((1, width))],
-        [whole((tok_count, 1))] + [whole((cols, tok_count))] * count,
-        [sds((tok_count, 1), f32)] + [sds((cols, tok_count), bf16)] * count,
+        [whole((tok_count, 1)), whole((count, cols, tok_count))],
+        [sds((tok_count, 1), f32), sds((count, cols, tok_count), bf16)],
     )(place, core, chip, tok_rows, norm_gain)
-    normed = [normed[0]] + [swap(normed[k], "fsdp", k) for k in dests]
+    normed = lax.all_to_all(normed, "fsdp", 0, 0, tiled=True)
 
     rows_step = 256
     low = call(
@@ -345,66 +339,58 @@
         pl.BlockSpec((rows_step, kv_cols), lambda i: (i, 0)),
         sds((cols, kv_cols), bf16),
     )(master_rows, inverse)
-    ordered, *spread = call(
+    ordered, spread = call(
         "spread",
         functools.partial(spread_body, count, plan.shape[0], scale),
         (),
-        1,
+        2,
         [resident] * (count + 1),
-        [resident] * (count + 1),
-        [sds((count * tok_count, kv_cols), bf16)] + [sds((tok_count, cols), bf16)] * count,
+        [resident] * 2,
+        [sds((count * tok_count, kv_cols), bf16), sds((count, tok_count, cols), bf16)],
         work=10**10,
-    )(plan, *cots, low)
-    spread = [spread[0]] + [swap(spread[k], "fsdp", k) for k in dests]
+    )(place, plan, *cots, low)
+    spread = lax.all_to_all(spread, "fsdp", 0, 0, tiled=True)
 
     state = pl.BlockSpec((rows_step, kv_cols), lambda i, *_: (i, 0))
-    moment_new, second_new, *rollout_parts, grad_mark = call(
+    moment_new, second_new, rollout_parts, grad_mark = call(
         "grad",
         functools.partial(grad_body, count, head, scale),
         (cols // rows_step,),
-        2,
-        [pl.BlockSpec((rows_step, tok_count), lambda i, *_: (i, 0))] * count
+        1,
+        [pl.BlockSpec((count, rows_step, tok_count), lambda i, *_: (0, i, 0))]
         + [resident, resident, resident, resident],
         [state, state]
-        + [pl.BlockSpec((2 * head, rows_step), lambda i, *_: (0, i))] * count
+        + [pl.BlockSpec((count, 2 * head, rows_step), lambda i, *_: (0, 0, i))]
         + [whole((8, 128))],
-        [sds((cols, kv_cols), f32)] * 2 + [sds((2 * head, cols), bf16)] * count + [mark],
+        [sds((cols, kv_cols), f32)] * 2 + [sds((count, 2 * head, cols), bf16), mark],
         scratch=[
             pltpu.VMEM((rows_step, count * tok_count), bf16),
             pltpu.VMEM((rows_step, kv_cols), bf16),
         ],
         vmem=20,
-    )(place, head_owner[0], *normed, ordered, master_rows, moment_rows, second_rows)
-
-    rollout = ()
-    rollout_mark = ()
-    for k in (0, 3, 1, 2):
-        part = swap(rollout_parts[k], "fsdp", k) if k else rollout_parts[k]
-        final = k == 2
-        rollout, *rollout_mark = call(
-            "place",
-            marked_body if final else place_body,
-            (1,),
-            1,
-            [whole((2 * head, cols))] + ([anywhere] if k else []),
-            [pl.BlockSpec((2 * head, cols), lambda i, place_ref, k=k: (0, place_ref[0] ^ k))]
-            + ([whole((8, 128))] if final else []),
-            [sds((2 * head, width), bf16)] + ([mark] if final else []),
-            aliases={2: 0} if k else None,
-            work=10**9,
-        )(place, part, *([rollout] if k else []))
+    )(head_owner[0], normed, ordered, master_rows, moment_rows, second_rows)
+
+    rollout, rollout_mark = call(
+        "rollout",
+        rollout_body,
+        (count,),
+        0,
+        [pl.BlockSpec((1, 2 * head, cols), lambda k: (k, 0, 0))],
+        [pl.BlockSpec((2 * head, cols), lambda k: (0, k)), whole((8, 128))],
+        [sds((2 * head, width), bf16), mark],
+        work=10**9,
+    )(lax.all_to_all(rollout_parts, "fsdp", 0, 0, tiled=True))
 
     keep, give = call(
         "own",
-        functools.partial(own_body, count),
+        own_body,
         (1,),
-        2,
+        1,
         [whole((tok_count, width)), whole((1, width)), whole((tok_count, 1))]
-        + [whole((tok_count, cols))] * count
-        + [anywhere],
+        + [whole((count, tok_count, cols)), anywhere],
         [whole((half, width))] * 2,
         [sds((half, width), bf16)] * 2,
-    )(place, core, tok_rows, norm_gain, inverse, *spread, grad_mark)
+    )(core, tok_rows, norm_gain, inverse, spread, grad_mark)
     got = swap(give, "section", 1)
 
     def chips(pairs):
@@ -431,7 +417,7 @@
         [full, full, part, part, part, part, anywhere],
         [pl.BlockSpec((half, width), lambda i, chip_ref, core_ref: (core_ref[0], 0)), full],
         [sds((tok_count, width), bf16), sds((half, width), bf16)],
-    )(chip, core, keep, got, one, two, three, four, *rollout_mark)
+    )(chip, core, keep, got, one, two, three, four, rollout_mark)
     other = swap(send, "section", 1)
     grads = call(
         "join",

time: 93.8 us -> 105 us (1.12)
  local copies, waits for them, and re-layouts: 4.59 us -> 16.8 us
  waiting for transfers between devices: 49.1 us -> 46.3 us
  Pallas kernels: 18.1 us -> 19.5 us
    ppermute x14 -> x5, waiting for transfers between devices: 40.4 us -> 6.31 us  [swap(): return lax.ppermute(x, axis, [(i, i ^ k) for i in range(count)])]
    all_to_all x0 -> x3, waiting for transfers between devices: none -> 31.7 us  [the longest x1 23 us: shards(): lax.all_to_all(rollout_parts, 'fsdp', 0, 0, tiled=True)]
    all_to_all x0 -> x3, starting transfers between devices: none -> 12.4 us  [the longest x1 4.69 us: shards(): lax.all_to_all(rollout_parts, 'fsdp', 0, 0, tiled=True)]
    ppermute x14 -> x5, starting transfers between devices: 16.9 us -> 4.68 us  [swap(): return lax.ppermute(x, axis, [(i, i ^ k) for i in range(count)])]
    unnamed x28 -> x30, local copies, waits for them, and re-layouts: 4.59 us -> 16.8 us
    pallas_call x1, Pallas kernels: 0.75 us -> 1.81 us  [shards(): call('prep', functools.partial(prep_body, count), (1,), 3, [whole((tok_co...]
    pallas_call x5 -> x2, Pallas kernels: 4.7 us -> 5.02 us  [the longest x1 3.98 us: shards(): call('rollout', rollout_body, (count,), 0, [pl.BlockSpec((1, 2 * head, co...]
  transfers between devices with their start and end apart: 18 -> 12, of which waited for: 11 -> 8; matrix products, arithmetic and copies ran while one was open for 0% -> 0% of each run, Pallas kernels for 16% -> 17%
where the time goes in v4:
time: 105 us; the launch traced here: 104 us
  waiting for transfers between devices  46.3 us (44%)
  starting transfers between devices  21 us (20%)
  Pallas kernels  19.5 us (19%)
  local copies, waits for them, and re-layouts  16.8 us (16%)
    all_to_all x1, waiting for transfers between devices, shards(): lax.all_to_all(rollout_parts, 'fsdp', 0, 0, tiled=True)  23 us
    unnamed x30, local copies, waits for them, and re-layouts  16.8 us
    all_to_all x1, waiting for transfers between devices, shards(): normed = lax.all_to_all(normed, 'fsdp', 0, 0, tiled=True)  8.76 us
    ppermute x1, waiting for transfers between devices, shards(): four = lax.ppermute(four, 'section', chips([(2, 0)]))  8.19 us
    pallas_call x1, Pallas kernels, shards(): call('grad', functools.partial(grad_body, count, head, scale), (cols // r...  7.62 us
    ppermute x5, waiting for transfers between devices, swap(): return lax.ppermute(x, axis, [(i, i ^ k) for i in range(count)])  6.31 us
    all_to_all x1, starting transfers between devices, shards(): lax.all_to_all(rollout_parts, 'fsdp', 0, 0, tiled=True)  4.69 us
    ppermute x5, starting transfers between devices, swap(): return lax.ppermute(x, axis, [(i, i ^ k) for i in range(count)])  4.68 us
  transfers between devices with their start and end apart: 12, of which 8 were waited for; matrix products, arithmetic and copies ran while one was open for 0% of the time, Pallas kernels for 17%

profile of v4, /device:TPU:0, one launch (start us, length us, event | category | flops | bytes accessed | tf_op | source)
XLA Modules:
  0.0 104.4 jit_solution(16628619649970483213)
XLA Ops:
  0.6 4.0 %collective-permute-start.2 = (bf16[128,1024]{1,0:T(8,128)(2,1)}, bf16[128,1024]{1,0:T(8,128)(2,1)S(1)}, u32[]{:S(2)}, u32[]{:S(2)}) collective-permute-start(bf16[128,1024]{1,0:T(8,128)(2,1)} %bitcast.20), channel_id=1, source_target_pairs={{0,3},{1,2},{2,1},{3,0},{4,7},{5,6},{6,5},{7,4},{8,11},{9,10},{10,... | collective-permute-start | bytes 786440 | tf_op jit(solution)/shard_map/ppermute | solution.py:25
  4.6 0.5 collective-permute-start.1
  5.1 0.1 collective-permute-start
  5.2 0.0 copy-start.2
  5.2 1.3 %copy-done.2 = bf16[1,128,5120]{2,1,0:T(8,128)(2,1)S(1)} copy-done((bf16[1,128,5120]{2,1,0:T(8,128)(2,1)S(1)}, bf16[1,128,5120]{2,1,0:T(8,128)(2,1)}, u32[]{:S(2)}) %copy-start.2) | copy-done | bytes 1310744
  6.6 0.0 copy-start.10
  6.6 0.7 copy-done.10
  7.3 1.8 %prep.1 = (f32[128,1]{1,0:T(8,128)S(1)}, bf16[4,1280,128]{2,1,0:T(8,128)(2,1)}) custom-call(s32[1]{0:T(128)} %bitcast.3.place_ref, s32[1]{0:T(128)} %bitcast.core_ref, s32[1]{0:T(128)} %bitcast.1.chip_ref, bf16[128,5120]{1,0:T(8,128)(2,1)S(1)} %bitcast.15, f32[1,5120]{1,0:T(1,128)S(1)} %copy-done.10), custom_call_target="tpu_custom_call" | custom-call | flops 1 | bytes 1 | tf_op jit(solution)/shard_map/prep/pallas_call | solution.py:321
  9.1 4.1 %all-to-all-start.1 = ((bf16[4,1280,128]{2,1,0:T(8,128)(2,1)}), bf16[4,1280,128]{2,1,0:T(8,128)(2,1)S(1)}, u32[]{:S(2)}, u32[]{:S(2)}) async-start(bf16[4,1280,128]{2,1,0:T(8,128)(2,1)} %get-tuple-element.24), calls=%async_computation.1 | async-start | bytes 2621440 | tf_op jit(solution)/shard_map/all_to_all | solution.py:330
  13.2 0.0 copy-start
  13.2 2.5 %copy-done = f32[1,1280,1024]{2,1,0:T(8,128)S(1)} copy-done((f32[1,1280,1024]{2,1,0:T(8,128)S(1)}, f32[1,1280,1024]{2,1,0:T(8,128)}, u32[]{:S(2)}) %copy-start) | copy-done | bytes 5242904
  15.7 0.0 copy-start.13
  15.7 0.0 copy-start.14
  15.7 0.3 low.1.refs_4_
  16.0 0.0 collective-permute-done.2.refs_3_
  16.0 1.6 %collective-permute-done.1.refs_2_ = bf16[128,1024]{1,0:T(8,128)(2,1)S(1)} collective-permute-done((bf16[128,1024]{1,0:T(8,128)(2,1)}, bf16[128,1024]{1,0:T(8,128)(2,1)S(1)}, u32[]{:S(2)}, u32[]{:S(2)}) %collective-permute-start.1) | collective-permute-done | bytes 262176 | tf_op jit(solution)/shard_map/ppermute | solution.py:25
  17.7 0.5 collective-permute-done.refs_1_
  18.2 0.0 copy-done.13
  18.2 0.0 copy-done.14
  18.2 2.1 %spread.1 = (bf16[512,1024]{1,0:T(8,128)(2,1)S(1)}, bf16[4,128,1280]{2,1,0:T(8,128)(2,1)S(1)}) custom-call(s32[1]{0:T(128)} %bitcast.3.place_ref, s32[4]{0:T(128)S(1)} %copy-done.14, bf16[128,1024]{1,0:T(8,128)(2,1)S(1)} %bitcast.23, bf16[128,1024]{1,0:T(8,128)(2,1)S(1)} %collective-permute-done.refs_1_, ...), custom_call_target="tpu_custom_call" | custom-call | flops 10000000000 | bytes 1 | tf_op jit(solution)/shard_map/spread/pallas_call | solution.py:342
  20.3 0.0 copy-start.7
  20.3 1.1 %copy-done.7 = bf16[4,128,1280]{2,1,0:T(8,128)(2,1)} copy-done((bf16[4,128,1280]{2,1,0:T(8,128)(2,1)}, bf16[4,128,1280]{2,1,0:T(8,128)(2,1)S(1)}, u32[]{:S(2)}) %copy-start.7) | copy-done | bytes 1310744
  21.4 0.0 copy-start.8
  21.4 1.0 copy-done.8
  22.3 0.0 copy-start.12
  22.3 8.8 %all-to-all-done.1.normed_ref = bf16[4,1280,128]{2,1,0:T(8,128)(2,1)S(1)} async-done(((bf16[4,1280,128]{2,1,0:T(8,128)(2,1)}), bf16[4,1280,128]{2,1,0:T(8,128)(2,1)S(1)}, u32[]{:S(2)}, u32[]{:S(2)}) %all-to-all-start.1) | async-done | bytes 1310752 | tf_op jit(solution)/shard_map/all_to_all | solution.py:330
  31.1 3.6 %all-to-all-start = ((bf16[4,128,1280]{2,1,0:T(8,128)(2,1)}), bf16[4,128,1280]{2,1,0:T(8,128)(2,1)S(1)}, u32[]{:S(2)}, u32[]{:S(2)}) async-start(bf16[4,128,1280]{2,1,0:T(8,128)(2,1)} %copy-done.7), calls=%async_computation | async-start | bytes 2621440 | tf_op jit(solution)/shard_map/all_to_all | solution.py:352
  34.7 0.0 copy-done.12
  34.7 0.0 copy-start.1
  34.7 2.5 %copy-done.1 = f32[1,1280,1024]{2,1,0:T(8,128)S(1)} copy-done((f32[1,1280,1024]{2,1,0:T(8,128)S(1)}, f32[1,1280,1024]{2,1,0:T(8,128)}, u32[]{:S(2)}) %copy-start.1) | copy-done | bytes 5242904
  37.2 0.0 copy-start.4
  37.2 2.5 %copy-done.4 = f32[1,1280,1024]{2,1,0:T(8,128)S(1)} copy-done((f32[1,1280,1024]{2,1,0:T(8,128)S(1)}, f32[1,1280,1024]{2,1,0:T(8,128)}, u32[]{:S(2)}) %copy-start.4) | copy-done | bytes 5242904
  39.7 0.0 copy-start.5
  39.7 2.5 %copy-done.5 = f32[1,1280,1024]{2,1,0:T(8,128)S(1)} copy-done((f32[1,1280,1024]{2,1,0:T(8,128)S(1)}, f32[1,1280,1024]{2,1,0:T(8,128)}, u32[]{:S(2)}) %copy-start.5) | copy-done | bytes 5242904
  42.2 0.0 copy-start.9
  42.2 1.2 %copy-done.9 = bf16[512,1024]{1,0:T(8,128)(2,1)S(1)} copy-done((bf16[512,1024]{1,0:T(8,128)(2,1)S(1)}, bf16[512,1024]{1,0:T(8,128)(2,1)}, u32[]{:S(2)}) %copy-start.9) | copy-done | bytes 1048600
  43.4 7.6 %grad.1 = (f32[1280,1024]{1,0:T(8,128)}, f32[1280,1024]{1,0:T(8,128)}, bf16[4,256,1280]{2,1,0:T(8,128)(2,1)S(1)}, f32[8,128]{1,0:T(8,128)S(1)}) custom-call(s32[4]{0:T(128)S(1)} %bitcast.19, bf16[4,1280,128]{2,1,0:T(8,128)(2,1)S(1)} %all-to-all-done.1.normed_ref, bf16[512,1024]{1,0:T(8,128)(2,1)S(1)} %copy-done.9, f32[1280,1024]{1,0:T(8,128)S(1)} %bitcast.14, ...), custom_call_target="tpu_custom_call" | custom-call | flops 1 | bytes 1 | tf_op jit(solution)/shard_map/grad/pallas_call | solution.py:355
  51.0 0.0 copy-start.6
  51.0 1.5 %copy-done.6 = bf16[4,256,1280]{2,1,0:T(8,128)(2,1)} copy-done((bf16[4,256,1280]{2,1,0:T(8,128)(2,1)}, bf16[4,256,1280]{2,1,0:T(8,128)(2,1)S(1)}, u32[]{:S(2)}) %copy-start.6) | copy-done | bytes 2621464
  52.5 0.0 all-to-all-done.spread_ref
  52.5 0.0 copy-start.3
  52.5 0.0 copy-start.11
  52.5 4.7 %all-to-all-start.2 = ((bf16[4,256,1280]{2,1,0:T(8,128)(2,1)}), bf16[4,256,1280]{2,1,0:T(8,128)(2,1)}, u32[]{:S(2)}, u32[]{:S(2)}) async-start(bf16[4,256,1280]{2,1,0:T(8,128)(2,1)} %copy-done.6), calls=%async_computation.2 | async-start | bytes 5242880 | tf_op jit(solution)/shard_map/all_to_all | solution.py:382
  57.2 0.0 copy-done.3
  57.2 0.0 copy-done.11
  57.2 1.0 own.1
  58.3 0.1 collective-permute-start.3
  58.4 2.1 %collective-permute-done.3.got_ref = bf16[64,5120]{1,0:T(8,128)(2,1)S(1)} collective-permute-done((bf16[64,5120]{1,0:T(8,128)(2,1)S(1)}, bf16[64,5120]{1,0:T(8,128)(2,1)S(1)}, u32[]{:S(2)}, u32[]{:S(2)}) %collective-permute-start.3) | collective-permute-done | bytes 655392 | tf_op jit(solution)/shard_map/ppermute | solution.py:25
  60.5 0.2 pair.1
  60.6 0.7 collective-permute-start.4
  61.3 0.7 collective-permute-start.5
  62.0 0.0 collective-permute-done.4.one_ref
  62.0 0.0 collective-permute-done.5.two_ref
  62.0 0.2 middle.1
  62.3 1.3 %collective-permute-start.6 = (bf16[32,5120]{1,0:T(8,128)(2,1)S(1)}, bf16[32,5120]{1,0:T(8,128)(2,1)S(1)}, u32[]{:S(2)}, u32[]{:S(2)}) collective-permute-start(bf16[32,5120]{1,0:T(8,128)(2,1)S(1)} %get-tuple-element.31), channel_id=1, source_target_pairs={{8,0},{16,8},{24,16},{12,4},{20,12},{28,20},{9,1},{17,9},{25,17},{... | collective-permute-start | bytes 983048 | tf_op jit(solution)/shard_map/ppermute | solution.py:410
  63.6 1.3 %collective-permute-start.7 = (bf16[32,5120]{1,0:T(8,128)(2,1)S(1)}, bf16[32,5120]{1,0:T(8,128)(2,1)S(1)}, u32[]{:S(2)}, u32[]{:S(2)}) collective-permute-start(bf16[32,5120]{1,0:T(8,128)(2,1)S(1)} %get-tuple-element.32), channel_id=1, source_target_pairs={{16,0},{20,4},{17,1},{21,5},{18,2},{22,6},{19,3},{23,7}} | collective-permute-start | bytes 983048 | tf_op jit(solution)/shard_map/ppermute | solution.py:411
  64.9 23.0 %all-to-all-done.2.parts_ref = bf16[4,256,1280]{2,1,0:T(8,128)(2,1)} async-done(((bf16[4,256,1280]{2,1,0:T(8,128)(2,1)}), bf16[4,256,1280]{2,1,0:T(8,128)(2,1)}, u32[]{:S(2)}, u32[]{:S(2)}) %all-to-all-start.2) | async-done | bytes 2621472 | tf_op jit(solution)/shard_map/all_to_all | solution.py:382
  87.8 4.0 %rollout.1 = (bf16[256,5120]{1,0:T(8,128)(2,1)}, f32[8,128]{1,0:T(8,128)S(1)}) custom-call(bf16[4,256,1280]{2,1,0:T(8,128)(2,1)} %all-to-all-done.2.parts_ref), custom_call_target="tpu_custom_call" | custom-call | flops 1000000000 | bytes 1 | tf_op jit(solution)/shard_map/rollout/pallas_call | solution.py:373
  91.8 0.1 collective-permute-done.6.three_ref
  91.9 8.2 %collective-permute-done.7.four_ref = bf16[32,5120]{1,0:T(8,128)(2,1)S(1)} collective-permute-done((bf16[32,5120]{1,0:T(8,128)(2,1)S(1)}, bf16[32,5120]{1,0:T(8,128)(2,1)S(1)}, u32[]{:S(2)}, u32[]{:S(2)}) %collective-permute-start.7) | collective-permute-done | bytes 327712 | tf_op jit(solution)/shard_map/ppermute | solution.py:411
  100.1 1.3 %last.1 = (bf16[128,5120]{1,0:T(8,128)(2,1)}, bf16[64,5120]{1,0:T(8,128)(2,1)S(1)}) custom-call(s32[1]{0:T(128)} %bitcast.1.chip_ref, s32[1]{0:T(128)} %bitcast.core_ref, bf16[64,5120]{1,0:T(8,128)(2,1)S(1)} %get-tuple-element.27.keep_ref, bf16[64,5120]{1,0:T(8,128)(2,1)S(1)} %collective-permute-done.3.got_ref, ...), custom_call_target="tpu_custom_call" | custom-call | flops 1 | bytes 1 | tf_op jit(solution)/shard_map/last/pallas_call | solution.py:412
  101.4 0.0 collective-permute-start.8
  101.4 2.1 %collective-permute-done.8.part_ref = bf16[64,5120]{1,0:T(8,128)(2,1)S(1)} collective-permute-done((bf16[64,5120]{1,0:T(8,128)(2,1)S(1)}, bf16[64,5120]{1,0:T(8,128)(2,1)S(1)}, u32[]{:S(2)}, u32[]{:S(2)}) %collective-permute-start.8) | collective-permute-done | bytes 655392 | tf_op jit(solution)/shard_map/ppermute | solution.py:25
  103.5 0.9 join.1
Async XLA Ops:
  0.6 15.4 %collective-permute-start.2 = (bf16[128,1024]{1,0:T(8,128)(2,1)}, bf16[128,1024]{1,0:T(8,128)(2,1)S(1)}, u32[]{:S(2)}, u32[]{:S(2)}) collective-permute-start(bf16[128,1024]{1,0:T(8,128)(2,1)} %bitcast.20), channel_id=1, source_target_pairs={{0,3},{1,2},{2,1},{3,0},{4,7},{5,6},{6,5},{7,4},{8,11},{9,10},{10,... | collective-permute-start | bytes 786440 | tf_op jit(solution)/shard_map/ppermute | solution.py:25
  4.6 13.1 %collective-permute-start.1 = (bf16[128,1024]{1,0:T(8,128)(2,1)}, bf16[128,1024]{1,0:T(8,128)(2,1)S(1)}, u32[]{:S(2)}, u32[]{:S(2)}) collective-permute-start(bf16[128,1024]{1,0:T(8,128)(2,1)} %bitcast.21), channel_id=1, source_target_pairs={{0,2},{1,3},{2,0},{3,1},{4,6},{5,7},{6,4},{7,5},{8,10},{9,11},{10,... | collective-permute-start | bytes 786440 | tf_op jit(solution)/shard_map/ppermute | solution.py:25
  5.1 13.1 %collective-permute-start = (bf16[128,1024]{1,0:T(8,128)(2,1)}, bf16[128,1024]{1,0:T(8,128)(2,1)S(1)}, u32[]{:S(2)}, u32[]{:S(2)}) collective-permute-start(bf16[128,1024]{1,0:T(8,128)(2,1)} %bitcast.22), channel_id=1, source_target_pairs={{0,1},{1,0},{2,3},{3,2},{4,5},{5,4},{6,7},{7,6},{8,9},{9,8},{10,11... | collective-permute-start | bytes 786440 | tf_op jit(solution)/shard_map/ppermute | solution.py:25
  5.2 1.3 %copy-start.2 = (bf16[1,128,5120]{2,1,0:T(8,128)(2,1)S(1)}, bf16[1,128,5120]{2,1,0:T(8,128)(2,1)}, u32[]{:S(2)}) copy-start(bf16[1,128,5120]{2,1,0:T(8,128)(2,1)} %param.8) | copy-start | bytes 3932164
  6.6 0.7 copy-start.10
  9.1 22.0 %all-to-all-start.1 = ((bf16[4,1280,128]{2,1,0:T(8,128)(2,1)}), bf16[4,1280,128]{2,1,0:T(8,128)(2,1)S(1)}, u32[]{:S(2)}, u32[]{:S(2)}) async-start(bf16[4,1280,128]{2,1,0:T(8,128)(2,1)} %get-tuple-element.24), calls=%async_computation.1 | async-start | bytes 2621440 | tf_op jit(solution)/shard_map/all_to_all | solution.py:330
  13.2 2.5 %copy-start = (f32[1,1280,1024]{2,1,0:T(8,128)S(1)}, f32[1,1280,1024]{2,1,0:T(8,128)}, u32[]{:S(2)}) copy-start(f32[1,1280,1024]{2,1,0:T(8,128)} %param.11) | copy-start | bytes 15728644
  15.7 2.5 %copy-start.13 = (bf16[1,128,1024]{2,1,0:T(8,128)(2,1)S(1)}, bf16[1,128,1024]{2,1,0:T(8,128)(2,1)}, u32[]{:S(2)}) copy-start(bf16[1,128,1024]{2,1,0:T(8,128)(2,1)} %param.9) | copy-start | bytes 786436
  15.7 2.5 %copy-start.14 = (s32[4]{0:T(128)S(1)}, s32[4]{0:T(128)}, u32[]{:S(2)}) copy-start(s32[4]{0:T(128)} %plan_ref.1) | copy-start | bytes 52
  20.3 1.1 %copy-start.7 = (bf16[4,128,1280]{2,1,0:T(8,128)(2,1)}, bf16[4,128,1280]{2,1,0:T(8,128)(2,1)S(1)}, u32[]{:S(2)}) copy-start(bf16[4,128,1280]{2,1,0:T(8,128)(2,1)S(1)} %get-tuple-element.23) | copy-start | bytes 3932164
  21.4 1.0 copy-start.8
  22.3 12.4 %copy-start.12 = (s32[1,4]{1,0:T(1,128)S(1)}, s32[1,4]{1,0:T(1,128)}, u32[]{:S(2)}) copy-start(s32[1,4]{1,0:T(1,128)} %param.14) | copy-start | bytes 52
  31.1 21.4 %all-to-all-start = ((bf16[4,128,1280]{2,1,0:T(8,128)(2,1)}), bf16[4,128,1280]{2,1,0:T(8,128)(2,1)S(1)}, u32[]{:S(2)}, u32[]{:S(2)}) async-start(bf16[4,128,1280]{2,1,0:T(8,128)(2,1)} %copy-done.7), calls=%async_computation | async-start | bytes 2621440 | tf_op jit(solution)/shard_map/all_to_all | solution.py:352
  34.7 2.5 %copy-start.1 = (f32[1,1280,1024]{2,1,0:T(8,128)S(1)}, f32[1,1280,1024]{2,1,0:T(8,128)}, u32[]{:S(2)}) copy-start(f32[1,1280,1024]{2,1,0:T(8,128)} %param.11) | copy-start | bytes 15728644
  37.2 2.5 %copy-start.4 = (f32[1,1280,1024]{2,1,0:T(8,128)S(1)}, f32[1,1280,1024]{2,1,0:T(8,128)}, u32[]{:S(2)}) copy-start(f32[1,1280,1024]{2,1,0:T(8,128)} %param.12) | copy-start | bytes 15728644
  39.7 2.5 %copy-start.5 = (f32[1,1280,1024]{2,1,0:T(8,128)S(1)}, f32[1,1280,1024]{2,1,0:T(8,128)}, u32[]{:S(2)}) copy-start(f32[1,1280,1024]{2,1,0:T(8,128)} %param.13) | copy-start | bytes 15728644
  42.2 1.2 %copy-start.9 = (bf16[512,1024]{1,0:T(8,128)(2,1)S(1)}, bf16[512,1024]{1,0:T(8,128)(2,1)}, u32[]{:S(2)}) copy-start(bf16[512,1024]{1,0:T(8,128)(2,1)} %copy-done.8) | copy-start | bytes 3145732
  51.0 1.5 %copy-start.6 = (bf16[4,256,1280]{2,1,0:T(8,128)(2,1)}, bf16[4,256,1280]{2,1,0:T(8,128)(2,1)S(1)}, u32[]{:S(2)}) copy-start(bf16[4,256,1280]{2,1,0:T(8,128)(2,1)S(1)} %get-tuple-element.33) | copy-start | bytes 7864324
  52.5 4.7 %copy-start.3 = (bf16[1,128,5120]{2,1,0:T(8,128)(2,1)S(1)}, bf16[1,128,5120]{2,1,0:T(8,128)(2,1)}, u32[]{:S(2)}) copy-start(bf16[1,128,5120]{2,1,0:T(8,128)(2,1)} %param.8) | copy-start | bytes 3932164
  52.5 4.7 %copy-start.11 = (f32[1,5120]{1,0:T(1,128)S(1)}, f32[1,5120]{1,0:T(1,128)}, u32[]{:S(2)}) copy-start(f32[1,5120]{1,0:T(1,128)} %gain_ref.3) | copy-start | bytes 61444
  52.5 35.3 %all-to-all-start.2 = ((bf16[4,256,1280]{2,1,0:T(8,128)(2,1)}), bf16[4,256,1280]{2,1,0:T(8,128)(2,1)}, u32[]{:S(2)}, u32[]{:S(2)}) async-start(bf16[4,256,1280]{2,1,0:T(8,128)(2,1)} %copy-done.6), calls=%async_computation.2 | async-start | bytes 5242880 | tf_op jit(solution)/shard_map/all_to_all | solution.py:382
  58.3 2.2 %collective-permute-start.3 = (bf16[64,5120]{1,0:T(8,128)(2,1)S(1)}, bf16[64,5120]{1,0:T(8,128)(2,1)S(1)}, u32[]{:S(2)}, u32[]{:S(2)}) collective-permute-start(bf16[64,5120]{1,0:T(8,128)(2,1)S(1)} %get-tuple-element.28), channel_id=1, source_target_pairs={{0,4},{4,0},{8,12},{12,8},{16,20},{20,16},{24,28},{28,24},{1,5},{5... | collective-permute-start | bytes 1966088 | tf_op jit(solution)/shard_map/ppermute | solution.py:25
  60.6 1.4 %collective-permute-start.4 = (bf16[32,5120]{1,0:T(8,128)(2,1)S(1)}, bf16[32,5120]{1,0:T(8,128)(2,1)S(1)}, u32[]{:S(2)}, u32[]{:S(2)}) collective-permute-start(bf16[32,5120]{1,0:T(8,128)(2,1)S(1)} %get-tuple-element.29), channel_id=1, source_target_pairs={{24,8},{8,16},{28,12},{12,20},{25,9},{9,17},{29,13},{13,21},{26,10... | collective-permute-start | bytes 983048 | tf_op jit(solution)/shard_map/ppermute | solution.py:405
  61.3 0.7 collective-permute-start.5
  62.3 29.6 %collective-permute-start.6 = (bf16[32,5120]{1,0:T(8,128)(2,1)S(1)}, bf16[32,5120]{1,0:T(8,128)(2,1)S(1)}, u32[]{:S(2)}, u32[]{:S(2)}) collective-permute-start(bf16[32,5120]{1,0:T(8,128)(2,1)S(1)} %get-tuple-element.31), channel_id=1, source_target_pairs={{8,0},{16,8},{24,16},{12,4},{20,12},{28,20},{9,1},{17,9},{25,17},{... | collective-permute-start | bytes 983048 | tf_op jit(solution)/shard_map/ppermute | solution.py:410
  63.6 36.5 %collective-permute-start.7 = (bf16[32,5120]{1,0:T(8,128)(2,1)S(1)}, bf16[32,5120]{1,0:T(8,128)(2,1)S(1)}, u32[]{:S(2)}, u32[]{:S(2)}) collective-permute-start(bf16[32,5120]{1,0:T(8,128)(2,1)S(1)} %get-tuple-element.32), channel_id=1, source_target_pairs={{16,0},{20,4},{17,1},{21,5},{18,2},{22,6},{19,3},{23,7}} | collective-permute-start | bytes 983048 | tf_op jit(solution)/shard_map/ppermute | solution.py:411
  101.4 2.1 %collective-permute-start.8 = (bf16[64,5120]{1,0:T(8,128)(2,1)S(1)}, bf16[64,5120]{1,0:T(8,128)(2,1)S(1)}, u32[]{:S(2)}, u32[]{:S(2)}) collective-permute-start(bf16[64,5120]{1,0:T(8,128)(2,1)S(1)} %get-tuple-element.35), channel_id=1, source_target_pairs={{0,4},{4,0},{8,12},{12,8},{16,20},{20,16},{24,28},{28,24},{1,5},{5... | collective-permute-start | bytes 1966088 | tf_op jit(solution)/shard_map/ppermute | solution.py:25

commit v5 on v3

--- a/solution.py
+++ b/solution.py
@@ -227,30 +227,30 @@
             outs[k][p * head : (p + 1) * head, :] = fresh[:, lanes].T
 
 
-def own_body(count, place_ref, core_ref, tok_ref, gain_ref, inv_ref, *refs):
-    spread, (_, keep_ref, give_ref) = refs[:count], refs[count:]
+def own_body(count, mine, place_ref, core_ref, tok_ref, gain_ref, inv_ref, *refs):
+    spread, out_ref = refs[:count], refs[-1]
     place = place_ref[0]
     core = core_ref[0]
     width = tok_ref.shape[1]
     cols = width // count
     half = tok_ref.shape[0] // 2
-    for out_ref, pick in ((give_ref, 1 - core), (keep_ref, core)):
-        rows = pl.ds(pl.multiple_of(pick * half, half), half)
-        inverse = inv_ref[rows, :]
-        total = jnp.zeros((half, 1), f32)
-        for k in range(count):
-            part = part_of(place, k, cols)
-            scaled = spread[k][rows, :].astype(f32) * gain_ref[:, part]
-            total = total + jnp.sum(
-                scaled * tok_ref[rows, part].astype(f32), axis=-1, keepdims=True
-            )
-        factor = inverse * inverse * inverse * (total / width)
-        for k in range(count):
-            part = part_of(place, k, cols)
-            scaled = spread[k][rows, :].astype(f32) * gain_ref[:, part]
-            out_ref[:, part] = (
-                inverse * scaled - tok_ref[rows, part].astype(f32) * factor
-            ).astype(bf16)
+    pick = core if mine else 1 - core
+    rows = pl.ds(pl.multiple_of(pick * half, half), half)
+    inverse = inv_ref[rows, :]
+    total = jnp.zeros((half, 1), f32)
+    for k in range(count):
+        part = part_of(place, k, cols)
+        scaled = spread[k][rows, :].astype(f32) * gain_ref[:, part]
+        total = total + jnp.sum(
+            scaled * tok_ref[rows, part].astype(f32), axis=-1, keepdims=True
+        )
+    factor = inverse * inverse * inverse * (total / width)
+    for k in range(count):
+        part = part_of(place, k, cols)
+        scaled = spread[k][rows, :].astype(f32) * gain_ref[:, part]
+        out_ref[:, part] = (
+            inverse * scaled - tok_ref[rows, part].astype(f32) * factor
+        ).astype(bf16)
 
 
 def pair_body(chip_ref, keep_ref, got_ref, one_ref, two_ref):
@@ -272,10 +272,11 @@
     four_ref[...] = (mine + one).astype(bf16)
 
 
-def last_body(chip_ref, core_ref, keep_ref, got_ref, one_ref, two_ref, three_ref, four_ref, _, out_ref, send_ref):
+def last_body(mine, chip_ref, core_ref, keep_ref, got_ref, one_ref, two_ref, three_ref, four_ref, _, out_ref):
     z = chip_ref[0]
-    core = core_ref[0]
+    lower = (core_ref[0] == 0) == mine
     half = one_ref.shape[0]
+    kept, came = (keep_ref, got_ref) if mine else (got_ref, keep_ref)
     for part in range(2):
         rows = slice(part * half, (part + 1) * half)
         one = one_ref[...].astype(f32)
@@ -286,11 +287,9 @@
         else:
             four = four_ref[...].astype(f32)
             above = jnp.where(z == 0, four, jnp.where(z == 1, three, two))
-        keep = keep_ref[rows, :].astype(f32)
-        got = got_ref[rows, :].astype(f32)
-        both = keep + got + above
-        out_ref[rows, :] = jnp.where(core == 0, both, keep + above).astype(bf16)
-        send_ref[rows, :] = jnp.where(core == 0, got + above, both).astype(bf16)
+        total = kept[rows, :].astype(f32) + above
+        both = total + came[rows, :].astype(f32)
+        out_ref[rows, :] = jnp.where(lower, both, total).astype(bf16)
 
 
 def place_body(place_ref, part_ref, *refs):
@@ -391,20 +390,25 @@
             + ([whole((8, 128))] if final else []),
             [sds((2 * head, width), bf16)] + ([mark] if final else []),
             aliases={2: 0} if k else None,
-            work=10**9,
+            work=1,
         )(place, part, *([rollout] if k else []))
 
-    keep, give = call(
-        "own",
-        functools.partial(own_body, count),
-        (1,),
-        2,
-        [whole((tok_count, width)), whole((1, width)), whole((tok_count, 1))]
-        + [whole((tok_count, cols))] * count
-        + [anywhere],
-        [whole((half, width))] * 2,
-        [sds((half, width), bf16)] * 2,
-    )(place, core, tok_rows, norm_gain, inverse, *spread, grad_mark)
+    def own(name, mine, after):
+        (term,) = call(
+            name,
+            functools.partial(own_body, count, mine),
+            (1,),
+            2,
+            [whole((tok_count, width)), whole((1, width)), whole((tok_count, 1))]
+            + [whole((tok_count, cols))] * count
+            + [anywhere],
+            [whole((half, width))],
+            [sds((half, width), bf16)],
+        )(place, core, tok_rows, norm_gain, inverse, *spread, after)
+        return term
+
+    give = own("own", False, grad_mark)
+    keep = own("keep", True, give)
     got = swap(give, "section", 1)
 
     def chips(pairs):
@@ -423,16 +427,27 @@
     )(chip, keep, got, one, two)
     three = lax.ppermute(three, "section", chips([(1, 0), (2, 1), (3, 2)]))
     four = lax.ppermute(four, "section", chips([(2, 0)]))
-    grads, send = call(
+    terms = (chip, core, keep, got, one, two, three, four)
+    shapes = [full, full, part, part, part, part, anywhere]
+    (send,) = call(
         "last",
-        last_body,
+        functools.partial(last_body, False),
         (1,),
         2,
-        [full, full, part, part, part, part, anywhere],
-        [pl.BlockSpec((half, width), lambda i, chip_ref, core_ref: (core_ref[0], 0)), full],
-        [sds((tok_count, width), bf16), sds((half, width), bf16)],
-    )(chip, core, keep, got, one, two, three, four, *rollout_mark)
+        shapes,
+        [full],
+        [sds((half, width), bf16)],
+    )(*terms, *rollout_mark)
     other = swap(send, "section", 1)
+    (grads,) = call(
+        "mine",
+        functools.partial(last_body, True),
+        (1,),
+        2,
+        shapes,
+        [pl.BlockSpec((half, width), lambda i, chip_ref, core_ref: (core_ref[0], 0))],
+        [sds((tok_count, width), bf16)],
+    )(*terms, send)
     grads = call(
         "join",
         place_body,

time: 93.8 us -> 92.7 us (0.988)
  waiting for transfers between devices: 49.1 us -> 47.5 us
    ppermute x14, waiting for transfers between devices: 40.4 us -> 38.5 us  [swap(): return lax.ppermute(x, axis, [(i, i ^ k) for i in range(count)])]
    pallas_call x2 -> x4, Pallas kernels: 2.52 us -> 2.95 us  [the longest x1 1.31 us: shards(): call('mine', functools.partial(last_body, True), (1,), 2, shapes, [pl.Blo...]
  transfers between devices with their start and end apart: 18 -> 18, of which waited for: 11 -> 11; matrix products, arithmetic and copies ran while one was open for 0% -> 0% of each run, Pallas kernels for 16% -> 18%
where the time goes in v5:
time: 92.7 us; the launch traced here: 92.4 us
  waiting for transfers between devices  47.5 us (51%)
  starting transfers between devices  21 us (23%)
  Pallas kernels  18.5 us (20%)
  local copies, waits for them, and re-layouts  4.59 us (5%)
    ppermute x14, waiting for transfers between devices, swap(): return lax.ppermute(x, axis, [(i, i ^ k) for i in range(count)])  38.5 us
    ppermute x14, starting transfers between devices, swap(): return lax.ppermute(x, axis, [(i, i ^ k) for i in range(count)])  17 us
    ppermute x1, waiting for transfers between devices, shards(): four = lax.ppermute(four, 'section', chips([(2, 0)]))  8.19 us
    pallas_call x1, Pallas kernels, shards(): call('grad', functools.partial(grad_body, count, head, scale), (cols // r...  7.59 us
    unnamed x28, local copies, waits for them, and re-layouts  4.59 us
    pallas_call x4, Pallas kernels, shards(): call('place', marked_body if final else place_body, (1,), 1, [whole((2 *...  3.52 us
    pallas_call x1, Pallas kernels, shards(): call('spread', functools.partial(spread_body, count, plan.shape[0], scale...  2.1 us
  transfers between devices with their start and end apart: 18, of which 11 were waited for; matrix products, arithmetic and copies ran while one was open for 0% of the time, Pallas kernels for 18%

profile of v5, /device:TPU:0, one launch (start us, length us, event | category | flops | bytes accessed | tf_op | source)
XLA Modules:
  0.0 92.4 jit_solution(16909126801296776800)
XLA Ops:
  0.6 3.0 %collective-permute-start = (bf16[128,1024]{1,0:T(8,128)(2,1)}, bf16[128,1024]{1,0:T(8,128)(2,1)S(1)}, u32[]{:S(2)}, u32[]{:S(2)}) collective-permute-start(bf16[128,1024]{1,0:T(8,128)(2,1)} %bitcast.27), channel_id=1, source_target_pairs={{0,1},{1,0},{2,3},{3,2},{4,5},{5,4},{6,7},{7,6},{8,9},{9,8},{10,11... | collective-permute-start | bytes 786440 | tf_op jit(solution)/shard_map/ppermute | solution.py:25
  3.6 1.5 %collective-permute-start.1 = (bf16[128,1024]{1,0:T(8,128)(2,1)}, bf16[128,1024]{1,0:T(8,128)(2,1)S(1)}, u32[]{:S(2)}, u32[]{:S(2)}) collective-permute-start(bf16[128,1024]{1,0:T(8,128)(2,1)} %bitcast.28), channel_id=1, source_target_pairs={{0,2},{1,3},{2,0},{3,1},{4,6},{5,7},{6,4},{7,5},{8,10},{9,11},{10,... | collective-permute-start | bytes 786440 | tf_op jit(solution)/shard_map/ppermute | solution.py:25
  5.2 0.0 collective-permute-start.2
  5.2 1.3 %copy-done.1 = bf16[1,128,5120]{2,1,0:T(8,128)(2,1)S(1)} copy-done((bf16[1,128,5120]{2,1,0:T(8,128)(2,1)S(1)}, bf16[1,128,5120]{2,1,0:T(8,128)(2,1)}, u32[]{:S(2)}) %copy-start.1) | copy-done | bytes 1310744
  6.5 0.7 copy-done.3
  7.2 0.7 prep.1
  8.0 2.0 %collective-permute-start.6 = (bf16[1280,128]{1,0:T(8,128)(2,1)S(1)}, bf16[1280,128]{1,0:T(8,128)(2,1)S(1)}, u32[]{:S(2)}, u32[]{:S(2)}) collective-permute-start(bf16[1280,128]{1,0:T(8,128)(2,1)S(1)} %get-tuple-element.33), channel_id=1, source_target_pairs={{0,1},{1,0},{2,3},{3,2},{4,5},{5,4},{6,7},{7,6},{8,9},{9,8},{10,11... | collective-permute-start | bytes 983048 | tf_op jit(solution)/shard_map/ppermute | solution.py:25
  10.0 1.5 %collective-permute-start.7 = (bf16[1280,128]{1,0:T(8,128)(2,1)S(1)}, bf16[1280,128]{1,0:T(8,128)(2,1)S(1)}, u32[]{:S(2)}, u32[]{:S(2)}) collective-permute-start(bf16[1280,128]{1,0:T(8,128)(2,1)S(1)} %get-tuple-element.34), channel_id=1, source_target_pairs={{0,2},{1,3},{2,0},{3,1},{4,6},{5,7},{6,4},{7,5},{8,10},{9,11},{10,... | collective-permute-start | bytes 983048 | tf_op jit(solution)/shard_map/ppermute | solution.py:25
  11.5 2.5 %copy-done = f32[1,1280,1024]{2,1,0:T(8,128)S(1)} copy-done((f32[1,1280,1024]{2,1,0:T(8,128)S(1)}, f32[1,1280,1024]{2,1,0:T(8,128)}, u32[]{:S(2)}) %copy-start) | copy-done | bytes 5242904
  14.0 0.3 low.1.refs_4_
  14.3 0.0 collective-permute-done.refs_1_
  14.3 0.0 slice-start
  14.3 0.0 slice-start.2
  14.4 0.0 slice-start.4
  14.4 0.0 slice-start.1
  14.4 0.0 slice-start.3
  14.4 0.0 slice-start.5
  14.4 0.0 copy-start.5
  14.4 0.1 collective-permute-start.8
  14.5 3.3 %collective-permute-done.1.refs_2_ = bf16[128,1024]{1,0:T(8,128)(2,1)S(1)} collective-permute-done((bf16[128,1024]{1,0:T(8,128)(2,1)}, bf16[128,1024]{1,0:T(8,128)(2,1)S(1)}, u32[]{:S(2)}, u32[]{:S(2)}) %collective-permute-start.1) | collective-permute-done | bytes 262176 | tf_op jit(solution)/shard_map/ppermute | solution.py:25
  17.9 0.3 collective-permute-done.2.refs_3_
  18.2 2.1 %spread.1 = (bf16[512,1024]{1,0:T(8,128)(2,1)S(1)}, bf16[128,1280]{1,0:T(8,128)(2,1)S(1)}, bf16[128,1280]{1,0:T(8,128)(2,1)S(1)}, bf16[128,1280]{1,0:T(8,128)(2,1)S(1)}, bf16[128,1280]{1,0:T(8,128)(2,1)S(1)}) custom-call(s32[4]{0:T(128)S(1)} %copy-done.7, bf16[128,1024]{1,0:T(8,128)(2,1)S(1)} %bitcast.30, ...), custom_call_target="tpu_custom_call" | custom-call | flops 10000000000 | bytes 1 | tf_op jit(solution)/shard_map/spread/pallas_call | solution.py:347
  20.3 1.6 %collective-permute-start.3 = (bf16[128,1280]{1,0:T(8,128)(2,1)S(1)}, bf16[128,1280]{1,0:T(8,128)(2,1)S(1)}, u32[]{:S(2)}, u32[]{:S(2)}) collective-permute-start(bf16[128,1280]{1,0:T(8,128)(2,1)S(1)} %get-tuple-element.29), channel_id=1, source_target_pairs={{0,1},{1,0},{2,3},{3,2},{4,5},{5,4},{6,7},{7,6},{8,9},{9,8},{10,11... | collective-permute-start | bytes 983048 | tf_op jit(solution)/shard_map/ppermute | solution.py:25
  21.8 0.5 collective-permute-start.4
  22.4 1.3 %collective-permute-done.6.refs_1_ = bf16[1280,128]{1,0:T(8,128)(2,1)S(1)} collective-permute-done((bf16[1280,128]{1,0:T(8,128)(2,1)S(1)}, bf16[1280,128]{1,0:T(8,128)(2,1)S(1)}, u32[]{:S(2)}, u32[]{:S(2)}) %collective-permute-start.6) | collective-permute-done | bytes 327712 | tf_op jit(solution)/shard_map/ppermute | solution.py:25
  23.7 3.0 %collective-permute-start.5 = (bf16[128,1280]{1,0:T(8,128)(2,1)S(1)}, bf16[128,1280]{1,0:T(8,128)(2,1)S(1)}, u32[]{:S(2)}, u32[]{:S(2)}) collective-permute-start(bf16[128,1280]{1,0:T(8,128)(2,1)S(1)} %get-tuple-element.31), channel_id=1, source_target_pairs={{0,3},{1,2},{2,1},{3,0},{4,7},{5,6},{6,5},{7,4},{8,11},{9,10},{10,... | collective-permute-start | bytes 983048 | tf_op jit(solution)/shard_map/ppermute | solution.py:25
  26.7 5.2 %collective-permute-done.7.refs_2_ = bf16[1280,128]{1,0:T(8,128)(2,1)S(1)} collective-permute-done((bf16[1280,128]{1,0:T(8,128)(2,1)S(1)}, bf16[1280,128]{1,0:T(8,128)(2,1)S(1)}, u32[]{:S(2)}, u32[]{:S(2)}) %collective-permute-start.7) | collective-permute-done | bytes 327712 | tf_op jit(solution)/shard_map/ppermute | solution.py:25
  31.9 0.4 collective-permute-done.8.refs_3_
  32.3 0.0 slice-done.1
  32.3 0.0 copy-start.2
  32.3 0.0 copy-start.4
  32.4 7.6 %grad.1 = (f32[1280,1024]{1,0:T(8,128)}, f32[1280,1024]{1,0:T(8,128)}, bf16[256,1280]{1,0:T(8,128)(2,1)S(1)}, bf16[256,1280]{1,0:T(8,128)(2,1)S(1)}, bf16[256,12...) custom-call(s32[1]{0:T(128)} %bitcast.2.place_ref, s32[4]{0:T(128)S(1)} %bitcast.26, ...), custom_call_target="tpu_custom_call" | custom-call | flops 1 | bytes 1 | tf_op jit(solution)/shard_map/grad/pallas_call | solution.py:360
  39.9 0.0 collective-permute-done.3.refs_1_
  39.9 5.4 %collective-permute-done.4.refs_2_ = bf16[128,1280]{1,0:T(8,128)(2,1)S(1)} collective-permute-done((bf16[128,1280]{1,0:T(8,128)(2,1)S(1)}, bf16[128,1280]{1,0:T(8,128)(2,1)S(1)}, u32[]{:S(2)}, u32[]{:S(2)}) %collective-permute-start.4) | collective-permute-done | bytes 327712 | tf_op jit(solution)/shard_map/ppermute | solution.py:25
  45.3 0.0 collective-permute-done.5.refs_3_
  45.3 0.6 own.1.refs_4_
  45.9 0.1 collective-permute-start.9
  46.0 1.6 %collective-permute-start.16 = (bf16[256,1280]{1,0:T(8,128)(2,1)S(1)}, bf16[256,1280]{1,0:T(8,128)(2,1)S(1)}, u32[]{:S(2)}, u32[]{:S(2)}) collective-permute-start(bf16[256,1280]{1,0:T(8,128)(2,1)S(1)} %get-tuple-element.44), channel_id=1, source_target_pairs={{0,3},{1,2},{2,1},{3,0},{4,7},{5,6},{6,5},{7,4},{8,11},{9,10},{10,... | collective-permute-start | bytes 1966088 | tf_op jit(solution)/shard_map/ppermute | solution.py:25
  47.6 1.5 %collective-permute-start.15 = (bf16[256,1280]{1,0:T(8,128)(2,1)S(1)}, bf16[256,1280]{1,0:T(8,128)(2,1)S(1)}, u32[]{:S(2)}, u32[]{:S(2)}) collective-permute-start(bf16[256,1280]{1,0:T(8,128)(2,1)S(1)} %get-tuple-element.43), channel_id=1, source_target_pairs={{0,1},{1,0},{2,3},{3,2},{4,5},{5,4},{6,7},{7,6},{8,9},{9,8},{10,11... | collective-permute-start | bytes 1966088 | tf_op jit(solution)/shard_map/ppermute | solution.py:25
  49.0 0.6 keep.1.keep_ref
  49.6 0.0 collective-permute-done.9.got_ref
  49.6 0.2 pair.1
  49.8 0.7 collective-permute-start.10
  50.5 0.7 collective-permute-start.11
  51.2 0.6 collective-permute-start.14
  51.8 0.0 collective-permute-done.10.one_ref
  51.8 0.0 collective-permute-done.11.two_ref
  51.8 0.2 middle.1
  52.0 1.3 %collective-permute-start.12 = (bf16[32,5120]{1,0:T(8,128)(2,1)S(1)}, bf16[32,5120]{1,0:T(8,128)(2,1)S(1)}, u32[]{:S(2)}, u32[]{:S(2)}) collective-permute-start(bf16[32,5120]{1,0:T(8,128)(2,1)S(1)} %get-tuple-element.40), channel_id=1, source_target_pairs={{8,0},{16,8},{24,16},{12,4},{20,12},{28,20},{9,1},{17,9},{25,17},{... | collective-permute-start | bytes 983048 | tf_op jit(solution)/shard_map/ppermute | solution.py:428
  53.3 1.3 %collective-permute-start.13 = (bf16[32,5120]{1,0:T(8,128)(2,1)S(1)}, bf16[32,5120]{1,0:T(8,128)(2,1)S(1)}, u32[]{:S(2)}, u32[]{:S(2)}) collective-permute-start(bf16[32,5120]{1,0:T(8,128)(2,1)S(1)} %get-tuple-element.41), channel_id=1, source_target_pairs={{16,0},{20,4},{17,1},{21,5},{18,2},{22,6},{19,3},{23,7}} | collective-permute-start | bytes 983048 | tf_op jit(solution)/shard_map/ppermute | solution.py:429
  54.6 0.9 place.4.refs_0_
  55.5 9.0 %collective-permute-done.16.part_ref = bf16[256,1280]{1,0:T(8,128)(2,1)S(1)} collective-permute-done((bf16[256,1280]{1,0:T(8,128)(2,1)S(1)}, bf16[256,1280]{1,0:T(8,128)(2,1)S(1)}, u32[]{:S(2)}, u32[]{:S(2)}) %collective-permute-start.16) | collective-permute-done | bytes 655392 | tf_op jit(solution)/shard_map/ppermute | solution.py:25
  64.5 0.9 place.5.refs_0_
  65.4 12.8 %collective-permute-done.15.part_ref = bf16[256,1280]{1,0:T(8,128)(2,1)S(1)} collective-permute-done((bf16[256,1280]{1,0:T(8,128)(2,1)S(1)}, bf16[256,1280]{1,0:T(8,128)(2,1)S(1)}, u32[]{:S(2)}, u32[]{:S(2)}) %collective-permute-start.15) | collective-permute-done | bytes 655392 | tf_op jit(solution)/shard_map/ppermute | solution.py:25
  78.2 0.9 place.6._
  79.1 0.0 collective-permute-done.14.part_ref
  79.1 0.9 place.7
  80.0 0.8 collective-permute-done.12.three_ref
  80.7 8.2 %collective-permute-done.13.four_ref = bf16[32,5120]{1,0:T(8,128)(2,1)S(1)} collective-permute-done((bf16[32,5120]{1,0:T(8,128)(2,1)S(1)}, bf16[32,5120]{1,0:T(8,128)(2,1)S(1)}, u32[]{:S(2)}, u32[]{:S(2)}) %collective-permute-start.13) | collective-permute-done | bytes 327712 | tf_op jit(solution)/shard_map/ppermute | solution.py:429
  88.9 0.5 last.1._
  89.4 0.1 collective-permute-start.17
  89.5 1.3 %mine.1.refs_0_ = bf16[128,5120]{1,0:T(8,128)(2,1)} custom-call(s32[1]{0:T(128)} %bitcast.1.chip_ref, s32[1]{0:T(128)} %bitcast.core_ref.place_ref, bf16[64,5120]{1,0:T(8,128)(2,1)S(1)} %keep.1.keep_ref, bf16[64,5120]{1,0:T(8,128)(2,1)S(1)} %collective-permute-done.9.got_ref, bf16[32,5120]{1,0:T(8,128)(2,1)S(1)} %collective-permute-done.10.one_ref, ...), custom_call_target="tpu_custom_call" | custom-call | flops 1 | bytes 1 | tf_op jit(solution)/shard_map/mine/pallas_call | solution.py:442
  90.8 0.8 collective-permute-done.17.part_ref
  91.6 0.9 join.1
  (18 shorter events, 0.0 us)
Async XLA Ops:
  0.6 13.7 %collective-permute-start = (bf16[128,1024]{1,0:T(8,128)(2,1)}, bf16[128,1024]{1,0:T(8,128)(2,1)S(1)}, u32[]{:S(2)}, u32[]{:S(2)}) collective-permute-start(bf16[128,1024]{1,0:T(8,128)(2,1)} %bitcast.27), channel_id=1, source_target_pairs={{0,1},{1,0},{2,3},{3,2},{4,5},{5,4},{6,7},{7,6},{8,9},{9,8},{10,11... | collective-permute-start | bytes 786440 | tf_op jit(solution)/shard_map/ppermute | solution.py:25
  3.6 14.2 %collective-permute-start.1 = (bf16[128,1024]{1,0:T(8,128)(2,1)}, bf16[128,1024]{1,0:T(8,128)(2,1)S(1)}, u32[]{:S(2)}, u32[]{:S(2)}) collective-permute-start(bf16[128,1024]{1,0:T(8,128)(2,1)} %bitcast.28), channel_id=1, source_target_pairs={{0,2},{1,3},{2,0},{3,1},{4,6},{5,7},{6,4},{7,5},{8,10},{9,11},{10,... | collective-permute-start | bytes 786440 | tf_op jit(solution)/shard_map/ppermute | solution.py:25
  5.2 13.0 %collective-permute-start.2 = (bf16[128,1024]{1,0:T(8,128)(2,1)}, bf16[128,1024]{1,0:T(8,128)(2,1)S(1)}, u32[]{:S(2)}, u32[]{:S(2)}) collective-permute-start(bf16[128,1024]{1,0:T(8,128)(2,1)} %bitcast.29), channel_id=1, source_target_pairs={{0,3},{1,2},{2,1},{3,0},{4,7},{5,6},{6,5},{7,4},{8,11},{9,10},{10,... | collective-permute-start | bytes 786440 | tf_op jit(solution)/shard_map/ppermute | solution.py:25
  5.2 1.3 %copy-start.1 = (bf16[1,128,5120]{2,1,0:T(8,128)(2,1)S(1)}, bf16[1,128,5120]{2,1,0:T(8,128)(2,1)}, u32[]{:S(2)}) copy-start(bf16[1,128,5120]{2,1,0:T(8,128)(2,1)} %param.8) | copy-start | bytes 3932164
  6.5 0.7 copy-start.3
  8.0 15.7 %collective-permute-start.6 = (bf16[1280,128]{1,0:T(8,128)(2,1)S(1)}, bf16[1280,128]{1,0:T(8,128)(2,1)S(1)}, u32[]{:S(2)}, u32[]{:S(2)}) collective-permute-start(bf16[1280,128]{1,0:T(8,128)(2,1)S(1)} %get-tuple-element.33), channel_id=1, source_target_pairs={{0,1},{1,0},{2,3},{3,2},{4,5},{5,4},{6,7},{7,6},{8,9},{9,8},{10,11... | collective-permute-start | bytes 983048 | tf_op jit(solution)/shard_map/ppermute | solution.py:25
  10.0 21.9 %collective-permute-start.7 = (bf16[1280,128]{1,0:T(8,128)(2,1)S(1)}, bf16[1280,128]{1,0:T(8,128)(2,1)S(1)}, u32[]{:S(2)}, u32[]{:S(2)}) collective-permute-start(bf16[1280,128]{1,0:T(8,128)(2,1)S(1)} %get-tuple-element.34), channel_id=1, source_target_pairs={{0,2},{1,3},{2,0},{3,1},{4,6},{5,7},{6,4},{7,5},{8,10},{9,11},{10,... | collective-permute-start | bytes 983048 | tf_op jit(solution)/shard_map/ppermute | solution.py:25
  11.5 2.5 %copy-start = (f32[1,1280,1024]{2,1,0:T(8,128)S(1)}, f32[1,1280,1024]{2,1,0:T(8,128)}, u32[]{:S(2)}) copy-start(f32[1,1280,1024]{2,1,0:T(8,128)} %param.11) | copy-start | bytes 15728644
  14.0 4.2 %copy-start.6 = (bf16[1,128,1024]{2,1,0:T(8,128)(2,1)S(1)}, bf16[1,128,1024]{2,1,0:T(8,128)(2,1)}, u32[]{:S(2)}) copy-start(bf16[1,128,1024]{2,1,0:T(8,128)(2,1)} %param.9) | copy-start | bytes 786436
  14.0 4.2 %copy-start.7 = (s32[4]{0:T(128)S(1)}, s32[4]{0:T(128)}, u32[]{:S(2)}) copy-start(s32[4]{0:T(128)} %plan_ref.1) | copy-start | bytes 52
  14.3 17.9 %slice-start = ((s8[5242880]{0:T(1024)(128)(4,1)}), s8[4194304]{0:T(1024)(128)(4,1)S(1)}, s32[]{:S(2)}) async-start(s8[5242880]{0:T(1024)(128)(4,1)} %bitcast.14), calls=%async_computation | async-start | bytes 8388608
  14.3 17.9 %slice-start.2 = ((s8[5242880]{0:T(1024)(128)(4,1)}), s8[4194304]{0:T(1024)(128)(4,1)S(1)}, s32[]{:S(2)}) async-start(s8[5242880]{0:T(1024)(128)(4,1)} %bitcast.20), calls=%async_computation.2 | async-start | bytes 8388608
  14.4 17.9 %slice-start.4 = ((s8[5242880]{0:T(1024)(128)(4,1)}), s8[4194304]{0:T(1024)(128)(4,1)S(1)}, s32[]{:S(2)}) async-start(s8[5242880]{0:T(1024)(128)(4,1)} %bitcast.23), calls=%async_computation.4 | async-start | bytes 8388608
  14.4 17.9 %slice-start.1 = ((s8[5242880]{0:T(1024)(128)(4,1)}), s8[1048576]{0:T(1024)(128)(4,1)S(1)}, s32[]{:S(2)}) async-start(s8[5242880]{0:T(1024)(128)(4,1)} %bitcast.14), calls=%async_computation.1 | async-start | bytes 2097152
  14.4 17.9 %slice-start.3 = ((s8[5242880]{0:T(1024)(128)(4,1)}), s8[1048576]{0:T(1024)(128)(4,1)S(1)}, s32[]{:S(2)}) async-start(s8[5242880]{0:T(1024)(128)(4,1)} %bitcast.20), calls=%async_computation.3 | async-start | bytes 2097152
  14.4 17.9 %slice-start.5 = ((s8[5242880]{0:T(1024)(128)(4,1)}), s8[1048576]{0:T(1024)(128)(4,1)S(1)}, s32[]{:S(2)}) async-start(s8[5242880]{0:T(1024)(128)(4,1)} %bitcast.23), calls=%async_computation.5 | async-start | bytes 2097152
  14.4 17.9 %copy-start.5 = (s32[1,4]{1,0:T(1,128)S(1)}, s32[1,4]{1,0:T(1,128)}, u32[]{:S(2)}) copy-start(s32[1,4]{1,0:T(1,128)} %param.14) | copy-start | bytes 52
  14.4 17.8 %collective-permute-start.8 = (bf16[1280,128]{1,0:T(8,128)(2,1)S(1)}, bf16[1280,128]{1,0:T(8,128)(2,1)S(1)}, u32[]{:S(2)}, u32[]{:S(2)}) collective-permute-start(bf16[1280,128]{1,0:T(8,128)(2,1)S(1)} %get-tuple-element.35), channel_id=1, source_target_pairs={{0,3},{1,2},{2,1},{3,0},{4,7},{5,6},{6,5},{7,4},{8,11},{9,10},{10,... | collective-permute-start | bytes 983048 | tf_op jit(solution)/shard_map/ppermute | solution.py:25
  20.3 19.7 %collective-permute-start.3 = (bf16[128,1280]{1,0:T(8,128)(2,1)S(1)}, bf16[128,1280]{1,0:T(8,128)(2,1)S(1)}, u32[]{:S(2)}, u32[]{:S(2)}) collective-permute-start(bf16[128,1280]{1,0:T(8,128)(2,1)S(1)} %get-tuple-element.29), channel_id=1, source_target_pairs={{0,1},{1,0},{2,3},{3,2},{4,5},{5,4},{6,7},{7,6},{8,9},{9,8},{10,11... | collective-permute-start | bytes 983048 | tf_op jit(solution)/shard_map/ppermute | solution.py:25
  21.8 23.5 %collective-permute-start.4 = (bf16[128,1280]{1,0:T(8,128)(2,1)S(1)}, bf16[128,1280]{1,0:T(8,128)(2,1)S(1)}, u32[]{:S(2)}, u32[]{:S(2)}) collective-permute-start(bf16[128,1280]{1,0:T(8,128)(2,1)S(1)} %get-tuple-element.30), channel_id=1, source_target_pairs={{0,2},{1,3},{2,0},{3,1},{4,6},{5,7},{6,4},{7,5},{8,10},{9,11},{10,... | collective-permute-start | bytes 983048 | tf_op jit(solution)/shard_map/ppermute | solution.py:25
  23.7 21.7 %collective-permute-start.5 = (bf16[128,1280]{1,0:T(8,128)(2,1)S(1)}, bf16[128,1280]{1,0:T(8,128)(2,1)S(1)}, u32[]{:S(2)}, u32[]{:S(2)}) collective-permute-start(bf16[128,1280]{1,0:T(8,128)(2,1)S(1)} %get-tuple-element.31), channel_id=1, source_target_pairs={{0,3},{1,2},{2,1},{3,0},{4,7},{5,6},{6,5},{7,4},{8,11},{9,10},{10,... | collective-permute-start | bytes 983048 | tf_op jit(solution)/shard_map/ppermute | solution.py:25
  32.3 13.0 %copy-start.2 = (bf16[1,128,5120]{2,1,0:T(8,128)(2,1)S(1)}, bf16[1,128,5120]{2,1,0:T(8,128)(2,1)}, u32[]{:S(2)}) copy-start(bf16[1,128,5120]{2,1,0:T(8,128)(2,1)} %param.8) | copy-start | bytes 3932164
  32.3 13.0 %copy-start.4 = (f32[1,5120]{1,0:T(1,128)S(1)}, f32[1,5120]{1,0:T(1,128)}, u32[]{:S(2)}) copy-start(f32[1,5120]{1,0:T(1,128)} %gain_ref.5) | copy-start | bytes 61444
  45.9 3.7 %collective-permute-start.9 = (bf16[64,5120]{1,0:T(8,128)(2,1)S(1)}, bf16[64,5120]{1,0:T(8,128)(2,1)S(1)}, u32[]{:S(2)}, u32[]{:S(2)}) collective-permute-start(bf16[64,5120]{1,0:T(8,128)(2,1)S(1)} %own.1.refs_4_), channel_id=1, source_target_pairs={{0,4},{4,0},{8,12},{12,8},{16,20},{20,16},{24,28},{28,24},{1,5},{5... | collective-permute-start | bytes 1966088 | tf_op jit(solution)/shard_map/ppermute | solution.py:25
  46.0 18.5 %collective-permute-start.16 = (bf16[256,1280]{1,0:T(8,128)(2,1)S(1)}, bf16[256,1280]{1,0:T(8,128)(2,1)S(1)}, u32[]{:S(2)}, u32[]{:S(2)}) collective-permute-start(bf16[256,1280]{1,0:T(8,128)(2,1)S(1)} %get-tuple-element.44), channel_id=1, source_target_pairs={{0,3},{1,2},{2,1},{3,0},{4,7},{5,6},{6,5},{7,4},{8,11},{9,10},{10,... | collective-permute-start | bytes 1966088 | tf_op jit(solution)/shard_map/ppermute | solution.py:25
  47.6 30.6 %collective-permute-start.15 = (bf16[256,1280]{1,0:T(8,128)(2,1)S(1)}, bf16[256,1280]{1,0:T(8,128)(2,1)S(1)}, u32[]{:S(2)}, u32[]{:S(2)}) collective-permute-start(bf16[256,1280]{1,0:T(8,128)(2,1)S(1)} %get-tuple-element.43), channel_id=1, source_target_pairs={{0,1},{1,0},{2,3},{3,2},{4,5},{5,4},{6,7},{7,6},{8,9},{9,8},{10,11... | collective-permute-start | bytes 1966088 | tf_op jit(solution)/shard_map/ppermute | solution.py:25
  49.8 2.0 %collective-permute-start.10 = (bf16[32,5120]{1,0:T(8,128)(2,1)S(1)}, bf16[32,5120]{1,0:T(8,128)(2,1)S(1)}, u32[]{:S(2)}, u32[]{:S(2)}) collective-permute-start(bf16[32,5120]{1,0:T(8,128)(2,1)S(1)} %get-tuple-element.38), channel_id=1, source_target_pairs={{24,8},{8,16},{28,12},{12,20},{25,9},{9,17},{29,13},{13,21},{26,10... | collective-permute-start | bytes 983048 | tf_op jit(solution)/shard_map/ppermute | solution.py:423
  50.5 1.3 %collective-permute-start.11 = (bf16[32,5120]{1,0:T(8,128)(2,1)S(1)}, bf16[32,5120]{1,0:T(8,128)(2,1)S(1)}, u32[]{:S(2)}, u32[]{:S(2)}) collective-permute-start(bf16[32,5120]{1,0:T(8,128)(2,1)S(1)} %get-tuple-element.39), channel_id=1, source_target_pairs={{16,8},{24,16},{20,12},{28,20},{17,9},{25,17},{21,13},{29,21},{18,... | collective-permute-start | bytes 983048 | tf_op jit(solution)/shard_map/ppermute | solution.py:424
  51.2 27.9 %collective-permute-start.14 = (bf16[256,1280]{1,0:T(8,128)(2,1)S(1)}, bf16[256,1280]{1,0:T(8,128)(2,1)S(1)}, u32[]{:S(2)}, u32[]{:S(2)}) collective-permute-start(bf16[256,1280]{1,0:T(8,128)(2,1)S(1)} %get-tuple-element.42), channel_id=1, source_target_pairs={{0,2},{1,3},{2,0},{3,1},{4,6},{5,7},{6,4},{7,5},{8,10},{9,11},{10,... | collective-permute-start | bytes 1966088 | tf_op jit(solution)/shard_map/ppermute | solution.py:25
  52.0 28.7 %collective-permute-start.12 = (bf16[32,5120]{1,0:T(8,128)(2,1)S(1)}, bf16[32,5120]{1,0:T(8,128)(2,1)S(1)}, u32[]{:S(2)}, u32[]{:S(2)}) collective-permute-start(bf16[32,5120]{1,0:T(8,128)(2,1)S(1)} %get-tuple-element.40), channel_id=1, source_target_pairs={{8,0},{16,8},{24,16},{12,4},{20,12},{28,20},{9,1},{17,9},{25,17},{... | collective-permute-start | bytes 983048 | tf_op jit(solution)/shard_map/ppermute | solution.py:428
  53.3 35.6 %collective-permute-start.13 = (bf16[32,5120]{1,0:T(8,128)(2,1)S(1)}, bf16[32,5120]{1,0:T(8,128)(2,1)S(1)}, u32[]{:S(2)}, u32[]{:S(2)}) collective-permute-start(bf16[32,5120]{1,0:T(8,128)(2,1)S(1)} %get-tuple-element.41), channel_id=1, source_target_pairs={{16,0},{20,4},{17,1},{21,5},{18,2},{22,6},{19,3},{23,7}} | collective-permute-start | bytes 983048 | tf_op jit(solution)/shard_map/ppermute | solution.py:429
  89.4 2.2 %collective-permute-start.17 = (bf16[64,5120]{1,0:T(8,128)(2,1)S(1)}, bf16[64,5120]{1,0:T(8,128)(2,1)S(1)}, u32[]{:S(2)}, u32[]{:S(2)}) collective-permute-start(bf16[64,5120]{1,0:T(8,128)(2,1)S(1)} %last.1._), channel_id=1, source_target_pairs={{0,4},{4,0},{8,12},{12,8},{16,20},{20,16},{24,28},{28,24},{1,5},{5... | collective-permute-start | bytes 1966088 | tf_op jit(solution)/shard_map/ppermute | solution.py:25

commit v6 on v5

--- a/solution.py
+++ b/solution.py
@@ -172,7 +172,7 @@
 
 
 def spread_body(count, micro, scale, plan_ref, *refs):
-    cots, (low_ref, ordered_ref), outs = refs[:count], refs[count : count + 2], refs[count + 2 :]
+    cots, (low_ref, ordered_ref), outs = refs[:count][::-1], refs[count : count + 2], refs[count + 2 :]
     rows = cots[0].shape[0]
     size = rows // micro
     for k in range(count):
@@ -194,7 +194,7 @@
 
 
 def grad_body(count, head, scale, place_ref, owner_ref, *refs):
-    normed, refs = refs[:count], refs[count:]
+    normed, refs = refs[:count][::-1], refs[count:]
     ordered_ref, master_ref, moment_ref, second_ref, moment_out, second_out = refs[:6]
     outs, mark_ref, joined, fresh = refs[6 : 6 + count], *refs[6 + count :]
     tok_count = normed[0].shape[1]
@@ -228,7 +228,7 @@
 
 
 def own_body(count, mine, place_ref, core_ref, tok_ref, gain_ref, inv_ref, *refs):
-    spread, out_ref = refs[:count], refs[-1]
+    spread, out_ref = refs[:count][::-1], refs[-1]
     place = place_ref[0]
     core = core_ref[0]
     width = tok_ref.shape[1]
@@ -261,7 +261,7 @@
         out_ref[...] = (keep_ref[rows, :].astype(f32) + got_ref[rows, :].astype(f32)).astype(bf16)
 
 
-def middle_body(chip_ref, keep_ref, got_ref, one_ref, two_ref, three_ref, four_ref):
+def middle_body(chip_ref, keep_ref, got_ref, two_ref, one_ref, three_ref, four_ref):
     z = chip_ref[0]
     half = one_ref.shape[0]
     rows = pl.ds(pl.multiple_of(jnp.where(z == 2, half, 0), half), half)
@@ -272,7 +272,7 @@
     four_ref[...] = (mine + one).astype(bf16)
 
 
-def last_body(mine, chip_ref, core_ref, keep_ref, got_ref, one_ref, two_ref, three_ref, four_ref, _, out_ref):
+def last_body(mine, chip_ref, core_ref, keep_ref, got_ref, two_ref, one_ref, four_ref, three_ref, _, out_ref):
     z = chip_ref[0]
     lower = (core_ref[0] == 0) == mine
     half = one_ref.shape[0]
@@ -353,7 +353,7 @@
         [resident] * (count + 1),
         [sds((count * tok_count, kv_cols), bf16)] + [sds((tok_count, cols), bf16)] * count,
         work=10**10,
-    )(plan, *cots, low)
+    )(plan, *cots[::-1], low)
     spread = [spread[0]] + [swap(spread[k], "fsdp", k) for k in dests]
 
     state = pl.BlockSpec((rows_step, kv_cols), lambda i, *_: (i, 0))
@@ -373,7 +373,7 @@
             pltpu.VMEM((rows_step, kv_cols), bf16),
         ],
         vmem=20,
-    )(place, head_owner[0], *normed, ordered, master_rows, moment_rows, second_rows)
+    )(place, head_owner[0], *normed[::-1], ordered, master_rows, moment_rows, second_rows)
 
     rollout = ()
     rollout_mark = ()
@@ -404,7 +404,7 @@
             + [anywhere],
             [whole((half, width))],
             [sds((half, width), bf16)],
-        )(place, core, tok_rows, norm_gain, inverse, *spread, after)
+        )(place, core, tok_rows, norm_gain, inverse, *spread[::-1], after)
         return term
 
     give = own("own", False, grad_mark)
@@ -424,10 +424,10 @@
     two = lax.ppermute(two, "section", chips([(2, 1), (3, 2)]))
     three, four = call(
         "middle", middle_body, (1,), 1, [full, full, part, part], [part, part], [piece, piece]
-    )(chip, keep, got, one, two)
+    )(chip, keep, got, two, one)
     three = lax.ppermute(three, "section", chips([(1, 0), (2, 1), (3, 2)]))
     four = lax.ppermute(four, "section", chips([(2, 0)]))
-    terms = (chip, core, keep, got, one, two, three, four)
+    terms = (chip, core, keep, got, two, one, four, three)
     shapes = [full, full, part, part, part, part, anywhere]
     (send,) = call(
         "last",

time: 92.7 us -> 87.8 us (0.947)
  waiting for transfers between devices: 47.5 us -> 42.6 us
    ppermute x1, waiting for transfers between devices: 8.19 us -> 0.01 us  [shards(): four = lax.ppermute(four, 'section', chips([(2, 0)]))]
    ppermute x1, waiting for transfers between devices: 0.79 us -> 4.34 us  [shards(): three = lax.ppermute(three, 'section', chips([(1, 0), (2, 1), (3, 2)]))]
  transfers between devices with their start and end apart: 18 -> 18, of which waited for: 11 -> 11; matrix products, arithmetic and copies ran while one was open for 0% -> 0% of each run, Pallas kernels for 18% -> 19%
where the time goes in v6:
time: 87.8 us; the launch traced here: 87.5 us
  waiting for transfers between devices  42.6 us (49%)
  starting transfers between devices  21 us (24%)
  Pallas kernels  18.5 us (21%)
  local copies, waits for them, and re-layouts  4.59 us (5%)
  between operations  0.89 us (1%)
    ppermute x14, waiting for transfers between devices, swap(): return lax.ppermute(x, axis, [(i, i ^ k) for i in range(count)])  38.2 us
    ppermute x14, starting transfers between devices, swap(): return lax.ppermute(x, axis, [(i, i ^ k) for i in range(count)])  17 us
    pallas_call x1, Pallas kernels, shards(): call('grad', functools.partial(grad_body, count, head, scale), (cols // r...  7.59 us
    unnamed x28, local copies, waits for them, and re-layouts  4.59 us
    ppermute x1, waiting for transfers between devices, shards(): three = lax.ppermute(three, 'section', chips([(1, 0), (2, 1), (3, 2)]))  4.34 us
    pallas_call x4, Pallas kernels, shards(): call('place', marked_body if final else place_body, (1,), 1, [whole((2 *...  3.52 us
    pallas_call x1, Pallas kernels, shards(): call('spread', functools.partial(spread_body, count, plan.shape[0], scale...  2.1 us
  transfers between devices with their start and end apart: 18, of which 11 were waited for; matrix products, arithmetic and copies ran while one was open for 0% of the time, Pallas kernels for 19%

profile of v6, /device:TPU:0, one launch (start us, length us, event | category | flops | bytes accessed | tf_op | source)
XLA Modules:
  0.0 87.5 jit_solution(13336221667671833195)
XLA Ops:
  0.6 4.0 %collective-permute-start = (bf16[128,1024]{1,0:T(8,128)(2,1)}, bf16[128,1024]{1,0:T(8,128)(2,1)S(1)}, u32[]{:S(2)}, u32[]{:S(2)}) collective-permute-start(bf16[128,1024]{1,0:T(8,128)(2,1)} %bitcast.27), channel_id=1, source_target_pairs={{0,3},{1,2},{2,1},{3,0},{4,7},{5,6},{6,5},{7,4},{8,11},{9,10},{10,... | collective-permute-start | bytes 786440 | tf_op jit(solution)/shard_map/ppermute | solution.py:25
  4.6 0.5 collective-permute-start.1
  5.1 0.1 collective-permute-start.2
  5.2 1.3 %copy-done.1 = bf16[1,128,5120]{2,1,0:T(8,128)(2,1)S(1)} copy-done((bf16[1,128,5120]{2,1,0:T(8,128)(2,1)S(1)}, bf16[1,128,5120]{2,1,0:T(8,128)(2,1)}, u32[]{:S(2)}) %copy-start.1) | copy-done | bytes 1310744
  6.6 0.7 copy-done.3
  7.3 0.7 prep.1
  8.0 2.9 %collective-permute-start.6 = (bf16[1280,128]{1,0:T(8,128)(2,1)S(1)}, bf16[1280,128]{1,0:T(8,128)(2,1)S(1)}, u32[]{:S(2)}, u32[]{:S(2)}) collective-permute-start(bf16[1280,128]{1,0:T(8,128)(2,1)S(1)} %get-tuple-element.32), channel_id=1, source_target_pairs={{0,3},{1,2},{2,1},{3,0},{4,7},{5,6},{6,5},{7,4},{8,11},{9,10},{10,... | collective-permute-start | bytes 983048 | tf_op jit(solution)/shard_map/ppermute | solution.py:25
  10.9 0.5 collective-permute-start.7
  11.5 2.5 %copy-done = f32[1,1280,1024]{2,1,0:T(8,128)S(1)} copy-done((f32[1,1280,1024]{2,1,0:T(8,128)S(1)}, f32[1,1280,1024]{2,1,0:T(8,128)}, u32[]{:S(2)}) %copy-start) | copy-done | bytes 5242904
  13.9 0.3 low.1.refs_4_
  14.3 0.0 collective-permute-done.refs_0_
  14.3 0.0 slice-start
  14.3 0.0 slice-start.2
  14.3 0.0 slice-start.4
  14.3 0.0 slice-start.1
  14.3 0.0 slice-start.3
  14.3 0.0 slice-start.5
  14.4 0.0 copy-start.5
  14.4 0.2 collective-permute-start.8
  14.6 3.1 %collective-permute-done.1.refs_1_ = bf16[128,1024]{1,0:T(8,128)(2,1)S(1)} collective-permute-done((bf16[128,1024]{1,0:T(8,128)(2,1)}, bf16[128,1024]{1,0:T(8,128)(2,1)S(1)}, u32[]{:S(2)}, u32[]{:S(2)}) %collective-permute-start.1) | collective-permute-done | bytes 262176 | tf_op jit(solution)/shard_map/ppermute | solution.py:25
  17.7 0.5 collective-permute-done.2.refs_2_
  18.2 2.1 %spread.1 = (bf16[512,1024]{1,0:T(8,128)(2,1)S(1)}, bf16[128,1280]{1,0:T(8,128)(2,1)S(1)}, bf16[128,1280]{1,0:T(8,128)(2,1)S(1)}, bf16[128,1280]{1,0:T(8,128)(2,1)S(1)}, bf16[128,1280]{1,0:T(8,128)(2,1)S(1)}) custom-call(s32[4]{0:T(128)S(1)} %copy-done.7, bf16[128,1024]{1,0:T(8,128)(2,1)S(1)} %collective-permute-done.refs_0_, ...), custom_call_target="tpu_custom_call" | custom-call | flops 10000000000 | bytes 1 | tf_op jit(solution)/shard_map/spread/pallas_call | solution.py:347
  20.3 2.5 %collective-permute-start.3 = (bf16[128,1280]{1,0:T(8,128)(2,1)S(1)}, bf16[128,1280]{1,0:T(8,128)(2,1)S(1)}, u32[]{:S(2)}, u32[]{:S(2)}) collective-permute-start(bf16[128,1280]{1,0:T(8,128)(2,1)S(1)} %get-tuple-element.28), channel_id=1, source_target_pairs={{0,3},{1,2},{2,1},{3,0},{4,7},{5,6},{6,5},{7,4},{8,11},{9,10},{10,... | collective-permute-start | bytes 983048 | tf_op jit(solution)/shard_map/ppermute | solution.py:25
  22.8 0.5 collective-permute-start.4
  23.3 1.4 %collective-permute-done.6.refs_0_ = bf16[1280,128]{1,0:T(8,128)(2,1)S(1)} collective-permute-done((bf16[1280,128]{1,0:T(8,128)(2,1)S(1)}, bf16[1280,128]{1,0:T(8,128)(2,1)S(1)}, u32[]{:S(2)}, u32[]{:S(2)}) %collective-permute-start.6) | collective-permute-done | bytes 327712 | tf_op jit(solution)/shard_map/ppermute | solution.py:25
  24.7 2.0 %collective-permute-start.5 = (bf16[128,1280]{1,0:T(8,128)(2,1)S(1)}, bf16[128,1280]{1,0:T(8,128)(2,1)S(1)}, u32[]{:S(2)}, u32[]{:S(2)}) collective-permute-start(bf16[128,1280]{1,0:T(8,128)(2,1)S(1)} %get-tuple-element.30), channel_id=1, source_target_pairs={{0,1},{1,0},{2,3},{3,2},{4,5},{5,4},{6,7},{7,6},{8,9},{9,8},{10,11... | collective-permute-start | bytes 983048 | tf_op jit(solution)/shard_map/ppermute | solution.py:25
  26.7 5.0 %collective-permute-done.7.refs_1_ = bf16[1280,128]{1,0:T(8,128)(2,1)S(1)} collective-permute-done((bf16[1280,128]{1,0:T(8,128)(2,1)S(1)}, bf16[1280,128]{1,0:T(8,128)(2,1)S(1)}, u32[]{:S(2)}, u32[]{:S(2)}) %collective-permute-start.7) | collective-permute-done | bytes 327712 | tf_op jit(solution)/shard_map/ppermute | solution.py:25
  31.7 0.5 collective-permute-done.8.refs_2_
  32.3 0.0 slice-done.4
  32.3 0.0 copy-start.2
  32.3 0.0 copy-start.4
  32.4 7.6 %grad.1 = (f32[1280,1024]{1,0:T(8,128)}, f32[1280,1024]{1,0:T(8,128)}, bf16[256,1280]{1,0:T(8,128)(2,1)S(1)}, bf16[256,1280]{1,0:T(8,128)(2,1)S(1)}, bf16[256,12...) custom-call(s32[1]{0:T(128)} %bitcast.2.place_ref, s32[4]{0:T(128)S(1)} %bitcast.26, ...), custom_call_target="tpu_custom_call" | custom-call | flops 1 | bytes 1 | tf_op jit(solution)/shard_map/grad/pallas_call | solution.py:360
  39.9 0.0 collective-permute-done.3.refs_0_
  39.9 4.9 %collective-permute-done.4.refs_1_ = bf16[128,1280]{1,0:T(8,128)(2,1)S(1)} collective-permute-done((bf16[128,1280]{1,0:T(8,128)(2,1)S(1)}, bf16[128,1280]{1,0:T(8,128)(2,1)S(1)}, u32[]{:S(2)}, u32[]{:S(2)}) %collective-permute-start.4) | collective-permute-done | bytes 327712 | tf_op jit(solution)/shard_map/ppermute | solution.py:25
  44.8 0.4 collective-permute-done.5.refs_2_
  45.2 0.6 own.1.refs_4_
  45.8 0.1 collective-permute-start.9
  45.9 1.5 %collective-permute-start.16 = (bf16[256,1280]{1,0:T(8,128)(2,1)S(1)}, bf16[256,1280]{1,0:T(8,128)(2,1)S(1)}, u32[]{:S(2)}, u32[]{:S(2)}) collective-permute-start(bf16[256,1280]{1,0:T(8,128)(2,1)S(1)} %get-tuple-element.44), channel_id=1, source_target_pairs={{0,3},{1,2},{2,1},{3,0},{4,7},{5,6},{6,5},{7,4},{8,11},{9,10},{10,... | collective-permute-start | bytes 1966088 | tf_op jit(solution)/shard_map/ppermute | solution.py:25
  47.4 1.3 %collective-permute-start.15 = (bf16[256,1280]{1,0:T(8,128)(2,1)S(1)}, bf16[256,1280]{1,0:T(8,128)(2,1)S(1)}, u32[]{:S(2)}, u32[]{:S(2)}) collective-permute-start(bf16[256,1280]{1,0:T(8,128)(2,1)S(1)} %get-tuple-element.43), channel_id=1, source_target_pairs={{0,1},{1,0},{2,3},{3,2},{4,5},{5,4},{6,7},{7,6},{8,9},{9,8},{10,11... | collective-permute-start | bytes 1966088 | tf_op jit(solution)/shard_map/ppermute | solution.py:25
  48.7 0.6 keep.1.keep_ref
  49.3 0.0 collective-permute-done.9.got_ref
  49.3 0.2 pair.1
  49.5 0.7 collective-permute-start.10
  50.2 0.7 collective-permute-start.11
  50.9 0.7 collective-permute-start.14
  51.6 0.0 collective-permute-done.10.two_ref
  51.6 0.0 collective-permute-done.11.one_ref
  51.6 0.2 middle.1
  51.9 1.3 %collective-permute-start.12 = (bf16[32,5120]{1,0:T(8,128)(2,1)S(1)}, bf16[32,5120]{1,0:T(8,128)(2,1)S(1)}, u32[]{:S(2)}, u32[]{:S(2)}) collective-permute-start(bf16[32,5120]{1,0:T(8,128)(2,1)S(1)} %get-tuple-element.40), channel_id=1, source_target_pairs={{16,0},{20,4},{17,1},{21,5},{18,2},{22,6},{19,3},{23,7}} | collective-permute-start | bytes 983048 | tf_op jit(solution)/shard_map/ppermute | solution.py:429
  53.2 1.3 %collective-permute-start.13 = (bf16[32,5120]{1,0:T(8,128)(2,1)S(1)}, bf16[32,5120]{1,0:T(8,128)(2,1)S(1)}, u32[]{:S(2)}, u32[]{:S(2)}) collective-permute-start(bf16[32,5120]{1,0:T(8,128)(2,1)S(1)} %get-tuple-element.41), channel_id=1, source_target_pairs={{8,0},{16,8},{24,16},{12,4},{20,12},{28,20},{9,1},{17,9},{25,17},{... | collective-permute-start | bytes 983048 | tf_op jit(solution)/shard_map/ppermute | solution.py:428
  54.5 0.9 %place.4.refs_0_ = bf16[256,5120]{1,0:T(8,128)(2,1)} custom-call(s32[1]{0:T(128)} %bitcast.2.place_ref, bf16[256,1280]{1,0:T(8,128)(2,1)S(1)} %get-tuple-element.45.part_ref), custom_call_target="tpu_custom_call" | custom-call | flops 1 | bytes 1 | tf_op jit(solution)/shard_map/place/pallas_call | solution.py:383
  55.4 9.0 %collective-permute-done.16.part_ref = bf16[256,1280]{1,0:T(8,128)(2,1)S(1)} collective-permute-done((bf16[256,1280]{1,0:T(8,128)(2,1)S(1)}, bf16[256,1280]{1,0:T(8,128)(2,1)S(1)}, u32[]{:S(2)}, u32[]{:S(2)}) %collective-permute-start.16) | collective-permute-done | bytes 655392 | tf_op jit(solution)/shard_map/ppermute | solution.py:25
  64.4 0.9 %place.5.refs_0_ = bf16[256,5120]{1,0:T(8,128)(2,1)} custom-call(s32[1]{0:T(128)} %bitcast.2.place_ref, bf16[256,1280]{1,0:T(8,128)(2,1)S(1)} %collective-permute-done.16.part_ref, bf16[256,5120]{1,0:T(8,128)(2,1)} %place.4.refs_0_), custom_call_target="tpu_custom_call", output_to_operand_aliasing={{}: (2, {})} | custom-call | flops 1 | bytes 1 | tf_op jit(solution)/shard_map/place/pallas_call | solution.py:383
  65.3 12.6 %collective-permute-done.15.part_ref = bf16[256,1280]{1,0:T(8,128)(2,1)S(1)} collective-permute-done((bf16[256,1280]{1,0:T(8,128)(2,1)S(1)}, bf16[256,1280]{1,0:T(8,128)(2,1)S(1)}, u32[]{:S(2)}, u32[]{:S(2)}) %collective-permute-start.15) | collective-permute-done | bytes 655392 | tf_op jit(solution)/shard_map/ppermute | solution.py:25
  77.9 0.9 %place.6._ = bf16[256,5120]{1,0:T(8,128)(2,1)} custom-call(s32[1]{0:T(128)} %bitcast.2.place_ref, bf16[256,1280]{1,0:T(8,128)(2,1)S(1)} %collective-permute-done.15.part_ref, bf16[256,5120]{1,0:T(8,128)(2,1)} %place.5.refs_0_), custom_call_target="tpu_custom_call", output_to_operand_aliasing={{}: (2, {})} | custom-call | flops 1 | bytes 1 | tf_op jit(solution)/shard_map/place/pallas_call | solution.py:383
  78.8 0.0 collective-permute-done.14.part_ref
  78.8 0.9 %place.7 = (bf16[256,5120]{1,0:T(8,128)(2,1)}, f32[8,128]{1,0:T(8,128)S(1)}) custom-call(s32[1]{0:T(128)} %bitcast.2.place_ref, bf16[256,1280]{1,0:T(8,128)(2,1)S(1)} %collective-permute-done.14.part_ref, bf16[256,5120]{1,0:T(8,128)(2,1)} %place.6._), custom_call_target="tpu_custom_call", output_to_operand_aliasing={{0}: (2, {})} | custom-call | flops 1 | bytes 1 | tf_op jit(solution)/shard_map/place/pallas_call | solution.py:383
  79.6 0.0 collective-permute-done.12.four_ref
  79.6 4.3 %collective-permute-done.13.three_ref = bf16[32,5120]{1,0:T(8,128)(2,1)S(1)} collective-permute-done((bf16[32,5120]{1,0:T(8,128)(2,1)S(1)}, bf16[32,5120]{1,0:T(8,128)(2,1)S(1)}, u32[]{:S(2)}, u32[]{:S(2)}) %collective-permute-start.13) | collective-permute-done | bytes 327712 | tf_op jit(solution)/shard_map/ppermute | solution.py:428
  84.0 0.5 last.1._
  84.5 0.1 collective-permute-start.17
  84.5 1.3 %mine.1.refs_0_ = bf16[128,5120]{1,0:T(8,128)(2,1)} custom-call(s32[1]{0:T(128)} %bitcast.1.chip_ref, s32[1]{0:T(128)} %bitcast.core_ref.place_ref, bf16[64,5120]{1,0:T(8,128)(2,1)S(1)} %keep.1.keep_ref, bf16[64,5120]{1,0:T(8,128)(2,1)S(1)} %collective-permute-done.9.got_ref, bf16[32,5120]{1,0:T(8,128)(2,1)S(1)} %collective-permute-done.10.two_ref, ...), custom_call_target="tpu_custom_call" | custom-call | flops 1 | bytes 1 | tf_op jit(solution)/shard_map/mine/pallas_call | solution.py:442
  85.8 0.8 collective-permute-done.17.part_ref
  86.6 0.9 %join.1 = bf16[128,5120]{1,0:T(8,128)(2,1)} custom-call(s32[1]{0:T(128)} %bitcast.core_ref.place_ref, bf16[64,5120]{1,0:T(8,128)(2,1)S(1)} %collective-permute-done.17.part_ref, bf16[128,5120]{1,0:T(8,128)(2,1)} %mine.1.refs_0_), custom_call_target="tpu_custom_call", output_to_operand_aliasing={{}: (2, {})} | custom-call | flops 1 | bytes 1 | tf_op jit(solution)/shard_map/join/pallas_call | solution.py:451
  (18 shorter events, 0.0 us)
Async XLA Ops:
  0.6 13.6 %collective-permute-start = (bf16[128,1024]{1,0:T(8,128)(2,1)}, bf16[128,1024]{1,0:T(8,128)(2,1)S(1)}, u32[]{:S(2)}, u32[]{:S(2)}) collective-permute-start(bf16[128,1024]{1,0:T(8,128)(2,1)} %bitcast.27), channel_id=1, source_target_pairs={{0,3},{1,2},{2,1},{3,0},{4,7},{5,6},{6,5},{7,4},{8,11},{9,10},{10,... | collective-permute-start | bytes 786440 | tf_op jit(solution)/shard_map/ppermute | solution.py:25
  4.6 13.1 %collective-permute-start.1 = (bf16[128,1024]{1,0:T(8,128)(2,1)}, bf16[128,1024]{1,0:T(8,128)(2,1)S(1)}, u32[]{:S(2)}, u32[]{:S(2)}) collective-permute-start(bf16[128,1024]{1,0:T(8,128)(2,1)} %bitcast.28), channel_id=1, source_target_pairs={{0,2},{1,3},{2,0},{3,1},{4,6},{5,7},{6,4},{7,5},{8,10},{9,11},{10,... | collective-permute-start | bytes 786440 | tf_op jit(solution)/shard_map/ppermute | solution.py:25
  5.1 13.1 %collective-permute-start.2 = (bf16[128,1024]{1,0:T(8,128)(2,1)}, bf16[128,1024]{1,0:T(8,128)(2,1)S(1)}, u32[]{:S(2)}, u32[]{:S(2)}) collective-permute-start(bf16[128,1024]{1,0:T(8,128)(2,1)} %bitcast.29), channel_id=1, source_target_pairs={{0,1},{1,0},{2,3},{3,2},{4,5},{5,4},{6,7},{7,6},{8,9},{9,8},{10,11... | collective-permute-start | bytes 786440 | tf_op jit(solution)/shard_map/ppermute | solution.py:25
  5.2 1.3 %copy-start.1 = (bf16[1,128,5120]{2,1,0:T(8,128)(2,1)S(1)}, bf16[1,128,5120]{2,1,0:T(8,128)(2,1)}, u32[]{:S(2)}) copy-start(bf16[1,128,5120]{2,1,0:T(8,128)(2,1)} %param.8) | copy-start | bytes 3932164
  6.6 0.7 copy-start.3
  8.0 16.6 %collective-permute-start.6 = (bf16[1280,128]{1,0:T(8,128)(2,1)S(1)}, bf16[1280,128]{1,0:T(8,128)(2,1)S(1)}, u32[]{:S(2)}, u32[]{:S(2)}) collective-permute-start(bf16[1280,128]{1,0:T(8,128)(2,1)S(1)} %get-tuple-element.32), channel_id=1, source_target_pairs={{0,3},{1,2},{2,1},{3,0},{4,7},{5,6},{6,5},{7,4},{8,11},{9,10},{10,... | collective-permute-start | bytes 983048 | tf_op jit(solution)/shard_map/ppermute | solution.py:25
  10.9 20.8 %collective-permute-start.7 = (bf16[1280,128]{1,0:T(8,128)(2,1)S(1)}, bf16[1280,128]{1,0:T(8,128)(2,1)S(1)}, u32[]{:S(2)}, u32[]{:S(2)}) collective-permute-start(bf16[1280,128]{1,0:T(8,128)(2,1)S(1)} %get-tuple-element.33), channel_id=1, source_target_pairs={{0,2},{1,3},{2,0},{3,1},{4,6},{5,7},{6,4},{7,5},{8,10},{9,11},{10,... | collective-permute-start | bytes 983048 | tf_op jit(solution)/shard_map/ppermute | solution.py:25
  11.5 2.5 %copy-start = (f32[1,1280,1024]{2,1,0:T(8,128)S(1)}, f32[1,1280,1024]{2,1,0:T(8,128)}, u32[]{:S(2)}) copy-start(f32[1,1280,1024]{2,1,0:T(8,128)} %param.11) | copy-start | bytes 15728644
  13.9 4.2 %copy-start.6 = (bf16[1,128,1024]{2,1,0:T(8,128)(2,1)S(1)}, bf16[1,128,1024]{2,1,0:T(8,128)(2,1)}, u32[]{:S(2)}) copy-start(bf16[1,128,1024]{2,1,0:T(8,128)(2,1)} %param.9) | copy-start | bytes 786436
  13.9 4.2 %copy-start.7 = (s32[4]{0:T(128)S(1)}, s32[4]{0:T(128)}, u32[]{:S(2)}) copy-start(s32[4]{0:T(128)} %plan_ref.1) | copy-start | bytes 52
  14.3 18.0 %slice-start = ((s8[5242880]{0:T(1024)(128)(4,1)}), s8[4194304]{0:T(1024)(128)(4,1)S(1)}, s32[]{:S(2)}) async-start(s8[5242880]{0:T(1024)(128)(4,1)} %bitcast.14), calls=%async_computation | async-start | bytes 8388608
  14.3 18.0 %slice-start.2 = ((s8[5242880]{0:T(1024)(128)(4,1)}), s8[4194304]{0:T(1024)(128)(4,1)S(1)}, s32[]{:S(2)}) async-start(s8[5242880]{0:T(1024)(128)(4,1)} %bitcast.20), calls=%async_computation.2 | async-start | bytes 8388608
  14.3 17.9 %slice-start.4 = ((s8[5242880]{0:T(1024)(128)(4,1)}), s8[4194304]{0:T(1024)(128)(4,1)S(1)}, s32[]{:S(2)}) async-start(s8[5242880]{0:T(1024)(128)(4,1)} %bitcast.23), calls=%async_computation.4 | async-start | bytes 8388608
  14.3 17.9 %slice-start.1 = ((s8[5242880]{0:T(1024)(128)(4,1)}), s8[1048576]{0:T(1024)(128)(4,1)S(1)}, s32[]{:S(2)}) async-start(s8[5242880]{0:T(1024)(128)(4,1)} %bitcast.14), calls=%async_computation.1 | async-start | bytes 2097152
  14.3 17.9 %slice-start.3 = ((s8[5242880]{0:T(1024)(128)(4,1)}), s8[1048576]{0:T(1024)(128)(4,1)S(1)}, s32[]{:S(2)}) async-start(s8[5242880]{0:T(1024)(128)(4,1)} %bitcast.20), calls=%async_computation.3 | async-start | bytes 2097152
  14.3 17.9 %slice-start.5 = ((s8[5242880]{0:T(1024)(128)(4,1)}), s8[1048576]{0:T(1024)(128)(4,1)S(1)}, s32[]{:S(2)}) async-start(s8[5242880]{0:T(1024)(128)(4,1)} %bitcast.23), calls=%async_computation.5 | async-start | bytes 2097152
  14.4 17.9 %copy-start.5 = (s32[1,4]{1,0:T(1,128)S(1)}, s32[1,4]{1,0:T(1,128)}, u32[]{:S(2)}) copy-start(s32[1,4]{1,0:T(1,128)} %param.14) | copy-start | bytes 52
  14.4 17.9 %collective-permute-start.8 = (bf16[1280,128]{1,0:T(8,128)(2,1)S(1)}, bf16[1280,128]{1,0:T(8,128)(2,1)S(1)}, u32[]{:S(2)}, u32[]{:S(2)}) collective-permute-start(bf16[1280,128]{1,0:T(8,128)(2,1)S(1)} %get-tuple-element.34), channel_id=1, source_target_pairs={{0,1},{1,0},{2,3},{3,2},{4,5},{5,4},{6,7},{7,6},{8,9},{9,8},{10,11... | collective-permute-start | bytes 983048 | tf_op jit(solution)/shard_map/ppermute | solution.py:25
  20.3 19.7 %collective-permute-start.3 = (bf16[128,1280]{1,0:T(8,128)(2,1)S(1)}, bf16[128,1280]{1,0:T(8,128)(2,1)S(1)}, u32[]{:S(2)}, u32[]{:S(2)}) collective-permute-start(bf16[128,1280]{1,0:T(8,128)(2,1)S(1)} %get-tuple-element.28), channel_id=1, source_target_pairs={{0,3},{1,2},{2,1},{3,0},{4,7},{5,6},{6,5},{7,4},{8,11},{9,10},{10,... | collective-permute-start | bytes 983048 | tf_op jit(solution)/shard_map/ppermute | solution.py:25
  22.8 22.0 %collective-permute-start.4 = (bf16[128,1280]{1,0:T(8,128)(2,1)S(1)}, bf16[128,1280]{1,0:T(8,128)(2,1)S(1)}, u32[]{:S(2)}, u32[]{:S(2)}) collective-permute-start(bf16[128,1280]{1,0:T(8,128)(2,1)S(1)} %get-tuple-element.29), channel_id=1, source_target_pairs={{0,2},{1,3},{2,0},{3,1},{4,6},{5,7},{6,4},{7,5},{8,10},{9,11},{10,... | collective-permute-start | bytes 983048 | tf_op jit(solution)/shard_map/ppermute | solution.py:25
  24.7 20.5 %collective-permute-start.5 = (bf16[128,1280]{1,0:T(8,128)(2,1)S(1)}, bf16[128,1280]{1,0:T(8,128)(2,1)S(1)}, u32[]{:S(2)}, u32[]{:S(2)}) collective-permute-start(bf16[128,1280]{1,0:T(8,128)(2,1)S(1)} %get-tuple-element.30), channel_id=1, source_target_pairs={{0,1},{1,0},{2,3},{3,2},{4,5},{5,4},{6,7},{7,6},{8,9},{9,8},{10,11... | collective-permute-start | bytes 983048 | tf_op jit(solution)/shard_map/ppermute | solution.py:25
  32.3 12.9 %copy-start.2 = (bf16[1,128,5120]{2,1,0:T(8,128)(2,1)S(1)}, bf16[1,128,5120]{2,1,0:T(8,128)(2,1)}, u32[]{:S(2)}) copy-start(bf16[1,128,5120]{2,1,0:T(8,128)(2,1)} %param.8) | copy-start | bytes 3932164
  32.3 12.9 %copy-start.4 = (f32[1,5120]{1,0:T(1,128)S(1)}, f32[1,5120]{1,0:T(1,128)}, u32[]{:S(2)}) copy-start(f32[1,5120]{1,0:T(1,128)} %gain_ref.5) | copy-start | bytes 61444
  45.8 3.5 %collective-permute-start.9 = (bf16[64,5120]{1,0:T(8,128)(2,1)S(1)}, bf16[64,5120]{1,0:T(8,128)(2,1)S(1)}, u32[]{:S(2)}, u32[]{:S(2)}) collective-permute-start(bf16[64,5120]{1,0:T(8,128)(2,1)S(1)} %own.1.refs_4_), channel_id=1, source_target_pairs={{0,4},{4,0},{8,12},{12,8},{16,20},{20,16},{24,28},{28,24},{1,5},{5... | collective-permute-start | bytes 1966088 | tf_op jit(solution)/shard_map/ppermute | solution.py:25
  45.9 18.5 %collective-permute-start.16 = (bf16[256,1280]{1,0:T(8,128)(2,1)S(1)}, bf16[256,1280]{1,0:T(8,128)(2,1)S(1)}, u32[]{:S(2)}, u32[]{:S(2)}) collective-permute-start(bf16[256,1280]{1,0:T(8,128)(2,1)S(1)} %get-tuple-element.44), channel_id=1, source_target_pairs={{0,3},{1,2},{2,1},{3,0},{4,7},{5,6},{6,5},{7,4},{8,11},{9,10},{10,... | collective-permute-start | bytes 1966088 | tf_op jit(solution)/shard_map/ppermute | solution.py:25
  47.4 30.5 %collective-permute-start.15 = (bf16[256,1280]{1,0:T(8,128)(2,1)S(1)}, bf16[256,1280]{1,0:T(8,128)(2,1)S(1)}, u32[]{:S(2)}, u32[]{:S(2)}) collective-permute-start(bf16[256,1280]{1,0:T(8,128)(2,1)S(1)} %get-tuple-element.43), channel_id=1, source_target_pairs={{0,1},{1,0},{2,3},{3,2},{4,5},{5,4},{6,7},{7,6},{8,9},{9,8},{10,11... | collective-permute-start | bytes 1966088 | tf_op jit(solution)/shard_map/ppermute | solution.py:25
  49.5 2.1 %collective-permute-start.10 = (bf16[32,5120]{1,0:T(8,128)(2,1)S(1)}, bf16[32,5120]{1,0:T(8,128)(2,1)S(1)}, u32[]{:S(2)}, u32[]{:S(2)}) collective-permute-start(bf16[32,5120]{1,0:T(8,128)(2,1)S(1)} %get-tuple-element.38), channel_id=1, source_target_pairs={{16,8},{24,16},{20,12},{28,20},{17,9},{25,17},{21,13},{29,21},{18,... | collective-permute-start | bytes 983048 | tf_op jit(solution)/shard_map/ppermute | solution.py:424
  50.2 1.4 %collective-permute-start.11 = (bf16[32,5120]{1,0:T(8,128)(2,1)S(1)}, bf16[32,5120]{1,0:T(8,128)(2,1)S(1)}, u32[]{:S(2)}, u32[]{:S(2)}) collective-permute-start(bf16[32,5120]{1,0:T(8,128)(2,1)S(1)} %get-tuple-element.39), channel_id=1, source_target_pairs={{24,8},{8,16},{28,12},{12,20},{25,9},{9,17},{29,13},{13,21},{26,10... | collective-permute-start | bytes 983048 | tf_op jit(solution)/shard_map/ppermute | solution.py:423
  50.9 27.9 %collective-permute-start.14 = (bf16[256,1280]{1,0:T(8,128)(2,1)S(1)}, bf16[256,1280]{1,0:T(8,128)(2,1)S(1)}, u32[]{:S(2)}, u32[]{:S(2)}) collective-permute-start(bf16[256,1280]{1,0:T(8,128)(2,1)S(1)} %get-tuple-element.42), channel_id=1, source_target_pairs={{0,2},{1,3},{2,0},{3,1},{4,6},{5,7},{6,4},{7,5},{8,10},{9,11},{10,... | collective-permute-start | bytes 1966088 | tf_op jit(solution)/shard_map/ppermute | solution.py:25
  51.9 27.8 %collective-permute-start.12 = (bf16[32,5120]{1,0:T(8,128)(2,1)S(1)}, bf16[32,5120]{1,0:T(8,128)(2,1)S(1)}, u32[]{:S(2)}, u32[]{:S(2)}) collective-permute-start(bf16[32,5120]{1,0:T(8,128)(2,1)S(1)} %get-tuple-element.40), channel_id=1, source_target_pairs={{16,0},{20,4},{17,1},{21,5},{18,2},{22,6},{19,3},{23,7}} | collective-permute-start | bytes 983048 | tf_op jit(solution)/shard_map/ppermute | solution.py:429
  53.2 30.8 %collective-permute-start.13 = (bf16[32,5120]{1,0:T(8,128)(2,1)S(1)}, bf16[32,5120]{1,0:T(8,128)(2,1)S(1)}, u32[]{:S(2)}, u32[]{:S(2)}) collective-permute-start(bf16[32,5120]{1,0:T(8,128)(2,1)S(1)} %get-tuple-element.41), channel_id=1, source_target_pairs={{8,0},{16,8},{24,16},{12,4},{20,12},{28,20},{9,1},{17,9},{25,17},{... | collective-permute-start | bytes 983048 | tf_op jit(solution)/shard_map/ppermute | solution.py:428
  84.5 2.2 %collective-permute-start.17 = (bf16[64,5120]{1,0:T(8,128)(2,1)S(1)}, bf16[64,5120]{1,0:T(8,128)(2,1)S(1)}, u32[]{:S(2)}, u32[]{:S(2)}) collective-permute-start(bf16[64,5120]{1,0:T(8,128)(2,1)S(1)} %last.1._), channel_id=1, source_target_pairs={{0,4},{4,0},{8,12},{12,8},{16,20},{20,16},{24,28},{28,24},{1,5},{5... | collective-permute-start | bytes 1966088 | tf_op jit(solution)/shard_map/ppermute | solution.py:25

commit v7 on v6

--- a/solution.py
+++ b/solution.py
@@ -172,7 +172,7 @@
 
 
 def spread_body(count, micro, scale, plan_ref, *refs):
-    cots, (low_ref, ordered_ref), outs = refs[:count][::-1], refs[count : count + 2], refs[count + 2 :]
+    cots, (low_ref, ordered_ref), outs = refs[:count], refs[count : count + 2], refs[count + 2 :]
     rows = cots[0].shape[0]
     size = rows // micro
     for k in range(count):
@@ -194,7 +194,7 @@
 
 
 def grad_body(count, head, scale, place_ref, owner_ref, *refs):
-    normed, refs = refs[:count][::-1], refs[count:]
+    normed, refs = refs[:count], refs[count:]
     ordered_ref, master_ref, moment_ref, second_ref, moment_out, second_out = refs[:6]
     outs, mark_ref, joined, fresh = refs[6 : 6 + count], *refs[6 + count :]
     tok_count = normed[0].shape[1]
@@ -353,7 +353,7 @@
         [resident] * (count + 1),
         [sds((count * tok_count, kv_cols), bf16)] + [sds((tok_count, cols), bf16)] * count,
         work=10**10,
-    )(plan, *cots[::-1], low)
+    )(plan, *cots, low)
     spread = [spread[0]] + [swap(spread[k], "fsdp", k) for k in dests]
 
     state = pl.BlockSpec((rows_step, kv_cols), lambda i, *_: (i, 0))
@@ -373,7 +373,7 @@
             pltpu.VMEM((rows_step, kv_cols), bf16),
         ],
         vmem=20,
-    )(place, head_owner[0], *normed[::-1], ordered, master_rows, moment_rows, second_rows)
+    )(place, head_owner[0], *normed, ordered, master_rows, moment_rows, second_rows)
 
     rollout = ()
     rollout_mark = ()

time: 87.8 us -> 90.1 us (1.026)
  waiting for transfers between devices: 42.6 us -> 44.6 us
    ppermute x14, waiting for transfers between devices: 38.2 us -> 40.3 us  [swap(): return lax.ppermute(x, axis, [(i, i ^ k) for i in range(count)])]
  transfers between devices with their start and end apart: 18 -> 18, of which waited for: 11 -> 8; matrix products, arithmetic and copies ran while one was open for 0% -> 0% of each run, Pallas kernels for 19% -> 18%
where the time goes in v7:
time: 90.1 us; the launch traced here: 89.8 us
  waiting for transfers between devices  44.6 us (50%)
  starting transfers between devices  21.2 us (24%)
  Pallas kernels  18.5 us (21%)
  local copies, waits for them, and re-layouts  4.59 us (5%)
  between operations  0.94 us (1%)
    ppermute x14, waiting for transfers between devices, swap(): return lax.ppermute(x, axis, [(i, i ^ k) for i in range(count)])  40.3 us
    ppermute x14, starting transfers between devices, swap(): return lax.ppermute(x, axis, [(i, i ^ k) for i in range(count)])  17.3 us
    pallas_call x1, Pallas kernels, shards(): call('grad', functools.partial(grad_body, count, head, scale), (cols // r...  7.59 us
    unnamed x28, local copies, waits for them, and re-layouts  4.59 us
    ppermute x1, waiting for transfers between devices, shards(): three = lax.ppermute(three, 'section', chips([(1, 0), (2, 1), (3, 2)]))  4.29 us
    pallas_call x4, Pallas kernels, shards(): call('place', marked_body if final else place_body, (1,), 1, [whole((2 *...  3.52 us
    pallas_call x1, Pallas kernels, shards(): call('spread', functools.partial(spread_body, count, plan.shape[0], scale...  2.1 us
  transfers between devices with their start and end apart: 18, of which 8 were waited for; matrix products, arithmetic and copies ran while one was open for 0% of the time, Pallas kernels for 18%

profile of v7, /device:TPU:0, one launch (start us, length us, event | category | flops | bytes accessed | tf_op | source)
XLA Modules:
  0.0 89.8 jit_solution(12011214454485885192)
XLA Ops:
  0.6 3.0 %collective-permute-start = (bf16[128,1024]{1,0:T(8,128)(2,1)}, bf16[128,1024]{1,0:T(8,128)(2,1)S(1)}, u32[]{:S(2)}, u32[]{:S(2)}) collective-permute-start(bf16[128,1024]{1,0:T(8,128)(2,1)} %bitcast.27), channel_id=1, source_target_pairs={{0,1},{1,0},{2,3},{3,2},{4,5},{5,4},{6,7},{7,6},{8,9},{9,8},{10,11... | collective-permute-start | bytes 786440 | tf_op jit(solution)/shard_map/ppermute | solution.py:25
  3.6 1.5 %collective-permute-start.1 = (bf16[128,1024]{1,0:T(8,128)(2,1)}, bf16[128,1024]{1,0:T(8,128)(2,1)S(1)}, u32[]{:S(2)}, u32[]{:S(2)}) collective-permute-start(bf16[128,1024]{1,0:T(8,128)(2,1)} %bitcast.28), channel_id=1, source_target_pairs={{0,2},{1,3},{2,0},{3,1},{4,6},{5,7},{6,4},{7,5},{8,10},{9,11},{10,... | collective-permute-start | bytes 786440 | tf_op jit(solution)/shard_map/ppermute | solution.py:25
  5.2 0.0 collective-permute-start.2
  5.2 1.3 %copy-done.1 = bf16[1,128,5120]{2,1,0:T(8,128)(2,1)S(1)} copy-done((bf16[1,128,5120]{2,1,0:T(8,128)(2,1)S(1)}, bf16[1,128,5120]{2,1,0:T(8,128)(2,1)}, u32[]{:S(2)}) %copy-start.1) | copy-done | bytes 1310744
  6.5 0.7 copy-done.3
  7.2 0.7 prep.1
  8.0 2.0 %collective-permute-start.6 = (bf16[1280,128]{1,0:T(8,128)(2,1)S(1)}, bf16[1280,128]{1,0:T(8,128)(2,1)S(1)}, u32[]{:S(2)}, u32[]{:S(2)}) collective-permute-start(bf16[1280,128]{1,0:T(8,128)(2,1)S(1)} %get-tuple-element.33), channel_id=1, source_target_pairs={{0,1},{1,0},{2,3},{3,2},{4,5},{5,4},{6,7},{7,6},{8,9},{9,8},{10,11... | collective-permute-start | bytes 983048 | tf_op jit(solution)/shard_map/ppermute | solution.py:25
  10.0 1.5 %collective-permute-start.7 = (bf16[1280,128]{1,0:T(8,128)(2,1)S(1)}, bf16[1280,128]{1,0:T(8,128)(2,1)S(1)}, u32[]{:S(2)}, u32[]{:S(2)}) collective-permute-start(bf16[1280,128]{1,0:T(8,128)(2,1)S(1)} %get-tuple-element.34), channel_id=1, source_target_pairs={{0,2},{1,3},{2,0},{3,1},{4,6},{5,7},{6,4},{7,5},{8,10},{9,11},{10,... | collective-permute-start | bytes 983048 | tf_op jit(solution)/shard_map/ppermute | solution.py:25
  11.5 2.5 %copy-done = f32[1,1280,1024]{2,1,0:T(8,128)S(1)} copy-done((f32[1,1280,1024]{2,1,0:T(8,128)S(1)}, f32[1,1280,1024]{2,1,0:T(8,128)}, u32[]{:S(2)}) %copy-start) | copy-done | bytes 5242904
  14.0 0.3 low.1.refs_4_
  14.3 0.0 collective-permute-done.refs_1_
  14.3 0.0 slice-start
  14.3 0.0 slice-start.2
  14.4 0.0 slice-start.4
  14.4 0.0 slice-start.1
  14.4 0.0 slice-start.3
  14.4 0.0 slice-start.5
  14.4 0.0 copy-start.5
  14.4 0.1 collective-permute-start.8
  14.5 3.3 %collective-permute-done.1.refs_2_ = bf16[128,1024]{1,0:T(8,128)(2,1)S(1)} collective-permute-done((bf16[128,1024]{1,0:T(8,128)(2,1)}, bf16[128,1024]{1,0:T(8,128)(2,1)S(1)}, u32[]{:S(2)}, u32[]{:S(2)}) %collective-permute-start.1) | collective-permute-done | bytes 262176 | tf_op jit(solution)/shard_map/ppermute | solution.py:25
  17.9 0.3 collective-permute-done.2.refs_3_
  18.2 2.1 %spread.1 = (bf16[512,1024]{1,0:T(8,128)(2,1)S(1)}, bf16[128,1280]{1,0:T(8,128)(2,1)S(1)}, bf16[128,1280]{1,0:T(8,128)(2,1)S(1)}, bf16[128,1280]{1,0:T(8,128)(2,1)S(1)}, bf16[128,1280]{1,0:T(8,128)(2,1)S(1)}) custom-call(s32[4]{0:T(128)S(1)} %copy-done.7, bf16[128,1024]{1,0:T(8,128)(2,1)S(1)} %bitcast.30, ...), custom_call_target="tpu_custom_call" | custom-call | flops 10000000000 | bytes 1 | tf_op jit(solution)/shard_map/spread/pallas_call | solution.py:347
  20.3 1.5 %collective-permute-start.3 = (bf16[128,1280]{1,0:T(8,128)(2,1)S(1)}, bf16[128,1280]{1,0:T(8,128)(2,1)S(1)}, u32[]{:S(2)}, u32[]{:S(2)}) collective-permute-start(bf16[128,1280]{1,0:T(8,128)(2,1)S(1)} %get-tuple-element.28), channel_id=1, source_target_pairs={{0,3},{1,2},{2,1},{3,0},{4,7},{5,6},{6,5},{7,4},{8,11},{9,10},{10,... | collective-permute-start | bytes 983048 | tf_op jit(solution)/shard_map/ppermute | solution.py:25
  21.8 1.5 %collective-permute-start.4 = (bf16[128,1280]{1,0:T(8,128)(2,1)S(1)}, bf16[128,1280]{1,0:T(8,128)(2,1)S(1)}, u32[]{:S(2)}, u32[]{:S(2)}) collective-permute-start(bf16[128,1280]{1,0:T(8,128)(2,1)S(1)} %get-tuple-element.29), channel_id=1, source_target_pairs={{0,2},{1,3},{2,0},{3,1},{4,6},{5,7},{6,4},{7,5},{8,10},{9,11},{10,... | collective-permute-start | bytes 983048 | tf_op jit(solution)/shard_map/ppermute | solution.py:25
  23.3 0.4 collective-permute-done.6.refs_1_
  23.7 2.1 %collective-permute-start.5 = (bf16[128,1280]{1,0:T(8,128)(2,1)S(1)}, bf16[128,1280]{1,0:T(8,128)(2,1)S(1)}, u32[]{:S(2)}, u32[]{:S(2)}) collective-permute-start(bf16[128,1280]{1,0:T(8,128)(2,1)S(1)} %get-tuple-element.30), channel_id=1, source_target_pairs={{0,1},{1,0},{2,3},{3,2},{4,5},{5,4},{6,7},{7,6},{8,9},{9,8},{10,11... | collective-permute-start | bytes 983048 | tf_op jit(solution)/shard_map/ppermute | solution.py:25
  25.7 13.2 %collective-permute-done.7.refs_2_ = bf16[1280,128]{1,0:T(8,128)(2,1)S(1)} collective-permute-done((bf16[1280,128]{1,0:T(8,128)(2,1)S(1)}, bf16[1280,128]{1,0:T(8,128)(2,1)S(1)}, u32[]{:S(2)}, u32[]{:S(2)}) %collective-permute-start.7) | collective-permute-done | bytes 327712 | tf_op jit(solution)/shard_map/ppermute | solution.py:25
  38.9 0.0 collective-permute-done.8.refs_3_
  38.9 0.0 slice-done.2
  39.0 0.0 copy-start.2
  39.0 0.0 copy-start.4
  39.0 7.6 %grad.1 = (f32[1280,1024]{1,0:T(8,128)}, f32[1280,1024]{1,0:T(8,128)}, bf16[256,1280]{1,0:T(8,128)(2,1)S(1)}, bf16[256,1280]{1,0:T(8,128)(2,1)S(1)}, bf16[256,12...) custom-call(s32[1]{0:T(128)} %bitcast.2.place_ref, s32[4]{0:T(128)S(1)} %bitcast.26, ...), custom_call_target="tpu_custom_call" | custom-call | flops 1 | bytes 1 | tf_op jit(solution)/shard_map/grad/pallas_call | solution.py:360
  46.6 0.0 collective-permute-done.3.refs_0_
  46.6 0.0 collective-permute-done.4.refs_1_
  46.6 0.0 collective-permute-done.5.refs_2_
  46.6 0.6 own.1.refs_4_
  47.2 0.1 collective-permute-start.9
  47.3 1.7 %collective-permute-start.16 = (bf16[256,1280]{1,0:T(8,128)(2,1)S(1)}, bf16[256,1280]{1,0:T(8,128)(2,1)S(1)}, u32[]{:S(2)}, u32[]{:S(2)}) collective-permute-start(bf16[256,1280]{1,0:T(8,128)(2,1)S(1)} %get-tuple-element.44), channel_id=1, source_target_pairs={{0,3},{1,2},{2,1},{3,0},{4,7},{5,6},{6,5},{7,4},{8,11},{9,10},{10,... | collective-permute-start | bytes 1966088 | tf_op jit(solution)/shard_map/ppermute | solution.py:25
  49.0 2.1 %collective-permute-start.15 = (bf16[256,1280]{1,0:T(8,128)(2,1)S(1)}, bf16[256,1280]{1,0:T(8,128)(2,1)S(1)}, u32[]{:S(2)}, u32[]{:S(2)}) collective-permute-start(bf16[256,1280]{1,0:T(8,128)(2,1)S(1)} %get-tuple-element.43), channel_id=1, source_target_pairs={{0,1},{1,0},{2,3},{3,2},{4,5},{5,4},{6,7},{7,6},{8,9},{9,8},{10,11... | collective-permute-start | bytes 1966088 | tf_op jit(solution)/shard_map/ppermute | solution.py:25
  51.1 0.6 keep.1.keep_ref
  51.7 0.0 collective-permute-done.9.got_ref
  51.7 0.2 pair.1
  51.9 0.7 collective-permute-start.10
  52.5 0.7 collective-permute-start.11
  53.2 0.1 collective-permute-start.14
  53.3 0.0 collective-permute-done.10.two_ref
  53.3 0.0 collective-permute-done.11.one_ref
  53.3 0.2 middle.1
  53.6 1.3 %collective-permute-start.12 = (bf16[32,5120]{1,0:T(8,128)(2,1)S(1)}, bf16[32,5120]{1,0:T(8,128)(2,1)S(1)}, u32[]{:S(2)}, u32[]{:S(2)}) collective-permute-start(bf16[32,5120]{1,0:T(8,128)(2,1)S(1)} %get-tuple-element.40), channel_id=1, source_target_pairs={{16,0},{20,4},{17,1},{21,5},{18,2},{22,6},{19,3},{23,7}} | collective-permute-start | bytes 983048 | tf_op jit(solution)/shard_map/ppermute | solution.py:429
  54.9 1.3 %collective-permute-start.13 = (bf16[32,5120]{1,0:T(8,128)(2,1)S(1)}, bf16[32,5120]{1,0:T(8,128)(2,1)S(1)}, u32[]{:S(2)}, u32[]{:S(2)}) collective-permute-start(bf16[32,5120]{1,0:T(8,128)(2,1)S(1)} %get-tuple-element.41), channel_id=1, source_target_pairs={{8,0},{16,8},{24,16},{12,4},{20,12},{28,20},{9,1},{17,9},{25,17},{... | collective-permute-start | bytes 983048 | tf_op jit(solution)/shard_map/ppermute | solution.py:428
  56.2 0.9 place.4.refs_0_
  57.1 8.8 %collective-permute-done.16.part_ref = bf16[256,1280]{1,0:T(8,128)(2,1)S(1)} collective-permute-done((bf16[256,1280]{1,0:T(8,128)(2,1)S(1)}, bf16[256,1280]{1,0:T(8,128)(2,1)S(1)}, u32[]{:S(2)}, u32[]{:S(2)}) %collective-permute-start.16) | collective-permute-done | bytes 655392 | tf_op jit(solution)/shard_map/ppermute | solution.py:25
  65.8 0.9 place.5.refs_0_
  66.7 13.5 %collective-permute-done.15.part_ref = bf16[256,1280]{1,0:T(8,128)(2,1)S(1)} collective-permute-done((bf16[256,1280]{1,0:T(8,128)(2,1)S(1)}, bf16[256,1280]{1,0:T(8,128)(2,1)S(1)}, u32[]{:S(2)}, u32[]{:S(2)}) %collective-permute-start.15) | collective-permute-done | bytes 655392 | tf_op jit(solution)/shard_map/ppermute | solution.py:25
  80.2 0.9 place.6._
  81.1 0.0 collective-permute-done.14.part_ref
  81.1 0.9 place.7
  82.0 0.0 collective-permute-done.12.four_ref
  82.0 4.3 %collective-permute-done.13.three_ref = bf16[32,5120]{1,0:T(8,128)(2,1)S(1)} collective-permute-done((bf16[32,5120]{1,0:T(8,128)(2,1)S(1)}, bf16[32,5120]{1,0:T(8,128)(2,1)S(1)}, u32[]{:S(2)}, u32[]{:S(2)}) %collective-permute-start.13) | collective-permute-done | bytes 327712 | tf_op jit(solution)/shard_map/ppermute | solution.py:428
  86.3 0.5 last.1._
  86.8 0.1 collective-permute-start.17
  86.8 1.3 %mine.1.refs_0_ = bf16[128,5120]{1,0:T(8,128)(2,1)} custom-call(s32[1]{0:T(128)} %bitcast.1.chip_ref, s32[1]{0:T(128)} %bitcast.core_ref.place_ref, bf16[64,5120]{1,0:T(8,128)(2,1)S(1)} %keep.1.keep_ref, bf16[64,5120]{1,0:T(8,128)(2,1)S(1)} %collective-permute-done.9.got_ref, bf16[32,5120]{1,0:T(8,128)(2,1)S(1)} %collective-permute-done.10.two_ref, ...), custom_call_target="tpu_custom_call" | custom-call | flops 1 | bytes 1 | tf_op jit(solution)/shard_map/mine/pallas_call | solution.py:442
  88.2 0.8 collective-permute-done.17.part_ref
  88.9 0.9 join.1
  (18 shorter events, 0.0 us)
Async XLA Ops:
  0.6 13.7 %collective-permute-start = (bf16[128,1024]{1,0:T(8,128)(2,1)}, bf16[128,1024]{1,0:T(8,128)(2,1)S(1)}, u32[]{:S(2)}, u32[]{:S(2)}) collective-permute-start(bf16[128,1024]{1,0:T(8,128)(2,1)} %bitcast.27), channel_id=1, source_target_pairs={{0,1},{1,0},{2,3},{3,2},{4,5},{5,4},{6,7},{7,6},{8,9},{9,8},{10,11... | collective-permute-start | bytes 786440 | tf_op jit(solution)/shard_map/ppermute | solution.py:25
  3.6 14.2 %collective-permute-start.1 = (bf16[128,1024]{1,0:T(8,128)(2,1)}, bf16[128,1024]{1,0:T(8,128)(2,1)S(1)}, u32[]{:S(2)}, u32[]{:S(2)}) collective-permute-start(bf16[128,1024]{1,0:T(8,128)(2,1)} %bitcast.28), channel_id=1, source_target_pairs={{0,2},{1,3},{2,0},{3,1},{4,6},{5,7},{6,4},{7,5},{8,10},{9,11},{10,... | collective-permute-start | bytes 786440 | tf_op jit(solution)/shard_map/ppermute | solution.py:25
  5.2 13.0 %collective-permute-start.2 = (bf16[128,1024]{1,0:T(8,128)(2,1)}, bf16[128,1024]{1,0:T(8,128)(2,1)S(1)}, u32[]{:S(2)}, u32[]{:S(2)}) collective-permute-start(bf16[128,1024]{1,0:T(8,128)(2,1)} %bitcast.29), channel_id=1, source_target_pairs={{0,3},{1,2},{2,1},{3,0},{4,7},{5,6},{6,5},{7,4},{8,11},{9,10},{10,... | collective-permute-start | bytes 786440 | tf_op jit(solution)/shard_map/ppermute | solution.py:25
  5.2 1.3 %copy-start.1 = (bf16[1,128,5120]{2,1,0:T(8,128)(2,1)S(1)}, bf16[1,128,5120]{2,1,0:T(8,128)(2,1)}, u32[]{:S(2)}) copy-start(bf16[1,128,5120]{2,1,0:T(8,128)(2,1)} %param.8) | copy-start | bytes 3932164
  6.5 0.7 copy-start.3
  8.0 15.7 %collective-permute-start.6 = (bf16[1280,128]{1,0:T(8,128)(2,1)S(1)}, bf16[1280,128]{1,0:T(8,128)(2,1)S(1)}, u32[]{:S(2)}, u32[]{:S(2)}) collective-permute-start(bf16[1280,128]{1,0:T(8,128)(2,1)S(1)} %get-tuple-element.33), channel_id=1, source_target_pairs={{0,1},{1,0},{2,3},{3,2},{4,5},{5,4},{6,7},{7,6},{8,9},{9,8},{10,11... | collective-permute-start | bytes 983048 | tf_op jit(solution)/shard_map/ppermute | solution.py:25
  10.0 28.9 %collective-permute-start.7 = (bf16[1280,128]{1,0:T(8,128)(2,1)S(1)}, bf16[1280,128]{1,0:T(8,128)(2,1)S(1)}, u32[]{:S(2)}, u32[]{:S(2)}) collective-permute-start(bf16[1280,128]{1,0:T(8,128)(2,1)S(1)} %get-tuple-element.34), channel_id=1, source_target_pairs={{0,2},{1,3},{2,0},{3,1},{4,6},{5,7},{6,4},{7,5},{8,10},{9,11},{10,... | collective-permute-start | bytes 983048 | tf_op jit(solution)/shard_map/ppermute | solution.py:25
  11.5 2.5 %copy-start = (f32[1,1280,1024]{2,1,0:T(8,128)S(1)}, f32[1,1280,1024]{2,1,0:T(8,128)}, u32[]{:S(2)}) copy-start(f32[1,1280,1024]{2,1,0:T(8,128)} %param.11) | copy-start | bytes 15728644
  14.0 4.2 %copy-start.6 = (bf16[1,128,1024]{2,1,0:T(8,128)(2,1)S(1)}, bf16[1,128,1024]{2,1,0:T(8,128)(2,1)}, u32[]{:S(2)}) copy-start(bf16[1,128,1024]{2,1,0:T(8,128)(2,1)} %param.9) | copy-start | bytes 786436
  14.0 4.2 %copy-start.7 = (s32[4]{0:T(128)S(1)}, s32[4]{0:T(128)}, u32[]{:S(2)}) copy-start(s32[4]{0:T(128)} %plan_ref.1) | copy-start | bytes 52
  14.3 24.6 %slice-start = ((s8[5242880]{0:T(1024)(128)(4,1)}), s8[4194304]{0:T(1024)(128)(4,1)S(1)}, s32[]{:S(2)}) async-start(s8[5242880]{0:T(1024)(128)(4,1)} %bitcast.14), calls=%async_computation | async-start | bytes 8388608
  14.3 24.5 %slice-start.2 = ((s8[5242880]{0:T(1024)(128)(4,1)}), s8[4194304]{0:T(1024)(128)(4,1)S(1)}, s32[]{:S(2)}) async-start(s8[5242880]{0:T(1024)(128)(4,1)} %bitcast.20), calls=%async_computation.2 | async-start | bytes 8388608
  14.4 24.5 %slice-start.4 = ((s8[5242880]{0:T(1024)(128)(4,1)}), s8[4194304]{0:T(1024)(128)(4,1)S(1)}, s32[]{:S(2)}) async-start(s8[5242880]{0:T(1024)(128)(4,1)} %bitcast.23), calls=%async_computation.4 | async-start | bytes 8388608
  14.4 24.5 %slice-start.1 = ((s8[5242880]{0:T(1024)(128)(4,1)}), s8[1048576]{0:T(1024)(128)(4,1)S(1)}, s32[]{:S(2)}) async-start(s8[5242880]{0:T(1024)(128)(4,1)} %bitcast.14), calls=%async_computation.1 | async-start | bytes 2097152
  14.4 24.5 %slice-start.3 = ((s8[5242880]{0:T(1024)(128)(4,1)}), s8[1048576]{0:T(1024)(128)(4,1)S(1)}, s32[]{:S(2)}) async-start(s8[5242880]{0:T(1024)(128)(4,1)} %bitcast.20), calls=%async_computation.3 | async-start | bytes 2097152
  14.4 24.5 %slice-start.5 = ((s8[5242880]{0:T(1024)(128)(4,1)}), s8[1048576]{0:T(1024)(128)(4,1)S(1)}, s32[]{:S(2)}) async-start(s8[5242880]{0:T(1024)(128)(4,1)} %bitcast.23), calls=%async_computation.5 | async-start | bytes 2097152
  14.4 24.5 %copy-start.5 = (s32[1,4]{1,0:T(1,128)S(1)}, s32[1,4]{1,0:T(1,128)}, u32[]{:S(2)}) copy-start(s32[1,4]{1,0:T(1,128)} %param.14) | copy-start | bytes 52
  14.4 24.5 %collective-permute-start.8 = (bf16[1280,128]{1,0:T(8,128)(2,1)S(1)}, bf16[1280,128]{1,0:T(8,128)(2,1)S(1)}, u32[]{:S(2)}, u32[]{:S(2)}) collective-permute-start(bf16[1280,128]{1,0:T(8,128)(2,1)S(1)} %get-tuple-element.35), channel_id=1, source_target_pairs={{0,3},{1,2},{2,1},{3,0},{4,7},{5,6},{6,5},{7,4},{8,11},{9,10},{10,... | collective-permute-start | bytes 983048 | tf_op jit(solution)/shard_map/ppermute | solution.py:25
  20.3 26.3 %collective-permute-start.3 = (bf16[128,1280]{1,0:T(8,128)(2,1)S(1)}, bf16[128,1280]{1,0:T(8,128)(2,1)S(1)}, u32[]{:S(2)}, u32[]{:S(2)}) collective-permute-start(bf16[128,1280]{1,0:T(8,128)(2,1)S(1)} %get-tuple-element.28), channel_id=1, source_target_pairs={{0,3},{1,2},{2,1},{3,0},{4,7},{5,6},{6,5},{7,4},{8,11},{9,10},{10,... | collective-permute-start | bytes 983048 | tf_op jit(solution)/shard_map/ppermute | solution.py:25
  21.8 24.8 %collective-permute-start.4 = (bf16[128,1280]{1,0:T(8,128)(2,1)S(1)}, bf16[128,1280]{1,0:T(8,128)(2,1)S(1)}, u32[]{:S(2)}, u32[]{:S(2)}) collective-permute-start(bf16[128,1280]{1,0:T(8,128)(2,1)S(1)} %get-tuple-element.29), channel_id=1, source_target_pairs={{0,2},{1,3},{2,0},{3,1},{4,6},{5,7},{6,4},{7,5},{8,10},{9,11},{10,... | collective-permute-start | bytes 983048 | tf_op jit(solution)/shard_map/ppermute | solution.py:25
  23.7 22.9 %collective-permute-start.5 = (bf16[128,1280]{1,0:T(8,128)(2,1)S(1)}, bf16[128,1280]{1,0:T(8,128)(2,1)S(1)}, u32[]{:S(2)}, u32[]{:S(2)}) collective-permute-start(bf16[128,1280]{1,0:T(8,128)(2,1)S(1)} %get-tuple-element.30), channel_id=1, source_target_pairs={{0,1},{1,0},{2,3},{3,2},{4,5},{5,4},{6,7},{7,6},{8,9},{9,8},{10,11... | collective-permute-start | bytes 983048 | tf_op jit(solution)/shard_map/ppermute | solution.py:25
  39.0 7.6 %copy-start.2 = (bf16[1,128,5120]{2,1,0:T(8,128)(2,1)S(1)}, bf16[1,128,5120]{2,1,0:T(8,128)(2,1)}, u32[]{:S(2)}) copy-start(bf16[1,128,5120]{2,1,0:T(8,128)(2,1)} %param.8) | copy-start | bytes 3932164
  39.0 7.6 %copy-start.4 = (f32[1,5120]{1,0:T(1,128)S(1)}, f32[1,5120]{1,0:T(1,128)}, u32[]{:S(2)}) copy-start(f32[1,5120]{1,0:T(1,128)} %gain_ref.5) | copy-start | bytes 61444
  47.2 4.5 %collective-permute-start.9 = (bf16[64,5120]{1,0:T(8,128)(2,1)S(1)}, bf16[64,5120]{1,0:T(8,128)(2,1)S(1)}, u32[]{:S(2)}, u32[]{:S(2)}) collective-permute-start(bf16[64,5120]{1,0:T(8,128)(2,1)S(1)} %own.1.refs_4_), channel_id=1, source_target_pairs={{0,4},{4,0},{8,12},{12,8},{16,20},{20,16},{24,28},{28,24},{1,5},{5... | collective-permute-start | bytes 1966088 | tf_op jit(solution)/shard_map/ppermute | solution.py:25
  47.3 18.5 %collective-permute-start.16 = (bf16[256,1280]{1,0:T(8,128)(2,1)S(1)}, bf16[256,1280]{1,0:T(8,128)(2,1)S(1)}, u32[]{:S(2)}, u32[]{:S(2)}) collective-permute-start(bf16[256,1280]{1,0:T(8,128)(2,1)S(1)} %get-tuple-element.44), channel_id=1, source_target_pairs={{0,3},{1,2},{2,1},{3,0},{4,7},{5,6},{6,5},{7,4},{8,11},{9,10},{10,... | collective-permute-start | bytes 1966088 | tf_op jit(solution)/shard_map/ppermute | solution.py:25
  49.0 31.3 %collective-permute-start.15 = (bf16[256,1280]{1,0:T(8,128)(2,1)S(1)}, bf16[256,1280]{1,0:T(8,128)(2,1)S(1)}, u32[]{:S(2)}, u32[]{:S(2)}) collective-permute-start(bf16[256,1280]{1,0:T(8,128)(2,1)S(1)} %get-tuple-element.43), channel_id=1, source_target_pairs={{0,1},{1,0},{2,3},{3,2},{4,5},{5,4},{6,7},{7,6},{8,9},{9,8},{10,11... | collective-permute-start | bytes 1966088 | tf_op jit(solution)/shard_map/ppermute | solution.py:25
  51.9 1.5 %collective-permute-start.10 = (bf16[32,5120]{1,0:T(8,128)(2,1)S(1)}, bf16[32,5120]{1,0:T(8,128)(2,1)S(1)}, u32[]{:S(2)}, u32[]{:S(2)}) collective-permute-start(bf16[32,5120]{1,0:T(8,128)(2,1)S(1)} %get-tuple-element.38), channel_id=1, source_target_pairs={{16,8},{24,16},{20,12},{28,20},{17,9},{25,17},{21,13},{29,21},{18,... | collective-permute-start | bytes 983048 | tf_op jit(solution)/shard_map/ppermute | solution.py:424
  52.5 0.8 collective-permute-start.11
  53.2 27.9 %collective-permute-start.14 = (bf16[256,1280]{1,0:T(8,128)(2,1)S(1)}, bf16[256,1280]{1,0:T(8,128)(2,1)S(1)}, u32[]{:S(2)}, u32[]{:S(2)}) collective-permute-start(bf16[256,1280]{1,0:T(8,128)(2,1)S(1)} %get-tuple-element.42), channel_id=1, source_target_pairs={{0,2},{1,3},{2,0},{3,1},{4,6},{5,7},{6,4},{7,5},{8,10},{9,11},{10,... | collective-permute-start | bytes 1966088 | tf_op jit(solution)/shard_map/ppermute | solution.py:25
  53.6 28.4 %collective-permute-start.12 = (bf16[32,5120]{1,0:T(8,128)(2,1)S(1)}, bf16[32,5120]{1,0:T(8,128)(2,1)S(1)}, u32[]{:S(2)}, u32[]{:S(2)}) collective-permute-start(bf16[32,5120]{1,0:T(8,128)(2,1)S(1)} %get-tuple-element.40), channel_id=1, source_target_pairs={{16,0},{20,4},{17,1},{21,5},{18,2},{22,6},{19,3},{23,7}} | collective-permute-start | bytes 983048 | tf_op jit(solution)/shard_map/ppermute | solution.py:429
  54.9 31.4 %collective-permute-start.13 = (bf16[32,5120]{1,0:T(8,128)(2,1)S(1)}, bf16[32,5120]{1,0:T(8,128)(2,1)S(1)}, u32[]{:S(2)}, u32[]{:S(2)}) collective-permute-start(bf16[32,5120]{1,0:T(8,128)(2,1)S(1)} %get-tuple-element.41), channel_id=1, source_target_pairs={{8,0},{16,8},{24,16},{12,4},{20,12},{28,20},{9,1},{17,9},{25,17},{... | collective-permute-start | bytes 983048 | tf_op jit(solution)/shard_map/ppermute | solution.py:428
  86.8 2.2 %collective-permute-start.17 = (bf16[64,5120]{1,0:T(8,128)(2,1)S(1)}, bf16[64,5120]{1,0:T(8,128)(2,1)S(1)}, u32[]{:S(2)}, u32[]{:S(2)}) collective-permute-start(bf16[64,5120]{1,0:T(8,128)(2,1)S(1)} %last.1._), channel_id=1, source_target_pairs={{0,4},{4,0},{8,12},{12,8},{16,20},{20,16},{24,28},{28,24},{1,5},{5... | collective-permute-start | bytes 1966088 | tf_op jit(solution)/shard_map/ppermute | solution.py:25

commit v8 on v6

--- a/solution.py
+++ b/solution.py
@@ -228,7 +228,7 @@
 
 
 def own_body(count, mine, place_ref, core_ref, tok_ref, gain_ref, inv_ref, *refs):
-    spread, out_ref = refs[:count][::-1], refs[-1]
+    spread, out_ref = refs[:count], refs[-1]
     place = place_ref[0]
     core = core_ref[0]
     width = tok_ref.shape[1]
@@ -404,7 +404,7 @@
             + [anywhere],
             [whole((half, width))],
             [sds((half, width), bf16)],
-        )(place, core, tok_rows, norm_gain, inverse, *spread[::-1], after)
+        )(place, core, tok_rows, norm_gain, inverse, *spread, after)
         return term
 
     give = own("own", False, grad_mark)
@@ -423,7 +423,14 @@
     one = lax.ppermute(one, "section", chips([(3, 1), (1, 2)]))
     two = lax.ppermute(two, "section", chips([(2, 1), (3, 2)]))
     three, four = call(
-        "middle", middle_body, (1,), 1, [full, full, part, part], [part, part], [piece, piece]
+        "middle",
+        middle_body,
+        (1,),
+        1,
+        [full, full, part, part],
+        [part, part],
+        [piece, piece],
+        work=10**6,
     )(chip, keep, got, two, one)
     three = lax.ppermute(three, "section", chips([(1, 0), (2, 1), (3, 2)]))
     four = lax.ppermute(four, "section", chips([(2, 0)]))

time: 87.8 us -> 87.6 us (level)
  waiting for transfers between devices: 42.6 us -> 40.3 us
  starting transfers between devices: 21 us -> 23.1 us
    ppermute x14, starting transfers between devices: 17 us -> 19.1 us  [swap(): return lax.ppermute(x, axis, [(i, i ^ k) for i in range(count)])]
    ppermute x14, waiting for transfers between devices: 38.2 us -> 36.2 us  [swap(): return lax.ppermute(x, axis, [(i, i ^ k) for i in range(count)])]
  transfers between devices with their start and end apart: 18 -> 18, of which waited for: 11 -> 10; matrix products, arithmetic and copies ran while one was open for 0% -> 0% of each run, Pallas kernels for 19% -> 19%
where the time goes in v8:
time: 87.6 us; the launch traced here: 87.3 us
  waiting for transfers between devices  40.3 us (46%)
  starting transfers between devices  23.1 us (26%)
  Pallas kernels  18.5 us (21%)
  local copies, waits for them, and re-layouts  4.59 us (5%)
  between operations  0.89 us (1%)
    ppermute x14, waiting for transfers between devices, swap(): return lax.ppermute(x, axis, [(i, i ^ k) for i in range(count)])  36.2 us
    ppermute x14, starting transfers between devices, swap(): return lax.ppermute(x, axis, [(i, i ^ k) for i in range(count)])  19.1 us
    pallas_call x1, Pallas kernels, shards(): call('grad', functools.partial(grad_body, count, head, scale), (cols // r...  7.59 us
    unnamed x28, local copies, waits for them, and re-layouts  4.59 us
    ppermute x1, waiting for transfers between devices, shards(): three = lax.ppermute(three, 'section', chips([(1, 0), (2, 1), (3, 2)]))  4.1 us
    pallas_call x4, Pallas kernels, shards(): call('place', marked_body if final else place_body, (1,), 1, [whole((2 *...  3.52 us
    pallas_call x1, Pallas kernels, shards(): call('spread', functools.partial(spread_body, count, plan.shape[0], scale...  2.1 us
  transfers between devices with their start and end apart: 18, of which 10 were waited for; matrix products, arithmetic and copies ran while one was open for 0% of the time, Pallas kernels for 19%

profile of v8, /device:TPU:0, one launch (start us, length us, event | category | flops | bytes accessed | tf_op | source)
XLA Modules:
  0.0 87.3 jit_solution(5752619212002256447)
XLA Ops:
  0.6 4.0 %collective-permute-start = (bf16[128,1024]{1,0:T(8,128)(2,1)}, bf16[128,1024]{1,0:T(8,128)(2,1)S(1)}, u32[]{:S(2)}, u32[]{:S(2)}) collective-permute-start(bf16[128,1024]{1,0:T(8,128)(2,1)} %bitcast.27), channel_id=1, source_target_pairs={{0,3},{1,2},{2,1},{3,0},{4,7},{5,6},{6,5},{7,4},{8,11},{9,10},{10,... | collective-permute-start | bytes 786440 | tf_op jit(solution)/shard_map/ppermute | solution.py:25
  4.6 0.5 collective-permute-start.1
  5.1 0.1 collective-permute-start.2
  5.2 1.3 %copy-done.1 = bf16[1,128,5120]{2,1,0:T(8,128)(2,1)S(1)} copy-done((bf16[1,128,5120]{2,1,0:T(8,128)(2,1)S(1)}, bf16[1,128,5120]{2,1,0:T(8,128)(2,1)}, u32[]{:S(2)}) %copy-start.1) | copy-done | bytes 1310744
  6.6 0.7 copy-done.3
  7.3 0.7 prep.1
  8.0 2.9 %collective-permute-start.6 = (bf16[1280,128]{1,0:T(8,128)(2,1)S(1)}, bf16[1280,128]{1,0:T(8,128)(2,1)S(1)}, u32[]{:S(2)}, u32[]{:S(2)}) collective-permute-start(bf16[1280,128]{1,0:T(8,128)(2,1)S(1)} %get-tuple-element.32), channel_id=1, source_target_pairs={{0,3},{1,2},{2,1},{3,0},{4,7},{5,6},{6,5},{7,4},{8,11},{9,10},{10,... | collective-permute-start | bytes 983048 | tf_op jit(solution)/shard_map/ppermute | solution.py:25
  10.9 0.5 collective-permute-start.7
  11.5 2.5 %copy-done = f32[1,1280,1024]{2,1,0:T(8,128)S(1)} copy-done((f32[1,1280,1024]{2,1,0:T(8,128)S(1)}, f32[1,1280,1024]{2,1,0:T(8,128)}, u32[]{:S(2)}) %copy-start) | copy-done | bytes 5242904
  13.9 0.3 low.1.refs_4_
  14.3 0.0 collective-permute-done.refs_0_
  14.3 0.0 slice-start
  14.3 0.0 slice-start.2
  14.3 0.0 slice-start.4
  14.3 0.0 slice-start.1
  14.3 0.0 slice-start.3
  14.3 0.0 slice-start.5
  14.4 0.0 copy-start.5
  14.4 0.2 collective-permute-start.8
  14.6 3.1 %collective-permute-done.1.refs_1_ = bf16[128,1024]{1,0:T(8,128)(2,1)S(1)} collective-permute-done((bf16[128,1024]{1,0:T(8,128)(2,1)}, bf16[128,1024]{1,0:T(8,128)(2,1)S(1)}, u32[]{:S(2)}, u32[]{:S(2)}) %collective-permute-start.1) | collective-permute-done | bytes 262176 | tf_op jit(solution)/shard_map/ppermute | solution.py:25
  17.7 0.5 collective-permute-done.2.refs_2_
  18.2 0.0 copy-done.7
  18.2 2.1 %spread.1 = (bf16[512,1024]{1,0:T(8,128)(2,1)S(1)}, bf16[128,1280]{1,0:T(8,128)(2,1)S(1)}, bf16[128,1280]{1,0:T(8,128)(2,1)S(1)}, bf16[128,1280]{1,0:T(8,128)(2,1)S(1)}, bf16[128,1280]{1,0:T(8,128)(2,1)S(1)}) custom-call(s32[4]{0:T(128)S(1)} %copy-done.7, bf16[128,1024]{1,0:T(8,128)(2,1)S(1)} %collective-permute-done.refs_0_, ...), custom_call_target="tpu_custom_call" | custom-call | flops 10000000000 | bytes 1 | tf_op jit(solution)/shard_map/spread/pallas_call | solution.py:347
  20.3 1.6 %collective-permute-start.3 = (bf16[128,1280]{1,0:T(8,128)(2,1)S(1)}, bf16[128,1280]{1,0:T(8,128)(2,1)S(1)}, u32[]{:S(2)}, u32[]{:S(2)}) collective-permute-start(bf16[128,1280]{1,0:T(8,128)(2,1)S(1)} %get-tuple-element.29), channel_id=1, source_target_pairs={{0,1},{1,0},{2,3},{3,2},{4,5},{5,4},{6,7},{7,6},{8,9},{9,8},{10,11... | collective-permute-start | bytes 983048 | tf_op jit(solution)/shard_map/ppermute | solution.py:25
  21.8 1.5 %collective-permute-start.4 = (bf16[128,1280]{1,0:T(8,128)(2,1)S(1)}, bf16[128,1280]{1,0:T(8,128)(2,1)S(1)}, u32[]{:S(2)}, u32[]{:S(2)}) collective-permute-start(bf16[128,1280]{1,0:T(8,128)(2,1)S(1)} %get-tuple-element.30), channel_id=1, source_target_pairs={{0,2},{1,3},{2,0},{3,1},{4,6},{5,7},{6,4},{7,5},{8,10},{9,11},{10,... | collective-permute-start | bytes 983048 | tf_op jit(solution)/shard_map/ppermute | solution.py:25
  23.3 1.3 %collective-permute-done.6.refs_0_ = bf16[1280,128]{1,0:T(8,128)(2,1)S(1)} collective-permute-done((bf16[1280,128]{1,0:T(8,128)(2,1)S(1)}, bf16[1280,128]{1,0:T(8,128)(2,1)S(1)}, u32[]{:S(2)}, u32[]{:S(2)}) %collective-permute-start.6) | collective-permute-done | bytes 327712 | tf_op jit(solution)/shard_map/ppermute | solution.py:25
  24.7 2.9 %collective-permute-start.5 = (bf16[128,1280]{1,0:T(8,128)(2,1)S(1)}, bf16[128,1280]{1,0:T(8,128)(2,1)S(1)}, u32[]{:S(2)}, u32[]{:S(2)}) collective-permute-start(bf16[128,1280]{1,0:T(8,128)(2,1)S(1)} %get-tuple-element.31), channel_id=1, source_target_pairs={{0,3},{1,2},{2,1},{3,0},{4,7},{5,6},{6,5},{7,4},{8,11},{9,10},{10,... | collective-permute-start | bytes 983048 | tf_op jit(solution)/shard_map/ppermute | solution.py:25
  27.6 3.3 %collective-permute-done.7.refs_1_ = bf16[1280,128]{1,0:T(8,128)(2,1)S(1)} collective-permute-done((bf16[1280,128]{1,0:T(8,128)(2,1)S(1)}, bf16[1280,128]{1,0:T(8,128)(2,1)S(1)}, u32[]{:S(2)}, u32[]{:S(2)}) %collective-permute-start.7) | collective-permute-done | bytes 327712 | tf_op jit(solution)/shard_map/ppermute | solution.py:25
  30.9 1.4 %collective-permute-done.8.refs_2_ = bf16[1280,128]{1,0:T(8,128)(2,1)S(1)} collective-permute-done((bf16[1280,128]{1,0:T(8,128)(2,1)S(1)}, bf16[1280,128]{1,0:T(8,128)(2,1)S(1)}, u32[]{:S(2)}, u32[]{:S(2)}) %collective-permute-start.8) | collective-permute-done | bytes 327712 | tf_op jit(solution)/shard_map/ppermute | solution.py:25
  32.3 0.0 copy-start.2
  32.3 0.0 copy-start.4
  32.4 7.6 %grad.1 = (f32[1280,1024]{1,0:T(8,128)}, f32[1280,1024]{1,0:T(8,128)}, bf16[256,1280]{1,0:T(8,128)(2,1)S(1)}, bf16[256,1280]{1,0:T(8,128)(2,1)S(1)}, bf16[256,12...) custom-call(s32[1]{0:T(128)} %bitcast.2.place_ref, s32[4]{0:T(128)S(1)} %bitcast.26, ...), custom_call_target="tpu_custom_call" | custom-call | flops 1 | bytes 1 | tf_op jit(solution)/shard_map/grad/pallas_call | solution.py:360
  39.9 0.0 collective-permute-done.3.refs_1_
  39.9 0.0 collective-permute-done.4.refs_2_
  39.9 5.0 %collective-permute-done.5.refs_3_ = bf16[128,1280]{1,0:T(8,128)(2,1)S(1)} collective-permute-done((bf16[128,1280]{1,0:T(8,128)(2,1)S(1)}, bf16[128,1280]{1,0:T(8,128)(2,1)S(1)}, u32[]{:S(2)}, u32[]{:S(2)}) %collective-permute-start.5) | collective-permute-done | bytes 327712 | tf_op jit(solution)/shard_map/ppermute | solution.py:25
  44.9 0.6 own.1.refs_4_
  45.5 0.1 collective-permute-start.9
  45.6 2.7 %collective-permute-start.16 = (bf16[256,1280]{1,0:T(8,128)(2,1)S(1)}, bf16[256,1280]{1,0:T(8,128)(2,1)S(1)}, u32[]{:S(2)}, u32[]{:S(2)}) collective-permute-start(bf16[256,1280]{1,0:T(8,128)(2,1)S(1)} %get-tuple-element.44), channel_id=1, source_target_pairs={{0,3},{1,2},{2,1},{3,0},{4,7},{5,6},{6,5},{7,4},{8,11},{9,10},{10,... | collective-permute-start | bytes 1966088 | tf_op jit(solution)/shard_map/ppermute | solution.py:25
  48.3 0.6 keep.1.keep_ref
  48.9 0.0 collective-permute-done.9.got_ref
  48.9 0.2 pair.1
  49.1 0.7 collective-permute-start.10
  49.7 0.7 collective-permute-start.11
  50.4 0.6 collective-permute-start.15
  51.0 1.5 %collective-permute-start.14 = (bf16[256,1280]{1,0:T(8,128)(2,1)S(1)}, bf16[256,1280]{1,0:T(8,128)(2,1)S(1)}, u32[]{:S(2)}, u32[]{:S(2)}) collective-permute-start(bf16[256,1280]{1,0:T(8,128)(2,1)S(1)} %get-tuple-element.42), channel_id=1, source_target_pairs={{0,2},{1,3},{2,0},{3,1},{4,6},{5,7},{6,4},{7,5},{8,10},{9,11},{10,... | collective-permute-start | bytes 1966088 | tf_op jit(solution)/shard_map/ppermute | solution.py:25
  52.5 0.0 collective-permute-done.10.two_ref
  52.5 0.0 collective-permute-done.11.one_ref
  52.5 0.2 middle.1
  52.7 1.3 %collective-permute-start.12 = (bf16[32,5120]{1,0:T(8,128)(2,1)S(1)}, bf16[32,5120]{1,0:T(8,128)(2,1)S(1)}, u32[]{:S(2)}, u32[]{:S(2)}) collective-permute-start(bf16[32,5120]{1,0:T(8,128)(2,1)S(1)} %get-tuple-element.40), channel_id=1, source_target_pairs={{16,0},{20,4},{17,1},{21,5},{18,2},{22,6},{19,3},{23,7}} | collective-permute-start | bytes 983048 | tf_op jit(solution)/shard_map/ppermute | solution.py:436
  54.0 1.3 %collective-permute-start.13 = (bf16[32,5120]{1,0:T(8,128)(2,1)S(1)}, bf16[32,5120]{1,0:T(8,128)(2,1)S(1)}, u32[]{:S(2)}, u32[]{:S(2)}) collective-permute-start(bf16[32,5120]{1,0:T(8,128)(2,1)S(1)} %get-tuple-element.41), channel_id=1, source_target_pairs={{8,0},{16,8},{24,16},{12,4},{20,12},{28,20},{9,1},{17,9},{25,17},{... | collective-permute-start | bytes 983048 | tf_op jit(solution)/shard_map/ppermute | solution.py:435
  55.3 0.9 %place.4.refs_0_ = bf16[256,5120]{1,0:T(8,128)(2,1)} custom-call(s32[1]{0:T(128)} %bitcast.2.place_ref, bf16[256,1280]{1,0:T(8,128)(2,1)S(1)} %get-tuple-element.45.part_ref), custom_call_target="tpu_custom_call" | custom-call | flops 1 | bytes 1 | tf_op jit(solution)/shard_map/place/pallas_call | solution.py:383
  56.2 7.9 %collective-permute-done.16.part_ref = bf16[256,1280]{1,0:T(8,128)(2,1)S(1)} collective-permute-done((bf16[256,1280]{1,0:T(8,128)(2,1)S(1)}, bf16[256,1280]{1,0:T(8,128)(2,1)S(1)}, u32[]{:S(2)}, u32[]{:S(2)}) %collective-permute-start.16) | collective-permute-done | bytes 655392 | tf_op jit(solution)/shard_map/ppermute | solution.py:25
  64.1 0.9 %place.5.refs_0_ = bf16[256,5120]{1,0:T(8,128)(2,1)} custom-call(s32[1]{0:T(128)} %bitcast.2.place_ref, bf16[256,1280]{1,0:T(8,128)(2,1)S(1)} %collective-permute-done.16.part_ref, bf16[256,5120]{1,0:T(8,128)(2,1)} %place.4.refs_0_), custom_call_target="tpu_custom_call", output_to_operand_aliasing={{}: (2, {})} | custom-call | flops 1 | bytes 1 | tf_op jit(solution)/shard_map/place/pallas_call | solution.py:383
  65.0 13.0 %collective-permute-done.15.part_ref = bf16[256,1280]{1,0:T(8,128)(2,1)S(1)} collective-permute-done((bf16[256,1280]{1,0:T(8,128)(2,1)S(1)}, bf16[256,1280]{1,0:T(8,128)(2,1)S(1)}, u32[]{:S(2)}, u32[]{:S(2)}) %collective-permute-start.15) | collective-permute-done | bytes 655392 | tf_op jit(solution)/shard_map/ppermute | solution.py:25
  78.0 0.9 %place.6._ = bf16[256,5120]{1,0:T(8,128)(2,1)} custom-call(s32[1]{0:T(128)} %bitcast.2.place_ref, bf16[256,1280]{1,0:T(8,128)(2,1)S(1)} %collective-permute-done.15.part_ref, bf16[256,5120]{1,0:T(8,128)(2,1)} %place.5.refs_0_), custom_call_target="tpu_custom_call", output_to_operand_aliasing={{}: (2, {})} | custom-call | flops 1 | bytes 1 | tf_op jit(solution)/shard_map/place/pallas_call | solution.py:383
  78.8 0.0 collective-permute-done.14.part_ref
  78.8 0.9 %place.7 = (bf16[256,5120]{1,0:T(8,128)(2,1)}, f32[8,128]{1,0:T(8,128)S(1)}) custom-call(s32[1]{0:T(128)} %bitcast.2.place_ref, bf16[256,1280]{1,0:T(8,128)(2,1)S(1)} %collective-permute-done.14.part_ref, bf16[256,5120]{1,0:T(8,128)(2,1)} %place.6._), custom_call_target="tpu_custom_call", output_to_operand_aliasing={{0}: (2, {})} | custom-call | flops 1 | bytes 1 | tf_op jit(solution)/shard_map/place/pallas_call | solution.py:383
  79.7 0.0 collective-permute-done.12.four_ref
  79.7 4.1 %collective-permute-done.13.three_ref = bf16[32,5120]{1,0:T(8,128)(2,1)S(1)} collective-permute-done((bf16[32,5120]{1,0:T(8,128)(2,1)S(1)}, bf16[32,5120]{1,0:T(8,128)(2,1)S(1)}, u32[]{:S(2)}, u32[]{:S(2)}) %collective-permute-start.13) | collective-permute-done | bytes 327712 | tf_op jit(solution)/shard_map/ppermute | solution.py:435
  83.8 0.5 last.1._
  84.3 0.1 collective-permute-start.17
  84.4 1.3 %mine.1.refs_0_ = bf16[128,5120]{1,0:T(8,128)(2,1)} custom-call(s32[1]{0:T(128)} %bitcast.1.chip_ref, s32[1]{0:T(128)} %bitcast.core_ref.place_ref, bf16[64,5120]{1,0:T(8,128)(2,1)S(1)} %keep.1.keep_ref, bf16[64,5120]{1,0:T(8,128)(2,1)S(1)} %collective-permute-done.9.got_ref, bf16[32,5120]{1,0:T(8,128)(2,1)S(1)} %collective-permute-done.10.two_ref, ...), custom_call_target="tpu_custom_call" | custom-call | flops 1 | bytes 1 | tf_op jit(solution)/shard_map/mine/pallas_call | solution.py:449
  85.7 0.8 collective-permute-done.17.part_ref
  86.5 0.9 %join.1 = bf16[128,5120]{1,0:T(8,128)(2,1)} custom-call(s32[1]{0:T(128)} %bitcast.core_ref.place_ref, bf16[64,5120]{1,0:T(8,128)(2,1)S(1)} %collective-permute-done.17.part_ref, bf16[128,5120]{1,0:T(8,128)(2,1)} %mine.1.refs_0_), custom_call_target="tpu_custom_call", output_to_operand_aliasing={{}: (2, {})} | custom-call | flops 1 | bytes 1 | tf_op jit(solution)/shard_map/join/pallas_call | solution.py:458
  (18 shorter events, 0.0 us)
Async XLA Ops:
  0.6 13.6 %collective-permute-start = (bf16[128,1024]{1,0:T(8,128)(2,1)}, bf16[128,1024]{1,0:T(8,128)(2,1)S(1)}, u32[]{:S(2)}, u32[]{:S(2)}) collective-permute-start(bf16[128,1024]{1,0:T(8,128)(2,1)} %bitcast.27), channel_id=1, source_target_pairs={{0,3},{1,2},{2,1},{3,0},{4,7},{5,6},{6,5},{7,4},{8,11},{9,10},{10,... | collective-permute-start | bytes 786440 | tf_op jit(solution)/shard_map/ppermute | solution.py:25
  4.6 13.1 %collective-permute-start.1 = (bf16[128,1024]{1,0:T(8,128)(2,1)}, bf16[128,1024]{1,0:T(8,128)(2,1)S(1)}, u32[]{:S(2)}, u32[]{:S(2)}) collective-permute-start(bf16[128,1024]{1,0:T(8,128)(2,1)} %bitcast.28), channel_id=1, source_target_pairs={{0,2},{1,3},{2,0},{3,1},{4,6},{5,7},{6,4},{7,5},{8,10},{9,11},{10,... | collective-permute-start | bytes 786440 | tf_op jit(solution)/shard_map/ppermute | solution.py:25
  5.1 13.1 %collective-permute-start.2 = (bf16[128,1024]{1,0:T(8,128)(2,1)}, bf16[128,1024]{1,0:T(8,128)(2,1)S(1)}, u32[]{:S(2)}, u32[]{:S(2)}) collective-permute-start(bf16[128,1024]{1,0:T(8,128)(2,1)} %bitcast.29), channel_id=1, source_target_pairs={{0,1},{1,0},{2,3},{3,2},{4,5},{5,4},{6,7},{7,6},{8,9},{9,8},{10,11... | collective-permute-start | bytes 786440 | tf_op jit(solution)/shard_map/ppermute | solution.py:25
  5.2 1.3 %copy-start.1 = (bf16[1,128,5120]{2,1,0:T(8,128)(2,1)S(1)}, bf16[1,128,5120]{2,1,0:T(8,128)(2,1)}, u32[]{:S(2)}) copy-start(bf16[1,128,5120]{2,1,0:T(8,128)(2,1)} %param.8) | copy-start | bytes 3932164
  6.6 0.7 copy-start.3
  8.0 16.6 %collective-permute-start.6 = (bf16[1280,128]{1,0:T(8,128)(2,1)S(1)}, bf16[1280,128]{1,0:T(8,128)(2,1)S(1)}, u32[]{:S(2)}, u32[]{:S(2)}) collective-permute-start(bf16[1280,128]{1,0:T(8,128)(2,1)S(1)} %get-tuple-element.32), channel_id=1, source_target_pairs={{0,3},{1,2},{2,1},{3,0},{4,7},{5,6},{6,5},{7,4},{8,11},{9,10},{10,... | collective-permute-start | bytes 983048 | tf_op jit(solution)/shard_map/ppermute | solution.py:25
  10.9 19.9 %collective-permute-start.7 = (bf16[1280,128]{1,0:T(8,128)(2,1)S(1)}, bf16[1280,128]{1,0:T(8,128)(2,1)S(1)}, u32[]{:S(2)}, u32[]{:S(2)}) collective-permute-start(bf16[1280,128]{1,0:T(8,128)(2,1)S(1)} %get-tuple-element.33), channel_id=1, source_target_pairs={{0,2},{1,3},{2,0},{3,1},{4,6},{5,7},{6,4},{7,5},{8,10},{9,11},{10,... | collective-permute-start | bytes 983048 | tf_op jit(solution)/shard_map/ppermute | solution.py:25
  11.5 2.5 %copy-start = (f32[1,1280,1024]{2,1,0:T(8,128)S(1)}, f32[1,1280,1024]{2,1,0:T(8,128)}, u32[]{:S(2)}) copy-start(f32[1,1280,1024]{2,1,0:T(8,128)} %param.11) | copy-start | bytes 15728644
  13.9 4.2 %copy-start.6 = (bf16[1,128,1024]{2,1,0:T(8,128)(2,1)S(1)}, bf16[1,128,1024]{2,1,0:T(8,128)(2,1)}, u32[]{:S(2)}) copy-start(bf16[1,128,1024]{2,1,0:T(8,128)(2,1)} %param.9) | copy-start | bytes 786436
  13.9 4.2 %copy-start.7 = (s32[4]{0:T(128)S(1)}, s32[4]{0:T(128)}, u32[]{:S(2)}) copy-start(s32[4]{0:T(128)} %plan_ref.1) | copy-start | bytes 52
  14.3 18.0 %slice-start = ((s8[5242880]{0:T(1024)(128)(4,1)}), s8[4194304]{0:T(1024)(128)(4,1)S(1)}, s32[]{:S(2)}) async-start(s8[5242880]{0:T(1024)(128)(4,1)} %bitcast.14), calls=%async_computation | async-start | bytes 8388608
  14.3 18.0 %slice-start.2 = ((s8[5242880]{0:T(1024)(128)(4,1)}), s8[4194304]{0:T(1024)(128)(4,1)S(1)}, s32[]{:S(2)}) async-start(s8[5242880]{0:T(1024)(128)(4,1)} %bitcast.20), calls=%async_computation.2 | async-start | bytes 8388608
  14.3 17.9 %slice-start.4 = ((s8[5242880]{0:T(1024)(128)(4,1)}), s8[4194304]{0:T(1024)(128)(4,1)S(1)}, s32[]{:S(2)}) async-start(s8[5242880]{0:T(1024)(128)(4,1)} %bitcast.23), calls=%async_computation.4 | async-start | bytes 8388608
  14.3 17.9 %slice-start.1 = ((s8[5242880]{0:T(1024)(128)(4,1)}), s8[1048576]{0:T(1024)(128)(4,1)S(1)}, s32[]{:S(2)}) async-start(s8[5242880]{0:T(1024)(128)(4,1)} %bitcast.14), calls=%async_computation.1 | async-start | bytes 2097152
  14.3 17.9 %slice-start.3 = ((s8[5242880]{0:T(1024)(128)(4,1)}), s8[1048576]{0:T(1024)(128)(4,1)S(1)}, s32[]{:S(2)}) async-start(s8[5242880]{0:T(1024)(128)(4,1)} %bitcast.20), calls=%async_computation.3 | async-start | bytes 2097152
  14.3 17.9 %slice-start.5 = ((s8[5242880]{0:T(1024)(128)(4,1)}), s8[1048576]{0:T(1024)(128)(4,1)S(1)}, s32[]{:S(2)}) async-start(s8[5242880]{0:T(1024)(128)(4,1)} %bitcast.23), calls=%async_computation.5 | async-start | bytes 2097152
  14.4 17.9 %copy-start.5 = (s32[1,4]{1,0:T(1,128)S(1)}, s32[1,4]{1,0:T(1,128)}, u32[]{:S(2)}) copy-start(s32[1,4]{1,0:T(1,128)} %param.14) | copy-start | bytes 52
  14.4 17.9 %collective-permute-start.8 = (bf16[1280,128]{1,0:T(8,128)(2,1)S(1)}, bf16[1280,128]{1,0:T(8,128)(2,1)S(1)}, u32[]{:S(2)}, u32[]{:S(2)}) collective-permute-start(bf16[1280,128]{1,0:T(8,128)(2,1)S(1)} %get-tuple-element.34), channel_id=1, source_target_pairs={{0,1},{1,0},{2,3},{3,2},{4,5},{5,4},{6,7},{7,6},{8,9},{9,8},{10,11... | collective-permute-start | bytes 983048 | tf_op jit(solution)/shard_map/ppermute | solution.py:25
  20.3 19.7 %collective-permute-start.3 = (bf16[128,1280]{1,0:T(8,128)(2,1)S(1)}, bf16[128,1280]{1,0:T(8,128)(2,1)S(1)}, u32[]{:S(2)}, u32[]{:S(2)}) collective-permute-start(bf16[128,1280]{1,0:T(8,128)(2,1)S(1)} %get-tuple-element.29), channel_id=1, source_target_pairs={{0,1},{1,0},{2,3},{3,2},{4,5},{5,4},{6,7},{7,6},{8,9},{9,8},{10,11... | collective-permute-start | bytes 983048 | tf_op jit(solution)/shard_map/ppermute | solution.py:25
  21.8 18.1 %collective-permute-start.4 = (bf16[128,1280]{1,0:T(8,128)(2,1)S(1)}, bf16[128,1280]{1,0:T(8,128)(2,1)S(1)}, u32[]{:S(2)}, u32[]{:S(2)}) collective-permute-start(bf16[128,1280]{1,0:T(8,128)(2,1)S(1)} %get-tuple-element.30), channel_id=1, source_target_pairs={{0,2},{1,3},{2,0},{3,1},{4,6},{5,7},{6,4},{7,5},{8,10},{9,11},{10,... | collective-permute-start | bytes 983048 | tf_op jit(solution)/shard_map/ppermute | solution.py:25
  24.7 20.2 %collective-permute-start.5 = (bf16[128,1280]{1,0:T(8,128)(2,1)S(1)}, bf16[128,1280]{1,0:T(8,128)(2,1)S(1)}, u32[]{:S(2)}, u32[]{:S(2)}) collective-permute-start(bf16[128,1280]{1,0:T(8,128)(2,1)S(1)} %get-tuple-element.31), channel_id=1, source_target_pairs={{0,3},{1,2},{2,1},{3,0},{4,7},{5,6},{6,5},{7,4},{8,11},{9,10},{10,... | collective-permute-start | bytes 983048 | tf_op jit(solution)/shard_map/ppermute | solution.py:25
  32.3 12.6 %copy-start.2 = (bf16[1,128,5120]{2,1,0:T(8,128)(2,1)S(1)}, bf16[1,128,5120]{2,1,0:T(8,128)(2,1)}, u32[]{:S(2)}) copy-start(bf16[1,128,5120]{2,1,0:T(8,128)(2,1)} %param.8) | copy-start | bytes 3932164
  32.3 12.6 %copy-start.4 = (f32[1,5120]{1,0:T(1,128)S(1)}, f32[1,5120]{1,0:T(1,128)}, u32[]{:S(2)}) copy-start(f32[1,5120]{1,0:T(1,128)} %gain_ref.5) | copy-start | bytes 61444
  45.5 3.4 %collective-permute-start.9 = (bf16[64,5120]{1,0:T(8,128)(2,1)S(1)}, bf16[64,5120]{1,0:T(8,128)(2,1)S(1)}, u32[]{:S(2)}, u32[]{:S(2)}) collective-permute-start(bf16[64,5120]{1,0:T(8,128)(2,1)S(1)} %own.1.refs_4_), channel_id=1, source_target_pairs={{0,4},{4,0},{8,12},{12,8},{16,20},{20,16},{24,28},{28,24},{1,5},{5... | collective-permute-start | bytes 1966088 | tf_op jit(solution)/shard_map/ppermute | solution.py:25
  45.6 18.5 %collective-permute-start.16 = (bf16[256,1280]{1,0:T(8,128)(2,1)S(1)}, bf16[256,1280]{1,0:T(8,128)(2,1)S(1)}, u32[]{:S(2)}, u32[]{:S(2)}) collective-permute-start(bf16[256,1280]{1,0:T(8,128)(2,1)S(1)} %get-tuple-element.44), channel_id=1, source_target_pairs={{0,3},{1,2},{2,1},{3,0},{4,7},{5,6},{6,5},{7,4},{8,11},{9,10},{10,... | collective-permute-start | bytes 1966088 | tf_op jit(solution)/shard_map/ppermute | solution.py:25
  49.1 3.4 %collective-permute-start.10 = (bf16[32,5120]{1,0:T(8,128)(2,1)S(1)}, bf16[32,5120]{1,0:T(8,128)(2,1)S(1)}, u32[]{:S(2)}, u32[]{:S(2)}) collective-permute-start(bf16[32,5120]{1,0:T(8,128)(2,1)S(1)} %get-tuple-element.38), channel_id=1, source_target_pairs={{16,8},{24,16},{20,12},{28,20},{17,9},{25,17},{21,13},{29,21},{18,... | collective-permute-start | bytes 983048 | tf_op jit(solution)/shard_map/ppermute | solution.py:424
  49.7 2.7 %collective-permute-start.11 = (bf16[32,5120]{1,0:T(8,128)(2,1)S(1)}, bf16[32,5120]{1,0:T(8,128)(2,1)S(1)}, u32[]{:S(2)}, u32[]{:S(2)}) collective-permute-start(bf16[32,5120]{1,0:T(8,128)(2,1)S(1)} %get-tuple-element.39), channel_id=1, source_target_pairs={{24,8},{8,16},{28,12},{12,20},{25,9},{9,17},{29,13},{13,21},{26,10... | collective-permute-start | bytes 983048 | tf_op jit(solution)/shard_map/ppermute | solution.py:423
  50.4 27.5 %collective-permute-start.15 = (bf16[256,1280]{1,0:T(8,128)(2,1)S(1)}, bf16[256,1280]{1,0:T(8,128)(2,1)S(1)}, u32[]{:S(2)}, u32[]{:S(2)}) collective-permute-start(bf16[256,1280]{1,0:T(8,128)(2,1)S(1)} %get-tuple-element.43), channel_id=1, source_target_pairs={{0,1},{1,0},{2,3},{3,2},{4,5},{5,4},{6,7},{7,6},{8,9},{9,8},{10,11... | collective-permute-start | bytes 1966088 | tf_op jit(solution)/shard_map/ppermute | solution.py:25
  51.0 27.8 %collective-permute-start.14 = (bf16[256,1280]{1,0:T(8,128)(2,1)S(1)}, bf16[256,1280]{1,0:T(8,128)(2,1)S(1)}, u32[]{:S(2)}, u32[]{:S(2)}) collective-permute-start(bf16[256,1280]{1,0:T(8,128)(2,1)S(1)} %get-tuple-element.42), channel_id=1, source_target_pairs={{0,2},{1,3},{2,0},{3,1},{4,6},{5,7},{6,4},{7,5},{8,10},{9,11},{10,... | collective-permute-start | bytes 1966088 | tf_op jit(solution)/shard_map/ppermute | solution.py:25
  52.7 27.0 %collective-permute-start.12 = (bf16[32,5120]{1,0:T(8,128)(2,1)S(1)}, bf16[32,5120]{1,0:T(8,128)(2,1)S(1)}, u32[]{:S(2)}, u32[]{:S(2)}) collective-permute-start(bf16[32,5120]{1,0:T(8,128)(2,1)S(1)} %get-tuple-element.40), channel_id=1, source_target_pairs={{16,0},{20,4},{17,1},{21,5},{18,2},{22,6},{19,3},{23,7}} | collective-permute-start | bytes 983048 | tf_op jit(solution)/shard_map/ppermute | solution.py:436
  54.0 29.8 %collective-permute-start.13 = (bf16[32,5120]{1,0:T(8,128)(2,1)S(1)}, bf16[32,5120]{1,0:T(8,128)(2,1)S(1)}, u32[]{:S(2)}, u32[]{:S(2)}) collective-permute-start(bf16[32,5120]{1,0:T(8,128)(2,1)S(1)} %get-tuple-element.41), channel_id=1, source_target_pairs={{8,0},{16,8},{24,16},{12,4},{20,12},{28,20},{9,1},{17,9},{25,17},{... | collective-permute-start | bytes 983048 | tf_op jit(solution)/shard_map/ppermute | solution.py:435
  84.3 2.2 %collective-permute-start.17 = (bf16[64,5120]{1,0:T(8,128)(2,1)S(1)}, bf16[64,5120]{1,0:T(8,128)(2,1)S(1)}, u32[]{:S(2)}, u32[]{:S(2)}) collective-permute-start(bf16[64,5120]{1,0:T(8,128)(2,1)S(1)} %last.1._), channel_id=1, source_target_pairs={{0,4},{4,0},{8,12},{12,8},{16,20},{20,16},{24,28},{28,24},{1,5},{5... | collective-permute-start | bytes 1966088 | tf_op jit(solution)/shard_map/ppermute | solution.py:25
